TPU v7x, 256 devices: a whole 4x4x8 slice. The times are simulated.
256 devices in a mesh: user: 8 (over y, core), cand: 32 (over z, x).
Axes of the slice: x: 4, y: 4, z: 8, core: 2. Of those that a mesh axis runs over, the one named last changes fastest.
Arguments:
- cand_tokens: bfloat16 [8, 24576, 1024], P('user', 'cand'), may hold values from -6 to 6
- hist_keys: bfloat16 [8, 2048, 1024], P('user', 'cand'), may hold values from -6 to 6
- hist_values: bfloat16 [8, 2048, 1024], P('user', 'cand'), may hold values from -6 to 6
- hist_len: int32 [8], P('user'), may hold values from 512 to 2048, as said below
- cand_count: int32 [8], P('user'), may hold values from 3072 to 24576, as said below
- impressions: int32 [8, 24576], P('user', 'cand'), may hold values from 0 to 24575, each once within a row
- w_proj: bfloat16 [1024, 2048], P(None, 'user'), may hold values from -0.1875 to 0.1875
- w_out: bfloat16 [1024, 1024], replicated, may hold values from -0.1875 to 0.1875
- score_w: float32 [1024], replicated, may hold values from -0.1875 to 0.1875
Outputs:
- layer_out: bfloat16 [8, 24576, 1024], P('user', 'cand')
- ranked: float32 [8, 24576], P('user', 'cand')
Inputs may be any that keep to these rules, and one draw needn't show every extreme that they name: `hist_len`: some user has exactly 2048. `cand_count`: some user has exactly 24576. `impressions`: each row is a permutation of the slots.
All inputs are finite; a program needn't handle non-finite values.
Results may differ from a plain program's by a relative error of at most 0.0054.
Values may be sent and summed in bfloat16 or wider, within the bound.
No kernel may reach another device: no remote copies, remote signals or barrier semaphores. Data moves between devices by JAX's collectives and lax.ppermute only.
A program may use at most 128 MiB of HBM per device.

v0:
```python
import jax
import jax.numpy as jnp
from jax import lax
from jax.sharding import PartitionSpec as P

HEADS = 8


eps = 1e-05


def layer_norm(values):
    mean = jnp.mean(values, axis=-1, keepdims=True)
    centered = values - mean
    var = jnp.mean(centered * centered, axis=-1, keepdims=True)
    return centered * lax.rsqrt(var + eps)


def attend(query3, key_rows, value_rows, length, factor):
    count = key_rows.shape[0]
    heads = query3.shape[0]
    head_size = query3.shape[2]
    keys3 = key_rows.reshape(count, heads, head_size).transpose(1, 0, 2)
    values3 = value_rows.reshape(count, heads, head_size).transpose(1, 0, 2)
    valid = jnp.arange(count, dtype=jnp.int32) < length
    length_f = length.astype(jnp.float32)

    def per_head(trio):
        q_head, k_head, v_head = trio
        scores = jnp.einsum("rd,nd->rn", q_head, k_head, preferred_element_type=jnp.float32)
        weight = jnp.where(valid[None, :], jax.nn.silu(factor * scores) / length_f, 0.0).astype(
            jnp.bfloat16
        )
        return jnp.dot(weight, v_head, preferred_element_type=jnp.float32)

    return lax.map(per_head, (query3, keys3, values3))


def on_device(
    cand_tokens, hist_keys, hist_values, hist_len, cand_count, impressions, w_proj, w_out, score_w
):
    tokens = cand_tokens[0]
    rows = tokens.shape[0]
    width = tokens.shape[1]
    head_size = width // HEADS
    factor = float(head_size) ** (-0.5)
    inputs = tokens.astype(jnp.float32)
    normed = layer_norm(inputs).astype(jnp.bfloat16)
    proj = jax.nn.silu(
        jnp.dot(
            normed,
            lax.all_gather(w_proj, "user", axis=1, tiled=True),
            preferred_element_type=jnp.float32,
        )
    ).astype(jnp.bfloat16)
    gate = proj[:, :width]
    query = proj[:, width:]
    query3 = query.reshape(rows, HEADS, head_size).transpose(1, 0, 2)
    length = hist_len[0]
    all_keys, all_values = (
        lax.all_gather(hist_keys[0], "cand", axis=0, tiled=True),
        lax.all_gather(hist_values[0], "cand", axis=0, tiled=True),
    )
    attn = attend(query3, all_keys, all_values, length, factor)
    attn = attn.transpose(1, 0, 2).reshape(rows, width)
    gated = (layer_norm(attn) * gate.astype(jnp.float32)).astype(jnp.bfloat16)
    outputs = inputs + jnp.dot(gated, w_out, preferred_element_type=jnp.float32)
    slots = lax.axis_index("cand") * rows + jnp.arange(rows, dtype=jnp.int32)
    live = slots < cand_count[0]
    score = jnp.where(live, jnp.dot(outputs, score_w, precision=lax.Precision.HIGHEST), 0.0)
    every_score = lax.all_gather(score[None, :], "cand", axis=1, tiled=True)
    ranked = jnp.take_along_axis(every_score, impressions, axis=1)
    return (outputs.astype(jnp.bfloat16)[None], ranked)


def solution(mesh):
    return jax.shard_map(
        on_device,
        mesh=mesh,
        in_specs=(
            P("user", "cand", None),
            P("user", "cand", None),
            P("user", "cand", None),
            P("user"),
            P("user"),
            P("user", "cand"),
            P(None, "user"),
            P(),
            P(),
        ),
        out_specs=(P("user", "cand", None), P("user", "cand")),
        check_vma=False,
    )
```

profile of v0, /device:TPU:8, one launch (start us, length us, event | category | flops | bytes accessed | tf_op | source)
XLA Modules:
  0.0 332.0 jit_solution(8310223519465278040)
XLA Ops:
  11.4 1.7 convert_reduce_fusion
  13.1 2.0 fusion.24
  15.1 36.0 %all-gather.8.cloned.1.call-done = bf16[1024,2048]{1,0:T(8,128)(2,1)} async-done(((bf16[1024,256]{1,0:T(8,128)(2,1)}), bf16[1024,2048]{1,0:T(8,128)(2,1)}) %all-gather.8.cloned.1.call-update) | async-done | bytes 4194320 | tf_op jit(solution)/shard_map/all_gather | solution.py:52
  51.0 6.8 %multiply_convert_fusion = bf16[768,2048]{1,0:T(8,128)(2,1)S(1)} fusion(bf16[1024,2048]{1,0:T(8,128)(2,1)} %all-gather.8.cloned.1.call-done, bf16[1,768,1024]{2,1,0:T(8,128)(2,1)} %param.11, f32[768]{0:T(1024)S(1)} %add_rsqrt_fusion.1, f32[768]{0:T(1024)S(1)} %broadcast_multiply_fusion.1), kind=kOutput, calls=%fused_computation.17 | convolution fusion | flops 3232235520 | bytes 8919040 | tf_op jit(solution)/shard_map/dot_general | solution.py:50
  61.0 75.8 %all-gather.10.cloned.1.call-done = bf16[1,2048,1024]{2,1,0:T(8,128)(2,1)} async-done(((bf16[1,64,1024]{2,1,0:T(8,128)(2,1)}), bf16[1,2048,1024]{2,1,0:T(8,128)(2,1)}) %all-gather.10.cloned.1.call-update) | async-done | bytes 4194320 | tf_op jit(solution)/shard_map/all_gather | solution.py:61
  136.8 6.5 %copy.20 = bf16[1,2048,1024]{1,2,0:T(8,128)(2,1)} copy(bf16[1,2048,1024]{2,1,0:T(8,128)(2,1)} %all-gather.10.cloned.1.call-done) | data formatting | bytes 8388608 | tf_op jit(solution)/shard_map/all_gather | solution.py:61
  143.3 75.3 %all-gather.12.cloned.1.call-done = bf16[1,2048,1024]{2,1,0:T(8,128)(2,1)} async-done(((bf16[1,64,1024]{2,1,0:T(8,128)(2,1)}), bf16[1,2048,1024]{2,1,0:T(8,128)(2,1)}) %all-gather.12.cloned.1.call-update) | async-done | bytes 4194320 | tf_op jit(solution)/shard_map/all_gather | solution.py:62
  218.5 6.5 %copy.21 = bf16[1,2048,1024]{1,2,0:T(8,128)(2,1)} copy(bf16[1,2048,1024]{2,1,0:T(8,128)(2,1)} %all-gather.12.cloned.1.call-done) | data formatting | bytes 8388608 | tf_op jit(solution)/shard_map/all_gather | solution.py:62
  225.1 39.8 %while.11 = (s32[]{:T(128)}, f32[8,768,128]{2,1,0:T(8,128)}, bf16[8,768,128]{2,1,0:T(8,128)(2,1)}, bf16[8,2048,128]{1,2,0:T(8,128)(2,1)}, f32[]{:T(128)}, /*inde...) while((s32[]{:T(128)}, f32[8,768,128]{2,1,0:T(8,128)}, bf16[8,768,128]{2,1,0:T(8,128)(2,1)}, ...), condition=%wide.region_3.4_spmd.clone, body=%wide.region_2.3_spmd.clone.sunk | while | flops 817891328 | bytes 1645145 | solution.py:36
  225.7 4.3 %fusion.62 = f32[8,768,128]{2,1,0:T(8,128)} fusion(f32[8,768,128]{2,1,0:T(8,128)} %get-tuple-element.137, s32[]{:T(128)} %get-tuple-element.136, f32[]{:T(128)} %get-tuple-element.148, pred[2048]{0:T(1024)(128)(4,1)S(1)} %iota_compare_fusion.2, bf16[8,2048,128]{1,2,0:T(8,128)(2,1)} %get-tuple-element.149, ...), kind=kOutput, calls=%fused_computation.5.clone.1 | convolution fusion | flops 817889280 | bytes 1643008 | tf_op jit(solution)/shard_map/while/body/eval_jaxpr/dot_general | solution.py:34
  230.7 4.3 %fusion.62 = f32[8,768,128]{2,1,0:T(8,128)} fusion(f32[8,768,128]{2,1,0:T(8,128)} %get-tuple-element.137, s32[]{:T(128)} %get-tuple-element.136, f32[]{:T(128)} %get-tuple-element.148, pred[2048]{0:T(1024)(128)(4,1)S(1)} %iota_compare_fusion.2, bf16[8,2048,128]{1,2,0:T(8,128)(2,1)} %get-tuple-element.149, ...), kind=kOutput, calls=%fused_computation.5.clone.1 | convolution fusion | flops 817889280 | bytes 1643008 | tf_op jit(solution)/shard_map/while/body/eval_jaxpr/dot_general | solution.py:34
  235.7 4.3 %fusion.62 = f32[8,768,128]{2,1,0:T(8,128)} fusion(f32[8,768,128]{2,1,0:T(8,128)} %get-tuple-element.137, s32[]{:T(128)} %get-tuple-element.136, f32[]{:T(128)} %get-tuple-element.148, pred[2048]{0:T(1024)(128)(4,1)S(1)} %iota_compare_fusion.2, bf16[8,2048,128]{1,2,0:T(8,128)(2,1)} %get-tuple-element.149, ...), kind=kOutput, calls=%fused_computation.5.clone.1 | convolution fusion | flops 817889280 | bytes 1643008 | tf_op jit(solution)/shard_map/while/body/eval_jaxpr/dot_general | solution.py:34
  240.7 4.3 %fusion.62 = f32[8,768,128]{2,1,0:T(8,128)} fusion(f32[8,768,128]{2,1,0:T(8,128)} %get-tuple-element.137, s32[]{:T(128)} %get-tuple-element.136, f32[]{:T(128)} %get-tuple-element.148, pred[2048]{0:T(1024)(128)(4,1)S(1)} %iota_compare_fusion.2, bf16[8,2048,128]{1,2,0:T(8,128)(2,1)} %get-tuple-element.149, ...), kind=kOutput, calls=%fused_computation.5.clone.1 | convolution fusion | flops 817889280 | bytes 1643008 | tf_op jit(solution)/shard_map/while/body/eval_jaxpr/dot_general | solution.py:34
  245.6 4.3 %fusion.62 = f32[8,768,128]{2,1,0:T(8,128)} fusion(f32[8,768,128]{2,1,0:T(8,128)} %get-tuple-element.137, s32[]{:T(128)} %get-tuple-element.136, f32[]{:T(128)} %get-tuple-element.148, pred[2048]{0:T(1024)(128)(4,1)S(1)} %iota_compare_fusion.2, bf16[8,2048,128]{1,2,0:T(8,128)(2,1)} %get-tuple-element.149, ...), kind=kOutput, calls=%fused_computation.5.clone.1 | convolution fusion | flops 817889280 | bytes 1643008 | tf_op jit(solution)/shard_map/while/body/eval_jaxpr/dot_general | solution.py:34
  250.6 4.3 %fusion.62 = f32[8,768,128]{2,1,0:T(8,128)} fusion(f32[8,768,128]{2,1,0:T(8,128)} %get-tuple-element.137, s32[]{:T(128)} %get-tuple-element.136, f32[]{:T(128)} %get-tuple-element.148, pred[2048]{0:T(1024)(128)(4,1)S(1)} %iota_compare_fusion.2, bf16[8,2048,128]{1,2,0:T(8,128)(2,1)} %get-tuple-element.149, ...), kind=kOutput, calls=%fused_computation.5.clone.1 | convolution fusion | flops 817889280 | bytes 1643008 | tf_op jit(solution)/shard_map/while/body/eval_jaxpr/dot_general | solution.py:34
  255.6 4.3 %fusion.62 = f32[8,768,128]{2,1,0:T(8,128)} fusion(f32[8,768,128]{2,1,0:T(8,128)} %get-tuple-element.137, s32[]{:T(128)} %get-tuple-element.136, f32[]{:T(128)} %get-tuple-element.148, pred[2048]{0:T(1024)(128)(4,1)S(1)} %iota_compare_fusion.2, bf16[8,2048,128]{1,2,0:T(8,128)(2,1)} %get-tuple-element.149, ...), kind=kOutput, calls=%fused_computation.5.clone.1 | convolution fusion | flops 817889280 | bytes 1643008 | tf_op jit(solution)/shard_map/while/body/eval_jaxpr/dot_general | solution.py:34
  260.6 4.3 %fusion.62 = f32[8,768,128]{2,1,0:T(8,128)} fusion(f32[8,768,128]{2,1,0:T(8,128)} %get-tuple-element.137, s32[]{:T(128)} %get-tuple-element.136, f32[]{:T(128)} %get-tuple-element.148, pred[2048]{0:T(1024)(128)(4,1)S(1)} %iota_compare_fusion.2, bf16[8,2048,128]{1,2,0:T(8,128)(2,1)} %get-tuple-element.149, ...), kind=kOutput, calls=%fused_computation.5.clone.1 | convolution fusion | flops 817889280 | bytes 1643008 | tf_op jit(solution)/shard_map/while/body/eval_jaxpr/dot_general | solution.py:34
  264.9 2.1 reduce_sum.38
  267.0 2.5 fusion.30
  269.8 3.4 %fusion.35 = f32[768,1024]{1,0:T(8,128)S(1)} fusion(bf16[1024,1024]{1,0:T(8,128)(2,1)S(1)} %copy-done, bf16[768,2048]{1,0:T(8,128)(2,1)} %copy-done.3, f32[768]{0:T(1024)S(1)} %add_rsqrt_fusion, f32[768]{0:T(1024)S(1)} %broadcast_multiply_fusion, f32[8,768,128]{2,1,0:T(8,128)S(1)} %copy-done.2), kind=kOutput, calls=%fused_computation.36 | convolution fusion | flops 1614544896 | bytes 9967616 | tf_op jit(solution)/shard_map/dot_general | solution.py:67
  273.3 1.7 fusion.34
  275.1 2.9 fusion.46
  277.9 42.4 %all-gather.3 = f32[32,1,768]{2,1,0:T(1,128)S(1)} all-gather(f32[1,1,768]{2,1,0:T(1,128)S(1)} %reshape.87), channel_id=4, replica_groups=mesh['user'=8,'cand'=32] {'cand'}, dimensions={0}, use_global_device_ids=true | all-gather | bytes 101376 | tf_op jit(solution)/shard_map/all_gather | solution.py:71
  320.4 4.5 %gather_fusion = f32[768]{0:T(1024)S(1)} fusion(f32[24576]{0:T(1024)S(1)} %bitcast.92, s32[1024]{0:T(1024)S(1)} %pad_clamp_fusion), kind=kCustom, calls=%fused_computation | custom fusion | bytes 9216 | tf_op jit(solution)/shard_map/jit(take_along_axis)/gather | solution.py:72
  (37 shorter events, 12.1 us)
Async XLA Ops:
  7.2 262.3 %copy-start = (bf16[1024,1024]{1,0:T(8,128)(2,1)S(1)}, bf16[1024,1024]{1,0:T(8,128)(2,1)}, u32[]{:S(2)}) copy-start(bf16[1024,1024]{1,0:T(8,128)(2,1)} %param.18) | copy-start | bytes 6291460
  7.2 43.9 %all-gather.8.cloned.1.call-start = ((), (), s32[]{:S(2)}) async-start(), calls=%async_computation | async-start | bytes 4718592 | tf_op jit(solution)/shard_map/all_gather | solution.py:52
  7.9 128.8 %all-gather.10.cloned.1.call-start = ((), (), s32[]{:S(2)}) async-start(), calls=%async_computation.1 | async-start | bytes 4325376 | tf_op jit(solution)/shard_map/all_gather | solution.py:61
  8.7 209.9 %all-gather.12.cloned.1.call-start = ((), (), s32[]{:S(2)}) async-start(), calls=%async_computation.2 | async-start | bytes 4325376 | tf_op jit(solution)/shard_map/all_gather | solution.py:62
  57.9 1.7 copy-start.3
  267.0 2.8 copy-start.2
  269.8 3.5 %copy-start.1 = (bf16[1,768,1024]{2,1,0:T(8,128)(2,1)S(1)}, bf16[1,768,1024]{2,1,0:T(8,128)(2,1)}, u32[]{:S(2)}) copy-start(bf16[1,768,1024]{2,1,0:T(8,128)(2,1)} %param.11) | copy-start | bytes 4718596
  273.3 1.8 copy-start.5
  277.9 46.9 %copy-start.4 = (s32[1,768]{1,0:T(1,128)S(1)}, s32[1,768]{1,0:T(1,128)}, u32[]{:S(2)}) copy-start(s32[1,768]{1,0:T(1,128)} %param.16) | copy-start | bytes 9220
Sparse Core Ops, SparseCore 0:
  9.8 41.1 all-gather.7
  53.6 83.0 all-gather.9
  139.3 79.1 all-gather.11
where the time goes:
time: 333 us; the launch traced here: 332 us
  waiting for transfers between devices  189 us (57%)
  matrix products  47.7 us (14%)
  blocking collectives  42.4 us (13%)
  local copies, waits for them, and re-layouts  20.9 us (6%)
  other arithmetic  16.5 us (5%)
  between operations  15.2 us (5%)
    all_gather x1, waiting for transfers between devices, on_device(): lax.all_gather(hist_keys[0], 'cand', axis=0, tiled=True)  75.8 us
    all_gather x1, waiting for transfers between devices, on_device(): lax.all_gather(hist_values[0], 'cand', axis=0, tiled=True)  75.3 us
    all_gather x1, blocking collectives, on_device(): every_score = lax.all_gather(score[None, :], 'cand', axis=1, tiled=True)  42.4 us
    all_gather x1, waiting for transfers between devices, on_device(): lax.all_gather(w_proj, 'user', axis=1, tiled=True)  36 us
    dot_general x8, matrix products, per_head(): return jnp.dot(weight, v_head, preferred_element_type=jnp.float32)  34.6 us
    dot_general x1, matrix products, on_device(): jnp.dot(normed, lax.all_gather(w_proj, 'user', axis=1, tiled=True), prefe...  6.83 us
  transfers between devices with their start and end apart: 3, of which 3 were waited for; matrix products, arithmetic and copies ran while one was open for 6% of the time, Pallas kernels for 0%

commit v1 on v0

v1 whole, which is shorter than its diff:
```python
import functools

import jax
import jax.numpy as jnp
from jax import lax
from jax.experimental import pallas as pl
from jax.experimental.pallas import tpu as pltpu
from jax.sharding import Mesh
from jax.sharding import PartitionSpec as P

HEADS = 8
eps = 1e-05
VMEM_LIMIT = 48 * 2**20


def params():
    return pltpu.CompilerParams(vmem_limit_bytes=VMEM_LIMIT)


def layer_norm(values):
    mean = jnp.mean(values, axis=-1, keepdims=True)
    centered = values - mean
    var = jnp.mean(centered * centered, axis=-1, keepdims=True)
    return centered * lax.rsqrt(var + eps)


def shifted(size, step):
    return [(i, (i + step) % size) for i in range(size)]


def project_kernel(order_ref, tokens_ref, w_ref, out_ref, normed):
    @pl.when(pl.program_id(0) == 0)
    def _():
        normed[...] = layer_norm(tokens_ref[...].astype(jnp.float32)).astype(jnp.bfloat16)

    x = jnp.dot(normed[...], w_ref[0], preferred_element_type=jnp.float32)
    half = 0.5 * x
    out_ref[...] = (half + half * jnp.tanh(half)).astype(jnp.bfloat16)


def project(tokens, blocks, order):
    rows, width = tokens.shape
    count, _, columns = blocks.shape
    return pl.pallas_call(
        project_kernel,
        grid_spec=pltpu.PrefetchScalarGridSpec(
            num_scalar_prefetch=1,
            grid=(count,),
            in_specs=[
                pl.BlockSpec((rows, width), lambda j, o: (0, 0)),
                pl.BlockSpec((1, width, columns), lambda j, o: (o[j], 0, 0)),
            ],
            out_specs=pl.BlockSpec((rows, columns), lambda j, o: (0, j)),
            scratch_shapes=[pltpu.VMEM((rows, width), jnp.bfloat16)],
        ),
        out_shape=jax.ShapeDtypeStruct((rows, count * columns), jnp.bfloat16),
        compiler_params=params(),
        cost_estimate=pl.CostEstimate(
            flops=2 * rows * width * count * columns, bytes_accessed=9 * 2**20, transcendentals=rows * count * columns
        ),
    )(order, tokens, blocks)


def attend_kernel(q_ref, k_ref, v_ref, scale_ref, out_ref, *, factor, tile):
    head = q_ref.shape[1]
    k = k_ref[...].reshape(-1, head)
    v = v_ref[...].reshape(-1, head)
    for r in range(0, q_ref.shape[0], tile):
        s = lax.dot_general(
            q_ref[r : r + tile, :], k, (((1,), (1,)), ((), ())), preferred_element_type=jnp.float32
        )
        w = (s * jnp.tanh(s * (0.5 * factor)) + s).astype(jnp.bfloat16)
        out_ref[r : r + tile, :] = jnp.dot(w, v, preferred_element_type=jnp.float32) * scale_ref[0]


def attend(proj, history, scale, width):
    rows = proj.shape[0]
    parts, both, _ = history.shape
    own = both // 2
    head = width // HEADS
    return pl.pallas_call(
        functools.partial(attend_kernel, factor=float(head) ** -0.5, tile=256),
        grid=(HEADS,),
        in_specs=[
            pl.BlockSpec((rows, head), lambda h: (0, HEADS + h)),
            pl.BlockSpec((parts, own, head), lambda h: (0, 0, h)),
            pl.BlockSpec((parts, own, head), lambda h: (0, 1, h)),
            pl.BlockSpec(memory_space=pltpu.SMEM),
        ],
        out_specs=pl.BlockSpec((rows, head), lambda h: (0, h)),
        out_shape=jax.ShapeDtypeStruct((rows, width), jnp.float32),
        compiler_params=params(),
        cost_estimate=pl.CostEstimate(
            flops=8 * rows * parts * own * width, bytes_accessed=12 * 2**20, transcendentals=rows * parts * own * HEADS
        ),
    )(proj, history, history, scale)


def gate_kernel(attn_ref, gate_ref, tokens_ref, w_ref, sw_ref, live_ref, gated_ref, score_ref, ws):
    @pl.when(pl.program_id(0) == 0)
    def _():
        ws[...] = lax.dot_general(
            sw_ref[...],
            w_ref[...].astype(jnp.float32),
            (((1,), (1,)), ((), ())),
            precision=lax.Precision.HIGHEST,
            preferred_element_type=jnp.float32,
        )

    gated = (layer_norm(attn_ref[...]) * gate_ref[...].astype(jnp.float32)).astype(jnp.bfloat16)
    gated_ref[...] = gated
    total = gated.astype(jnp.float32) * ws[...] + tokens_ref[...].astype(jnp.float32) * sw_ref[...]
    score = jnp.sum(total, axis=-1)
    first = pl.program_id(0) * score.shape[0]
    slots = first + lax.broadcasted_iota(jnp.int32, (1, score.shape[0]), 1)
    score_ref[...] = jnp.where(slots < live_ref[0], score.reshape(1, -1), 0.0)


def gate_and_score(attn, proj, tokens, w_out, score_w, live, tile=256):
    rows, width = tokens.shape
    return pl.pallas_call(
        gate_kernel,
        grid=(rows // tile,),
        in_specs=[
            pl.BlockSpec((tile, width), lambda i: (i, 0)),
            pl.BlockSpec((tile, width), lambda i: (i, 0)),
            pl.BlockSpec((tile, width), lambda i: (i, 0)),
            pl.BlockSpec((width, width), lambda i: (0, 0)),
            pl.BlockSpec((1, width), lambda i: (0, 0)),
            pl.BlockSpec(memory_space=pltpu.SMEM),
        ],
        out_specs=[pl.BlockSpec((tile, width), lambda i: (i, 0)), pl.BlockSpec((1, tile), lambda i: (0, i))],
        out_shape=[
            jax.ShapeDtypeStruct((rows, width), jnp.bfloat16),
            jax.ShapeDtypeStruct((1, rows), jnp.float32),
        ],
        scratch_shapes=[pltpu.VMEM((1, width), jnp.float32)],
        compiler_params=params(),
    )(attn, proj, tokens, w_out, score_w, live)


def out_kernel(gated_ref, w_ref, tokens_ref, out_ref):
    y = tokens_ref[...].astype(jnp.float32) + jnp.dot(gated_ref[...], w_ref[...], preferred_element_type=jnp.float32)
    out_ref[...] = y.astype(jnp.bfloat16)


def project_out(gated, w_out, tokens, tile=256):
    rows, width = tokens.shape
    return pl.pallas_call(
        out_kernel,
        grid=(rows // tile,),
        in_specs=[
            pl.BlockSpec((tile, width), lambda i: (i, 0)),
            pl.BlockSpec((width, width), lambda i: (0, 0)),
            pl.BlockSpec((tile, width), lambda i: (i, 0)),
        ],
        out_specs=pl.BlockSpec((tile, width), lambda i: (i, 0)),
        out_shape=jax.ShapeDtypeStruct((rows, width), jnp.bfloat16),
        compiler_params=params(),
        cost_estimate=pl.CostEstimate(flops=2 * rows * width * width, bytes_accessed=7 * 2**20, transcendentals=0),
    )(gated, w_out, tokens)


def pick_kernel(index_ref, table_ref, out_ref):
    index = index_ref[...]
    count = index.shape[0]
    height, lanes = table_ref.shape
    onehot = (lax.broadcasted_iota(jnp.int32, (count, height), 1) == index // lanes).astype(jnp.bfloat16)
    rest = table_ref[...]
    rows = jnp.zeros((count, lanes), jnp.float32)
    for _ in range(3):
        part = rest.astype(jnp.bfloat16)
        rows += jnp.dot(onehot, part, preferred_element_type=jnp.float32)
        rest = rest - part.astype(jnp.float32)
    mine = lax.broadcasted_iota(jnp.int32, (count, lanes), 1) == index % lanes
    out_ref[...] = jnp.sum(jnp.where(mine, rows, 0.0), axis=-1).reshape(1, -1)


def pick(index, table):
    count = index.shape[0]
    return pl.pallas_call(
        pick_kernel,
        out_shape=jax.ShapeDtypeStruct((1, count), jnp.float32),
        compiler_params=params(),
    )(index.reshape(count, 1), table.reshape(-1, 128))


def on_device(
    cand_tokens, hist_keys, hist_values, hist_len, cand_count, impressions, w_proj, w_out, score_w
):
    tokens = cand_tokens[0]
    rows, width = tokens.shape
    own = hist_keys.shape[1]
    cand = lax.axis_index(("z", "x"))
    y, core = lax.axis_index("y"), lax.axis_index("core")
    many_y, many_core = lax.axis_size("y"), lax.axis_size("core")
    parts = lax.axis_size(("z", "x"))

    position = cand * own + jnp.arange(own, dtype=jnp.int32)
    keys = jnp.where((position < hist_len[0])[:, None], hist_keys[0], jnp.zeros((), jnp.bfloat16))
    mine = jnp.concatenate([keys, hist_values[0]], axis=0)
    history = lax.all_gather(mine, ("z", "x"), axis=0, tiled=False)

    blocks = [w_proj] + [lax.ppermute(w_proj, "y", shifted(many_y, step)) for step in range(1, many_y)]
    blocks = [each for block in blocks for each in (block, lax.ppermute(block, "core", [(0, 1), (1, 0)]))]
    user = jnp.arange(many_y * many_core, dtype=jnp.int32)
    order = ((y - user // many_core) % many_y) * many_core + (user % many_core != core).astype(jnp.int32)
    proj = project(tokens, jnp.stack(blocks), order.astype(jnp.int32))

    scale = 0.5 * float(width // HEADS) ** -0.5 / hist_len.astype(jnp.float32)
    attn = attend(proj, history, scale, width)
    live = cand_count - cand * rows
    gated, score = gate_and_score(attn, proj, tokens, w_out, score_w[None, :], live)
    sent = jnp.broadcast_to(score[:, None, :], (parts, 1, rows))
    every = lax.all_to_all(sent, ("z", "x"), split_axis=0, concat_axis=0, tiled=True)
    layer_out = project_out(gated, w_out, tokens)
    ranked = pick(impressions[0], every)
    return (layer_out[None], ranked)


def solution(mesh):
    split = Mesh(mesh.devices.reshape(4, 2, 8, 4), ("y", "core", "z", "x"))
    users, cands = ("y", "core"), ("z", "x")
    return jax.shard_map(
        on_device,
        mesh=split,
        in_specs=(
            P(users, cands, None),
            P(users, cands, None),
            P(users, cands, None),
            P(users),
            P(users),
            P(users, cands),
            P(None, users),
            P(),
            P(),
        ),
        out_specs=(P(users, cands, None), P(users, cands)),
        check_vma=False,
    )
```

time: 333 us -> 165 us (0.50)
  waiting for transfers between devices: 189 us -> 79.5 us
  matrix products: 47.7 us -> 0 us
  blocking collectives: 42.4 us -> 0 us
  Pallas kernels: 0 us -> 37.9 us
  other arithmetic: 16.5 us -> 2.65 us
  starting transfers between devices: 0.11 us -> 10.9 us
    all_gather x3 -> x1, waiting for transfers between devices: 187 us -> 57.8 us  [on_device(): history = lax.all_gather(mine, ('z', 'x'), axis=0, tiled=False)]
    dot_general x11 -> x0, matrix products: 47.7 us -> none  [the longest x8 34.6 us: per_head(): return jnp.dot(weight, v_head, preferred_element_type=jnp.float32)]
    all_gather x1 -> x0, blocking collectives: 42.4 us -> none  [on_device(): every_score = lax.all_gather(score[None, :], 'cand', axis=1, tiled=True)]
    pallas_call x0 -> x5, Pallas kernels: none -> 37.9 us  [the longest x1 17.2 us: attend(): pl.pallas_call(functools.partial(attend_kernel, factor=float(head) ** (-0...]
    ppermute x0 -> x7, waiting for transfers between devices: none -> 17.5 us  [the longest x3 17.5 us: on_device(): lax.ppermute(w_proj, 'y', shifted(many_y, step))]
    unnamed x13 -> x27, local copies, waits for them, and re-layouts: 2 us -> 16.5 us
    all_gather x2 -> x0, local copies, waits for them, and re-layouts: 13 us -> none  [the longest x1 6.52 us: on_device(): lax.all_gather(hist_values[0], 'cand', axis=0, tiled=True)]
    reduce_sum x4 -> x0, other arithmetic: 8.24 us -> none  [the longest x2 4.45 us: layer_norm(): var = jnp.mean(centered * centered, axis=-1, keepdims=True)]
  transfers between devices with their start and end apart: 3 -> 9, of which waited for: 3 -> 5; matrix products, arithmetic and copies ran while one was open for 6% -> 6% of each run, Pallas kernels for 0% -> 7%
where the time goes in v1:
time: 165 us
  waiting for transfers between devices  79.5 us (48%)
  Pallas kernels  37.9 us (23%)
  local copies, waits for them, and re-layouts  18.2 us (11%)
  between operations  15.5 us (9%)
  starting transfers between devices  10.9 us (7%)
  other arithmetic  2.65 us (2%)
    all_gather x1, waiting for transfers between devices, on_device(): history = lax.all_gather(mine, ('z', 'x'), axis=0, tiled=False)  57.8 us
    ppermute x3, waiting for transfers between devices, on_device(): lax.ppermute(w_proj, 'y', shifted(many_y, step))  17.5 us
    pallas_call x1, Pallas kernels, attend(): pl.pallas_call(functools.partial(attend_kernel, factor=float(head) ** (-0...  17.2 us
    unnamed x27, local copies, waits for them, and re-layouts  16.5 us
    pallas_call x1, Pallas kernels, project(): pl.pallas_call(project_kernel, grid_spec=pltpu.PrefetchScalarGridSpec(num...  8.93 us
    pallas_call x1, Pallas kernels, gate_and_score(): pl.pallas_call(gate_kernel, grid=(rows // tile,), in_specs=[pl.BlockSpec(...  7.39 us
    all_to_all x1, starting transfers between devices, on_device(): lax.all_to_all(sent, ('z', 'x'), split_axis=0, concat_axis=0, tiled=True)  5.63 us
    ppermute x3, starting transfers between devices, on_device(): lax.ppermute(w_proj, 'y', shifted(many_y, step))  5 us
  transfers between devices with their start and end apart: 9, of which 5 were waited for; matrix products, arithmetic and copies ran while one was open for 6% of the time, Pallas kernels for 7%

profile of v1, /device:TPU:8, one launch (start us, length us, event | category | flops | bytes accessed | tf_op | source)
XLA Modules:
  0.0 164.6 jit_solution(17597174747748986020)
XLA Ops:
  7.9 1.0 bitcast_select_fusion
  8.9 1.6 pad_maximum_fusion
  10.5 1.7 %collective-permute-start.1 = (bf16[1024,256]{1,0:T(8,128)(2,1)}, bf16[1024,256]{1,0:T(8,128)(2,1)S(1)}, u32[]{:S(2)}, u32[]{:S(2)}) collective-permute-start(bf16[1024,256]{1,0:T(8,128)(2,1)} %param.15), channel_id=1, source_target_pairs={{0,64},{64,128},{128,192},{192,0},{1,65},{65,129},{129,193},{193,1... | collective-permute-start | bytes 1572872 | tf_op jit(solution)/shard_map/ppermute | solution.py:204
  12.2 2.7 %collective-permute-start.3 = (bf16[1024,256]{1,0:T(8,128)(2,1)}, bf16[1024,256]{1,0:T(8,128)(2,1)S(1)}, u32[]{:S(2)}, u32[]{:S(2)}) collective-permute-start(bf16[1024,256]{1,0:T(8,128)(2,1)} %param.15), channel_id=1, source_target_pairs={{0,128},{64,192},{128,0},{192,64},{1,129},{65,193},{129,1},{193,65... | collective-permute-start | bytes 1572872 | tf_op jit(solution)/shard_map/ppermute | solution.py:204
  15.5 2.1 %bitcast_dynamic-update-slice_fusion.7 = bf16[8,1024,256]{2,1,0:T(8,128)(2,1)} fusion(bf16[1024,256]{1,0:T(8,128)(2,1)} %param.15), kind=kLoop, calls=%fused_computation.7 | loop fusion | bytes 1048576
  17.6 8.2 %collective-permute-done.1 = bf16[1024,256]{1,0:T(8,128)(2,1)S(1)} collective-permute-done((bf16[1024,256]{1,0:T(8,128)(2,1)}, bf16[1024,256]{1,0:T(8,128)(2,1)S(1)}, u32[]{:S(2)}, u32[]{:S(2)}) %collective-permute-start.1) | collective-permute-done | bytes 524320 | tf_op jit(solution)/shard_map/ppermute | solution.py:204
  26.5 2.3 %collective-permute-done.3 = bf16[1024,256]{1,0:T(8,128)(2,1)S(1)} collective-permute-done((bf16[1024,256]{1,0:T(8,128)(2,1)}, bf16[1024,256]{1,0:T(8,128)(2,1)S(1)}, u32[]{:S(2)}, u32[]{:S(2)}) %collective-permute-start.3) | collective-permute-done | bytes 524320 | tf_op jit(solution)/shard_map/ppermute | solution.py:204
  28.8 1.9 %bitcast_dynamic-update-slice_fusion.6 = bf16[8,1024,256]{2,1,0:T(8,128)(2,1)} fusion(bf16[8,1024,256]{2,1,0:T(8,128)(2,1)} %bitcast_dynamic-update-slice_fusion.7, bf16[1024,256]{1,0:T(8,128)(2,1)} %collective-permute-done), kind=kLoop, calls=%fused_computation.6 | loop fusion | bytes 1048576
  31.5 7.0 %collective-permute-done.5 = bf16[1024,256]{1,0:T(8,128)(2,1)S(1)} collective-permute-done((bf16[1024,256]{1,0:T(8,128)(2,1)}, bf16[1024,256]{1,0:T(8,128)(2,1)S(1)}, u32[]{:S(2)}, u32[]{:S(2)}) %collective-permute-start.5) | collective-permute-done | bytes 524320 | tf_op jit(solution)/shard_map/ppermute | solution.py:204
  38.7 1.9 %bitcast_dynamic-update-slice_fusion.4 = bf16[8,1024,256]{2,1,0:T(8,128)(2,1)} fusion(bf16[8,1024,256]{2,1,0:T(8,128)(2,1)} %bitcast_dynamic-update-slice_fusion.5, bf16[1024,256]{1,0:T(8,128)(2,1)} %collective-permute-done.2), kind=kLoop, calls=%fused_computation.4 | loop fusion | bytes 1048576
  43.1 0.9 bitcast_dynamic-update-slice_fusion.w_ref
  43.9 8.9 %shard_map.104.q_ref.gate_ref = bf16[768,2048]{1,0:T(8,128)(2,1)S(1)} custom-call(s32[8]{0:T(128)S(1)} %fusion.order_ref, bf16[768,1024]{1,0:T(8,128)(2,1)S(1)} %bitcast.28, bf16[8,1024,256]{2,1,0:T(8,128)(2,1)} %bitcast_dynamic-update-slice_fusion.w_ref), custom_call_target="tpu_custom_call" | custom-call | flops 3221225472 | bytes 9437184 | tf_op jit(solution)/shard_map/pallas_call | solution.py:44
  52.9 1.7 %copy-done.4 = bf16[768,2048]{1,0:T(8,128)(2,1)} copy-done((bf16[768,2048]{1,0:T(8,128)(2,1)}, bf16[768,2048]{1,0:T(8,128)(2,1)S(1)}, u32[]{:S(2)}) %copy-start.4) | copy-done | bytes 3145752
  54.6 57.8 %all-gather.3.cloned.1.call-done = bf16[4096,1024]{1,0:T(8,128)(2,1)} async-done(((bf16[128,1024]{1,0:T(8,128)(2,1)}), bf16[4096,1024]{1,0:T(8,128)(2,1)}) %all-gather.3.cloned.1.call-update) | async-done | bytes 8388624 | tf_op jit(solution)/shard_map/all_gather | solution.py:202
  112.4 17.2 %shard_map.105.attn_ref = f32[768,1024]{1,0:T(8,128)S(1)} custom-call(bf16[768,2048]{1,0:T(8,128)(2,1)} %copy-done.4, bf16[32,128,1024]{2,1,0:T(8,128)(2,1)} %bitcast.36, bf16[32,128,1024]{2,1,0:T(8,128)(2,1)} %bitcast.37, f32[1]{0:T(128)S(6)} %div.10.scale_ref), custom_call_target="tpu_custom_call" | custom-call | flops 12884901888 | bytes 12582912 | tf_op jit(solution)/shard_map/pallas_call | solution.py:81
  129.6 1.6 copy-done.5
  131.3 7.4 %shard_map.106 = (bf16[768,1024]{1,0:T(8,128)(2,1)S(1)}, f32[1,768]{1,0:T(1,128)S(1)}) custom-call(f32[768,1024]{1,0:T(8,128)} %copy-done.5, bf16[768,2048]{1,0:T(8,128)(2,1)} %copy-done.4, bf16[768,1024]{1,0:T(8,128)(2,1)S(1)} %bitcast.29, bf16[1024,1024]{1,0:T(8,128)(2,1)S(1)} %copy-done, f32[1,1024]{1,0:T(1,128)S(1)} %bitcast.32, s32[1]{0:T(128)S(6)} %sub.20.live_ref), custom_call_target="tpu_custom_call" | custom-call | tf_op jit(solution)/shard_map/pallas_call | solution.py:121
  138.7 1.1 copy-done.6
  140.5 5.6 %all-to-all-start = ((f32[32,1,768]{2,1,0:T(1,128)}), f32[32,1,768]{2,1,0:T(1,128)S(1)}, u32[]{:S(2)}, u32[]{:S(2)}) async-start(f32[32,1,768]{2,1,0:T(1,128)} %broadcast_in_dim.32), calls=%async_computation | async-start | bytes 196608 | tf_op jit(solution)/shard_map/all_to_all | solution.py:215
  146.4 1.4 copy-done.3
  147.8 1.4 copy-done.7
  149.2 3.0 %shard_map.107 = bf16[768,1024]{1,0:T(8,128)(2,1)} custom-call(bf16[768,1024]{1,0:T(8,128)(2,1)S(1)} %copy-done.7, bf16[1024,1024]{1,0:T(8,128)(2,1)S(1)} %copy-done, bf16[768,1024]{1,0:T(8,128)(2,1)S(1)} %bitcast.30), custom_call_target="tpu_custom_call" | custom-call | flops 1610612736 | bytes 7340032 | tf_op jit(solution)/shard_map/pallas_call | solution.py:149
  152.2 4.2 %all-to-all-done = f32[32,1,768]{2,1,0:T(1,128)S(1)} async-done(((f32[32,1,768]{2,1,0:T(1,128)}), f32[32,1,768]{2,1,0:T(1,128)S(1)}, u32[]{:S(2)}, u32[]{:S(2)}) %all-to-all-start) | async-done | bytes 98336 | tf_op jit(solution)/shard_map/all_to_all | solution.py:215
  156.4 1.3 shard_map.108
  (35 shorter events, 5.2 us)
Async XLA Ops:
  7.2 105.2 %all-gather.3.cloned.1.call-start = ((), (), s32[]{:S(2)}) async-start(), calls=%async_computation.1 | async-start | bytes 8650752 | tf_op jit(solution)/shard_map/all_gather | solution.py:202
  10.5 15.3 %collective-permute-start.1 = (bf16[1024,256]{1,0:T(8,128)(2,1)}, bf16[1024,256]{1,0:T(8,128)(2,1)S(1)}, u32[]{:S(2)}, u32[]{:S(2)}) collective-permute-start(bf16[1024,256]{1,0:T(8,128)(2,1)} %param.15), channel_id=1, source_target_pairs={{0,64},{64,128},{128,192},{192,0},{1,65},{65,129},{129,193},{193,1... | collective-permute-start | bytes 1572872 | tf_op jit(solution)/shard_map/ppermute | solution.py:204
  12.2 16.6 %collective-permute-start.3 = (bf16[1024,256]{1,0:T(8,128)(2,1)}, bf16[1024,256]{1,0:T(8,128)(2,1)S(1)}, u32[]{:S(2)}, u32[]{:S(2)}) collective-permute-start(bf16[1024,256]{1,0:T(8,128)(2,1)} %param.15), channel_id=1, source_target_pairs={{0,128},{64,192},{128,0},{192,64},{1,129},{65,193},{129,1},{193,65... | collective-permute-start | bytes 1572872 | tf_op jit(solution)/shard_map/ppermute | solution.py:204
  14.8 13.9 %collective-permute-start = (bf16[1024,256]{1,0:T(8,128)(2,1)}, bf16[1024,256]{1,0:T(8,128)(2,1)}, u32[]{:S(2)}, u32[]{:S(2)}) collective-permute-start(bf16[1024,256]{1,0:T(8,128)(2,1)} %param.15), channel_id=1, source_target_pairs={{0,32},{32,0},{1,33},{33,1},{2,34},{34,2},{3,35},{35,3},{4,36},{36... | collective-permute-start | bytes 1572872 | tf_op jit(solution)/shard_map/ppermute | solution.py:205
  14.9 23.7 %collective-permute-start.5 = (bf16[1024,256]{1,0:T(8,128)(2,1)}, bf16[1024,256]{1,0:T(8,128)(2,1)S(1)}, u32[]{:S(2)}, u32[]{:S(2)}) collective-permute-start(bf16[1024,256]{1,0:T(8,128)(2,1)} %param.15), channel_id=1, source_target_pairs={{0,192},{64,0},{128,64},{192,128},{1,193},{65,1},{129,65},{193,129... | collective-permute-start | bytes 1572872 | tf_op jit(solution)/shard_map/ppermute | solution.py:204
  15.5 28.4 %copy-start.1 = (bf16[1,768,1024]{2,1,0:T(8,128)(2,1)S(1)}, bf16[1,768,1024]{2,1,0:T(8,128)(2,1)}, u32[]{:S(2)}) copy-start(bf16[1,768,1024]{2,1,0:T(8,128)(2,1)} %param.9) | copy-start | bytes 4718596
  25.8 12.9 %collective-permute-start.2 = (bf16[1024,256]{1,0:T(8,128)(2,1)S(1)}, bf16[1024,256]{1,0:T(8,128)(2,1)}, u32[]{:S(2)}, u32[]{:S(2)}) collective-permute-start(bf16[1024,256]{1,0:T(8,128)(2,1)S(1)} %collective-permute-done.1), channel_id=1, source_target_pairs={{0,32},{32,0},{1,33},{33,1},{2,34},{34,2},{3,35},{35,3},{4,36},{36... | collective-permute-start | bytes 1572872 | tf_op jit(solution)/shard_map/ppermute | solution.py:205
  28.8 12.6 %collective-permute-start.4 = (bf16[1024,256]{1,0:T(8,128)(2,1)S(1)}, bf16[1024,256]{1,0:T(8,128)(2,1)S(1)}, u32[]{:S(2)}, u32[]{:S(2)}) collective-permute-start(bf16[1024,256]{1,0:T(8,128)(2,1)S(1)} %collective-permute-done.3), channel_id=1, source_target_pairs={{0,32},{32,0},{1,33},{33,1},{2,34},{34,2},{3,35},{35,3},{4,36},{36... | collective-permute-start | bytes 1572872 | tf_op jit(solution)/shard_map/ppermute | solution.py:205
  38.5 4.6 %collective-permute-start.6 = (bf16[1024,256]{1,0:T(8,128)(2,1)S(1)}, bf16[1024,256]{1,0:T(8,128)(2,1)S(1)}, u32[]{:S(2)}, u32[]{:S(2)}) collective-permute-start(bf16[1024,256]{1,0:T(8,128)(2,1)S(1)} %collective-permute-done.5), channel_id=1, source_target_pairs={{0,32},{32,0},{1,33},{33,1},{2,34},{34,2},{3,35},{35,3},{4,36},{36... | collective-permute-start | bytes 1572872 | tf_op jit(solution)/shard_map/ppermute | solution.py:205
  52.9 1.7 %copy-start.4 = (bf16[768,2048]{1,0:T(8,128)(2,1)}, bf16[768,2048]{1,0:T(8,128)(2,1)S(1)}, u32[]{:S(2)}) copy-start(bf16[768,2048]{1,0:T(8,128)(2,1)S(1)} %shard_map.104.q_ref.gate_ref) | copy-start | bytes 9437188
  112.4 18.9 %copy-start = (bf16[1024,1024]{1,0:T(8,128)(2,1)S(1)}, bf16[1024,1024]{1,0:T(8,128)(2,1)}, u32[]{:S(2)}) copy-start(bf16[1024,1024]{1,0:T(8,128)(2,1)} %w_ref.3) | copy-start | bytes 6291460
  112.4 18.9 %copy-start.2 = (bf16[1,768,1024]{2,1,0:T(8,128)(2,1)S(1)}, bf16[1,768,1024]{2,1,0:T(8,128)(2,1)}, u32[]{:S(2)}) copy-start(bf16[1,768,1024]{2,1,0:T(8,128)(2,1)} %param.9) | copy-start | bytes 4718596
  112.4 18.9 %copy-start.8 = (f32[1024]{0:T(1024)S(1)}, f32[1024]{0:T(1024)}, u32[]{:S(2)}) copy-start(f32[1024]{0:T(1024)} %param.17) | copy-start | bytes 12292
  129.6 1.7 %copy-start.5 = (f32[768,1024]{1,0:T(8,128)}, f32[768,1024]{1,0:T(8,128)S(1)}, u32[]{:S(2)}) copy-start(f32[768,1024]{1,0:T(8,128)S(1)} %shard_map.105.attn_ref) | copy-start | bytes 9437188
  131.3 14.9 %copy-start.9 = (s32[1,768]{1,0:T(1,128)S(1)}, s32[1,768]{1,0:T(1,128)}, u32[]{:S(2)}) copy-start(s32[1,768]{1,0:T(1,128)} %param.14) | copy-start | bytes 9220
  138.7 1.1 copy-start.6
  140.5 15.9 %all-to-all-start = ((f32[32,1,768]{2,1,0:T(1,128)}), f32[32,1,768]{2,1,0:T(1,128)S(1)}, u32[]{:S(2)}, u32[]{:S(2)}) async-start(f32[32,1,768]{2,1,0:T(1,128)} %broadcast_in_dim.32), calls=%async_computation | async-start | bytes 196608 | tf_op jit(solution)/shard_map/all_to_all | solution.py:215
  146.4 1.4 copy-start.3
  147.8 1.4 copy-start.7
Sparse Core Ops, SparseCore 0:
  11.2 101.1 all-gather.2

commit v2 on v1

v2 whole, which is shorter than its diff:
```python
import functools

import jax
import jax.numpy as jnp
from jax import lax
from jax.experimental import pallas as pl
from jax.experimental.pallas import tpu as pltpu
from jax.sharding import Mesh
from jax.sharding import PartitionSpec as P

HEADS = 8
eps = 1e-05
VMEM_LIMIT = 58 * 2**20


def params():
    return pltpu.CompilerParams(vmem_limit_bytes=VMEM_LIMIT)


def layer_norm(values):
    mean = jnp.mean(values, axis=-1, keepdims=True)
    centered = values - mean
    var = jnp.mean(centered * centered, axis=-1, keepdims=True)
    return centered * lax.rsqrt(var + eps)


def shifted(size, step):
    return [(i, (i + step) % size) for i in range(size)]


def prepare_kernel(tokens_ref, w_ref, sw_ref, normed_ref, ws_ref):
    normed_ref[...] = layer_norm(tokens_ref[...].astype(jnp.float32)).astype(jnp.bfloat16)
    ws_ref[...] = lax.dot_general(
        sw_ref[...],
        w_ref[...].astype(jnp.float32),
        (((1,), (1,)), ((), ())),
        precision=lax.Precision.HIGHEST,
        preferred_element_type=jnp.float32,
    )


def prepare(tokens, w_out, score_w, steps=4):
    rows, width = tokens.shape
    tile, part = rows // steps, width // steps
    return pl.pallas_call(
        prepare_kernel,
        grid=(steps,),
        in_specs=[
            pl.BlockSpec((tile, width), lambda i: (i, 0)),
            pl.BlockSpec((part, width), lambda i: (i, 0)),
            pl.BlockSpec((1, width), lambda i: (0, 0)),
        ],
        out_specs=[pl.BlockSpec((tile, width), lambda i: (i, 0)), pl.BlockSpec((1, part), lambda i: (0, i))],
        out_shape=[
            jax.ShapeDtypeStruct((rows, width), jnp.bfloat16),
            jax.ShapeDtypeStruct((1, width), jnp.float32),
        ],
        compiler_params=params(),
        cost_estimate=pl.CostEstimate(flops=2**27, bytes_accessed=6 * 2**20, transcendentals=rows),
    )(tokens, w_out, score_w)


def project_kernel(place_ref, normed_ref, w_ref, *rest):
    x = 0.5 * jnp.dot(normed_ref[...], w_ref[0], preferred_element_type=jnp.float32)
    rest[-1][...] = (x + x * jnp.tanh(x)).astype(jnp.bfloat16)


def project(normed, blocks, place, total, into=None):
    rows, width = normed.shape
    many, _, columns = blocks.shape
    more = into is not None
    return pl.pallas_call(
        project_kernel,
        grid_spec=pltpu.PrefetchScalarGridSpec(
            num_scalar_prefetch=1,
            grid=(many,),
            in_specs=[
                pl.BlockSpec((rows, width), lambda j, o: (0, 0)),
                pl.BlockSpec((1, width, columns), lambda j, o: (j, 0, 0)),
            ]
            + [pl.BlockSpec(memory_space=pl.ANY)] * more,
            out_specs=pl.BlockSpec((rows, columns), lambda j, o: (0, o[j])),
        ),
        out_shape=jax.ShapeDtypeStruct((rows, total), jnp.bfloat16),
        input_output_aliases={3: 0} if more else {},
        compiler_params=params(),
        cost_estimate=pl.CostEstimate(
            flops=2 * rows * width * many * columns, bytes_accessed=5 * 2**20, transcendentals=rows * many * columns
        ),
    )(place, normed, blocks, *([into] if more else []))


def copies_kernel(*refs):
    ins, out, held, into, back = refs[:-4], refs[-4], refs[-3], refs[-2], refs[-1]
    reads = [pltpu.make_async_copy(ref, held.at[j], into.at[j]) for j, ref in enumerate(ins)]
    for read in reads:
        read.start()
    writes = []
    for j, read in enumerate(reads):
        read.wait()
        for i in range(out.shape[0]):
            write = pltpu.make_async_copy(held.at[j], out.at[i, j], back.at[i, j])
            write.start()
            writes.append(write)
    for write in writes:
        write.wait()


def copies(times, *blocks):
    held = (len(blocks),) + blocks[0].shape
    return pl.pallas_call(
        copies_kernel,
        in_specs=[pl.BlockSpec(memory_space=pl.ANY)] * len(blocks),
        out_specs=pl.BlockSpec(memory_space=pl.ANY),
        out_shape=jax.ShapeDtypeStruct((times,) + held, blocks[0].dtype),
        scratch_shapes=[
            pltpu.VMEM(held, blocks[0].dtype),
            pltpu.SemaphoreType.DMA((len(blocks),)),
            pltpu.SemaphoreType.DMA((times, len(blocks))),
        ],
        compiler_params=params(),
        cost_estimate=pl.CostEstimate(flops=0, bytes_accessed=2**22, transcendentals=0),
    )(*blocks)


def side_by_side(refs):
    blocks = [ref[...].reshape(-1, ref.shape[-1]) for ref in refs]
    return jnp.concatenate(blocks, axis=0) if len(blocks) > 1 else blocks[0]


def weigh(q, k, v, factor):
    s = lax.dot_general(q, k, (((1,), (1,)), ((), ())), preferred_element_type=jnp.float32)
    w = (s * jnp.tanh(s * (0.5 * factor)) + s).astype(jnp.bfloat16)
    return jnp.dot(w, v, preferred_element_type=jnp.float32)


def partial_kernel(*refs, count, factor, tile, more):
    q_ref, ks, vs, out_ref = refs[0], refs[1 : 1 + count], refs[1 + count : 1 + 2 * count], refs[-1]
    k, v = side_by_side(ks), side_by_side(vs)
    for r in range(0, q_ref.shape[0], tile):
        sums = weigh(q_ref[r : r + tile, :], k, v, factor)
        if more:
            sums += refs[-2][r : r + tile, :]
        out_ref[r : r + tile, :] = sums


def key_specs(arrays, head, column):
    keys = [pl.BlockSpec((a.shape[0], a.shape[1] // 2, head), lambda h: (0, 0, column(h))) for a in arrays]
    values = [pl.BlockSpec((a.shape[0], a.shape[1] // 2, head), lambda h: (0, 1, column(h))) for a in arrays]
    return keys + values


def attend_part(proj, first, arrays, before=None):
    rows, head = proj.shape[0], proj.shape[1] // (2 * HEADS)
    heads = arrays[0].shape[2] // head
    keys = sum(a.shape[0] * a.shape[1] // 2 for a in arrays)
    sums = pl.BlockSpec((rows, head), lambda h: (0, h))
    more = before is not None
    return pl.pallas_call(
        functools.partial(partial_kernel, count=len(arrays), factor=float(head) ** -0.5, tile=256, more=more),
        grid=(heads,),
        in_specs=[pl.BlockSpec((rows, head), lambda h: (0, HEADS + first + h))]
        + key_specs(arrays, head, lambda h: h)
        + [sums] * more,
        out_specs=sums,
        out_shape=jax.ShapeDtypeStruct((rows, heads * head), jnp.float32),
        compiler_params=params(),
        cost_estimate=pl.CostEstimate(
            flops=8 * rows * keys * heads * head, bytes_accessed=4 * 2**20, transcendentals=rows * keys * heads
        ),
    )(proj, *arrays, *arrays, *([before] if more else []))


def finish_kernel(*refs, count, factor, tile):
    q_ref, ks, vs = refs[0], refs[1 : 1 + count], refs[1 + count : 1 + 2 * count]
    sums_ref, done_ref, gate_ref, tokens_ref, ws_ref, sw_ref, scale_ref, live_ref, gated_ref, score_ref, attn = refs[1 + 2 * count :]
    h = pl.program_id(0)
    rows = q_ref.shape[0]
    k, v = side_by_side(ks), side_by_side(vs)
    for r in range(0, rows, tile):
        attn[h, r : r + tile, :] = weigh(q_ref[r : r + tile, :], k, v, factor) + sums_ref[r : r + tile, :]

    @pl.when(h == pl.num_programs(0) - 1)
    def _():
        for r in range(0, rows, tile):
            heads = [attn[i, r : r + tile, :] for i in range(attn.shape[0])] + [done_ref[r : r + tile, :]]
            whole = jnp.concatenate(heads, axis=1) * scale_ref[0]
            gated = (layer_norm(whole) * gate_ref[r : r + tile, :].astype(jnp.float32)).astype(jnp.bfloat16)
            gated_ref[r : r + tile, :] = gated
            total = gated.astype(jnp.float32) * ws_ref[...]
            total += tokens_ref[r : r + tile, :].astype(jnp.float32) * sw_ref[...]
            slots = r + lax.broadcasted_iota(jnp.int32, (1, tile), 1)
            score = jnp.sum(total, axis=-1).reshape(1, -1)
            score = jnp.where(slots < live_ref[0], score, 0.0)
            score_ref[:, :, r : r + tile] = jnp.broadcast_to(score[None], (score_ref.shape[0], 1, tile))


def finish(proj, arrays, sums, done, tokens, ws, score_w, scale, live, parts):
    rows, width = tokens.shape
    head = width // HEADS
    left = arrays[0].shape[2] // head
    whole = pl.BlockSpec((rows, width), lambda h: (0, 0))
    line = pl.BlockSpec((1, width), lambda h: (0, 0))
    return pl.pallas_call(
        functools.partial(finish_kernel, count=len(arrays), factor=float(head) ** -0.5, tile=256),
        grid=(left,),
        in_specs=[pl.BlockSpec((rows, head), lambda h: (0, HEADS + h))]
        + key_specs(arrays, head, lambda h: h)
        + [
            pl.BlockSpec((rows, head), lambda h: (0, h)),
            pl.BlockSpec(done.shape, lambda h: (0, 0)),
            whole,
            whole,
            line,
            line,
            pl.BlockSpec(memory_space=pltpu.SMEM),
            pl.BlockSpec(memory_space=pltpu.SMEM),
        ],
        out_specs=[whole, pl.BlockSpec((parts, 1, rows), lambda h: (0, 0, 0))],
        out_shape=[
            jax.ShapeDtypeStruct((rows, width), jnp.bfloat16),
            jax.ShapeDtypeStruct((parts, 1, rows), jnp.float32),
        ],
        scratch_shapes=[pltpu.VMEM((left, rows, head), jnp.float32)],
        compiler_params=params(),
        cost_estimate=pl.CostEstimate(flops=2**32, bytes_accessed=12 * 2**20, transcendentals=2**22),
    )(proj, *arrays, *arrays, sums, done, proj, tokens, ws, score_w, scale, live)


def out_kernel(gated_ref, w_ref, tokens_ref, out_ref):
    y = tokens_ref[...].astype(jnp.float32) + jnp.dot(gated_ref[...], w_ref[...], preferred_element_type=jnp.float32)
    out_ref[...] = y.astype(jnp.bfloat16)


def project_out(gated, w_out, tokens, tile=256):
    rows, width = tokens.shape
    return pl.pallas_call(
        out_kernel,
        grid=(rows // tile,),
        in_specs=[
            pl.BlockSpec((tile, width), lambda i: (i, 0)),
            pl.BlockSpec((width, width), lambda i: (0, 0)),
            pl.BlockSpec((tile, width), lambda i: (i, 0)),
        ],
        out_specs=pl.BlockSpec((tile, width), lambda i: (i, 0)),
        out_shape=jax.ShapeDtypeStruct((rows, width), jnp.bfloat16),
        compiler_params=params(),
        cost_estimate=pl.CostEstimate(flops=2 * rows * width * width, bytes_accessed=7 * 2**20, transcendentals=0),
    )(gated, w_out, tokens)


def pick_kernel(index_ref, table_ref, out_ref):
    index = index_ref[...]
    count = index.shape[0]
    height, lanes = table_ref.shape
    onehot = (lax.broadcasted_iota(jnp.int32, (count, height), 1) == index // lanes).astype(jnp.bfloat16)
    rest = table_ref[...]
    rows = jnp.zeros((count, lanes), jnp.float32)
    for _ in range(3):
        part = rest.astype(jnp.bfloat16)
        rows += jnp.dot(onehot, part, preferred_element_type=jnp.float32)
        rest = rest - part.astype(jnp.float32)
    mine = lax.broadcasted_iota(jnp.int32, (count, lanes), 1) == index % lanes
    out_ref[...] = jnp.sum(jnp.where(mine, rows, 0.0), axis=-1).reshape(1, -1)


def pick(index, table):
    count = index.shape[0]
    return pl.pallas_call(
        pick_kernel,
        out_shape=jax.ShapeDtypeStruct((1, count), jnp.float32),
        compiler_params=params(),
    )(index.reshape(count, 1), table.reshape(-1, 128))


HEADS_A = 5
tie = lax.optimization_barrier


def shift(block, axis, step):
    return lax.ppermute(block, axis, shifted(lax.axis_size(axis), step))


def on_device(
    cand_tokens, hist_keys, hist_values, hist_len, cand_count, impressions, w_proj, w_out, score_w
):
    tokens = cand_tokens[0]
    rows, width = tokens.shape
    own = hist_keys.shape[1]
    head = width // HEADS
    cand = lax.axis_index(("z", "x"))
    core = lax.axis_index("core")
    many_y, many_core = lax.axis_size("y"), lax.axis_size("core")
    parts, many_z, many_x = lax.axis_size(("z", "x")), lax.axis_size("z"), lax.axis_size("x")

    position = cand * own + jnp.arange(own, dtype=jnp.int32)
    keys = jnp.where((position < hist_len[0])[:, None], hist_keys[0], jnp.zeros((), jnp.bfloat16))
    values = hist_values[0]
    cut = HEADS_A * head
    mine_a = jnp.concatenate([keys[:, :cut], values[:, :cut]], axis=0)
    mine_b = jnp.concatenate([keys[:, cut:], values[:, cut:]], axis=0)

    xs = [mine_a, shift(mine_a, "x", 1), shift(mine_a, "x", -1), shift(mine_a, "x", 2)]
    zs = lax.all_to_all(copies(many_z, mine_b)[:, 0], "z", split_axis=0, concat_axis=0, tiled=True)
    w_near = [w_proj, shift(w_proj, "y", 1), shift(w_proj, "y", -1)]
    w_far, xs, w_near = tie((w_proj, xs, w_near))
    w_parts = w_near + [shift(w_far, "y", 2)]
    normed, ws = prepare(tokens, w_out, score_w[None, :])

    p = q = start = copies(1, *xs)[0]
    zs = copies(many_x, zs)[:, 0]
    p, q, w_parts, normed, zs = tie((shift(p, "z", 1), shift(q, "z", -1), w_parts, normed, zs))
    w_mine = copies(1, *w_parts)[0]
    b = lax.all_to_all(zs, "x", split_axis=0, concat_axis=0, tiled=True)
    b = b.reshape(-1, *mine_b.shape)
    block = (lax.axis_index("y") - jnp.array([0, 1, -1, 2])) % many_y * many_core
    proj = project(normed, w_mine, (block + core).astype(jnp.int32), 2 * width)
    w_other = lax.ppermute(w_mine, "core", [(0, 1), (1, 0)])
    near = [start, p, q]
    p, q = shift(p, "z", 1), shift(q, "z", -1)
    proj = project(normed, w_other, (block + 1 - core).astype(jnp.int32), 2 * width, proj)
    p, q, proj = tie((p, q, proj))
    middle = [p, q]
    p, q = shift(p, "z", 1), shift(q, "z", -1)
    sums = attend_part(proj, 0, near)
    p, q, sums = tie((p, q, sums))
    half = many_x // 2
    far = [p, q, shift(p[:half], "z", 1), shift(q[half:], "z", -1)]
    sums = attend_part(proj, 0, middle, sums)
    done = attend_part(proj, HEADS_A, [b])

    scale = 0.5 * float(head) ** -0.5 / hist_len.astype(jnp.float32)
    live = cand_count - cand * rows
    gated, sent = finish(proj, far, sums, done, tokens, ws, score_w[None, :], scale, live, parts)
    every = lax.all_to_all(sent, ("z", "x"), split_axis=0, concat_axis=0, tiled=True)
    layer_out = project_out(gated, w_out, tokens)
    ranked = pick(impressions[0], every)
    return (layer_out[None], ranked)


def solution(mesh):
    split = Mesh(mesh.devices.reshape(4, 2, 8, 4), ("y", "core", "z", "x"))
    users, cands = ("y", "core"), ("z", "x")
    return jax.shard_map(
        on_device,
        mesh=split,
        in_specs=(
            P(users, cands, None),
            P(users, cands, None),
            P(users, cands, None),
            P(users),
            P(users),
            P(users, cands),
            P(None, users),
            P(),
            P(),
        ),
        out_specs=(P(users, cands, None), P(users, cands)),
        check_vma=False,
    )
```

time: 165 us -> 149 us (0.903)
  waiting for transfers between devices: 79.5 us -> 22.7 us
  starting transfers between devices: 10.9 us -> 43.4 us
  Pallas kernels: 37.9 us -> 68.9 us
  between operations: 15.5 us -> 2.26 us
  local copies, waits for them, and re-layouts: 18.2 us -> 7.69 us
    all_gather x1 -> x0, waiting for transfers between devices: 57.8 us -> none  [on_device(): history = lax.all_gather(mine, ('z', 'x'), axis=0, tiled=False)]
    pallas_call x2 -> x9, Pallas kernels: 24.6 us -> 48.8 us  [the longest x3 22.3 us: attend_part(): pl.pallas_call(functools.partial(partial_kernel, count=len(arrays), facto...]
    ppermute x7 -> x15, starting transfers between devices: 5.19 us -> 22.7 us  [the longest x14 22.6 us: shift(): return lax.ppermute(block, axis, shifted(lax.axis_size(axis), step))]
    unnamed x27 -> x28, local copies, waits for them, and re-layouts: 16.5 us -> 3.19 us
    all_to_all x0 -> x2, starting transfers between devices: none -> 12.8 us  [the longest x1 8.48 us: on_device(): lax.all_to_all(copies(many_z, mine_b)[:, 0], 'z', split_axis=0, concat_ax...]
    slice x0 -> x6, local copies, waits for them, and re-layouts: none -> 3.56 us  [the longest x2 2.73 us: on_device(): far = [p, q, shift(p[:half], 'z', 1), shift(q[half:], 'z', -1)]]
    pallas_call x1 -> x2, Pallas kernels: 8.93 us -> 12.2 us  [project(): pl.pallas_call(project_kernel, grid_spec=pltpu.PrefetchScalarGridSpec(num...]
    pallas_call x1, Pallas kernels: 3.01 us -> 5.55 us  [project_out(): pl.pallas_call(out_kernel, grid=(rows // tile,), in_specs=[pl.BlockSpec((...]
  transfers between devices with their start and end apart: 9 -> 18, of which waited for: 5 -> 10; matrix products, arithmetic and copies ran while one was open for 6% -> 3% of each run, Pallas kernels for 7% -> 35%
where the time goes in v2:
time: 149 us; the launch traced here: 148 us
  Pallas kernels  68.9 us (46%)
  starting transfers between devices  43.4 us (29%)
  waiting for transfers between devices  22.7 us (15%)
  local copies, waits for them, and re-layouts  7.69 us (5%)
  other arithmetic  2.76 us (2%)
  between operations  2.26 us (2%)
    ppermute x14, starting transfers between devices, shift(): return lax.ppermute(block, axis, shifted(lax.axis_size(axis), step))  22.6 us
    pallas_call x3, Pallas kernels, attend_part(): pl.pallas_call(functools.partial(partial_kernel, count=len(arrays), facto...  22.3 us
    ppermute x14, waiting for transfers between devices, shift(): return lax.ppermute(block, axis, shifted(lax.axis_size(axis), step))  19 us
    pallas_call x2, Pallas kernels, project(): pl.pallas_call(project_kernel, grid_spec=pltpu.PrefetchScalarGridSpec(num...  12.2 us
    pallas_call x1, Pallas kernels, finish(): pl.pallas_call(functools.partial(finish_kernel, count=len(arrays), factor...  11.2 us
    pallas_call x4, Pallas kernels, copies(): pl.pallas_call(copies_kernel, in_specs=[pl.BlockSpec(memory_space=pl.ANY)...  9.24 us
    all_to_all x1, starting transfers between devices, on_device(): lax.all_to_all(copies(many_z, mine_b)[:, 0], 'z', split_axis=0, concat_ax...  8.48 us
    all_to_all x1, starting transfers between devices, on_device(): lax.all_to_all(sent, ('z', 'x'), split_axis=0, concat_axis=0, tiled=True)  7.9 us
  transfers between devices with their start and end apart: 18, of which 10 were waited for; matrix products, arithmetic and copies ran while one was open for 3% of the time, Pallas kernels for 35%

profile of v2, /device:TPU:8, one launch (start us, length us, event | category | flops | bytes accessed | tf_op | source)
XLA Modules:
  0.0 147.7 jit_solution(12211842067115117070)
XLA Ops:
  3.8 1.9 %shard_map.115 = bf16[8,1,128,384]{3,2,1,0:T(8,128)(2,1)} custom-call(bf16[128,384]{1,0:T(8,128)(2,1)} %pad_maximum_fusion.1.refs_0_), custom_call_target="tpu_custom_call" | custom-call | bytes 4194304 | tf_op jit(solution)/shard_map/pallas_call | solution.py:111
  5.7 8.5 %all-to-all-start = ((bf16[8,128,384]{2,1,0:T(8,128)(2,1)}), bf16[8,128,384]{2,1,0:T(8,128)(2,1)S(1)}, u32[]{:S(2)}, u32[]{:S(2)}) async-start(bf16[8,128,384]{2,1,0:T(8,128)(2,1)} %bitcast.23), calls=%async_computation | async-start | bytes 1572864 | tf_op jit(solution)/shard_map/all_to_all | solution.py:304
  21.5 2.2 %collective-permute-done.refs_1_ = bf16[128,640]{1,0:T(8,128)(2,1)S(1)} collective-permute-done((bf16[128,640]{1,0:T(8,128)(2,1)S(1)}, bf16[128,640]{1,0:T(8,128)(2,1)S(1)}, u32[]{:S(2)}, u32[]{:S(2)}) %collective-permute-start) | collective-permute-done | bytes 163872 | tf_op jit(solution)/shard_map/ppermute | solution.py:281
  24.6 2.9 %collective-permute-done.2.refs_3_ = bf16[128,640]{1,0:T(8,128)(2,1)S(1)} collective-permute-done((bf16[128,640]{1,0:T(8,128)(2,1)S(1)}, bf16[128,640]{1,0:T(8,128)(2,1)S(1)}, u32[]{:S(2)}, u32[]{:S(2)}) %collective-permute-start.2) | collective-permute-done | bytes 163872 | tf_op jit(solution)/shard_map/ppermute | solution.py:281
  29.0 2.1 %shard_map.113 = bf16[1,4,128,640]{3,2,1,0:T(8,128)(2,1)} custom-call(bf16[128,640]{1,0:T(8,128)(2,1)} %copy-done.2, bf16[128,640]{1,0:T(8,128)(2,1)} %copy-done.8, bf16[128,640]{1,0:T(8,128)(2,1)} %copy-done.9, bf16[128,640]{1,0:T(8,128)(2,1)} %copy-done.10), custom_call_target="tpu_custom_call" | custom-call | bytes 4194304 | tf_op jit(solution)/shard_map/pallas_call | solution.py:111
  34.4 2.3 %collective-permute-start.7 = (bf16[1024,256]{1,0:T(8,128)(2,1)S(1)}, bf16[1024,256]{1,0:T(8,128)(2,1)S(1)}, u32[]{:S(2)}, u32[]{:S(2)}) collective-permute-start(bf16[1024,256]{1,0:T(8,128)(2,1)S(1)} %copy-done.3), channel_id=1, source_target_pairs={{0,128},{64,192},{128,0},{192,64},{1,129},{65,193},{129,1},{193,65... | collective-permute-start | bytes 1572872 | tf_op jit(solution)/shard_map/ppermute | solution.py:281
  36.7 6.0 %shard_map.114 = (bf16[768,1024]{1,0:T(8,128)(2,1)}, f32[1,1024]{1,0:T(1,128)}) custom-call(bf16[768,1024]{1,0:T(8,128)(2,1)} %bitcast.18, bf16[1024,1024]{1,0:T(8,128)(2,1)} %w_ref.3, f32[1,1024]{1,0:T(1,128)} %bitcast.32), custom_call_target="tpu_custom_call" | custom-call | flops 134217728 | bytes 6291456 | tf_op jit(solution)/shard_map/pallas_call | solution.py:45
  43.6 2.8 %shard_map.116 = bf16[4,1,8,128,384]{4,3,2,1,0:T(8,128)(2,1)} custom-call(bf16[8,128,384]{2,1,0:T(8,128)(2,1)} %copy-done.1), custom_call_target="tpu_custom_call" | custom-call | bytes 4194304 | tf_op jit(solution)/shard_map/pallas_call | solution.py:111
  47.5 2.2 %collective-permute-done.5.refs_2_.refs_5_ = bf16[4,128,640]{2,1,0:T(8,128)(2,1)} collective-permute-done((bf16[4,128,640]{2,1,0:T(8,128)(2,1)}, bf16[4,128,640]{2,1,0:T(8,128)(2,1)}, u32[]{:S(2)}, u32[]{:S(2)}) %collective-permute-start.5) | collective-permute-done | bytes 655392 | tf_op jit(solution)/shard_map/ppermute | solution.py:281
  49.7 2.5 %shard_map.117 = bf16[1,4,1024,256]{3,2,1,0:T(8,128)(2,1)} custom-call(bf16[1024,256]{1,0:T(8,128)(2,1)} %refs_0_, bf16[1024,256]{1,0:T(8,128)(2,1)} %copy-done.4, bf16[1024,256]{1,0:T(8,128)(2,1)} %copy-done.5, bf16[1024,256]{1,0:T(8,128)(2,1)} %copy-done.6), custom_call_target="tpu_custom_call" | custom-call | bytes 4194304 | tf_op jit(solution)/shard_map/pallas_call | solution.py:111
  52.3 4.3 %all-to-all-start.1 = ((bf16[4,8,128,384]{3,2,1,0:T(8,128)(2,1)}), bf16[4,8,128,384]{3,2,1,0:T(8,128)(2,1)S(1)}, u32[]{:S(2)}, u32[]{:S(2)}) async-start(bf16[4,8,128,384]{3,2,1,0:T(8,128)(2,1)} %bitcast.7), calls=%async_computation.1 | async-start | bytes 6291456 | tf_op jit(solution)/shard_map/all_to_all | solution.py:314
  57.1 2.8 %collective-permute-start.9 = (bf16[4,128,640]{2,1,0:T(8,128)(2,1)}, bf16[4,128,640]{2,1,0:T(8,128)(2,1)}, u32[]{:S(2)}, u32[]{:S(2)}) collective-permute-start(bf16[4,128,640]{2,1,0:T(8,128)(2,1)} %collective-permute-done.6.refs_3_.refs_6_), channel_id=1, source_target_pairs={{0,28},{4,0},{8,4},{12,8},{16,12},{20,16},{24,20},{28,24},{1,29},{... | collective-permute-start | bytes 1966088 | tf_op jit(solution)/shard_map/ppermute | solution.py:281
  61.0 6.1 %shard_map.118.rest_0_ = bf16[768,2048]{1,0:T(8,128)(2,1)} custom-call(s32[4]{0:T(128)} %get-tuple-element.54.place_ref, bf16[768,1024]{1,0:T(8,128)(2,1)} %get-tuple-element.39.normed_ref, bf16[4,1024,256]{2,1,0:T(8,128)(2,1)} %bitcast.17), custom_call_target="tpu_custom_call" | custom-call | flops 1610612736 | bytes 5242880 | tf_op jit(solution)/shard_map/pallas_call | solution.py:72
  67.1 6.1 %shard_map.119.refs_0_.refs_11_ = bf16[768,2048]{1,0:T(8,128)(2,1)} custom-call(s32[4]{0:T(128)} %add_subtract_fusion.place_ref, bf16[768,1024]{1,0:T(8,128)(2,1)} %get-tuple-element.39.normed_ref, bf16[4,1024,256]{2,1,0:T(8,128)(2,1)} %collective-permute-done.10.w_ref, bf16[768,2048]{1,0:T(8,128)(2,1)} %shard_map.118.rest_0_), custom_call_target="tpu_custom_call", output_to_operand_aliasing={{}: (3, {})} | custom-call | flops 1610612736 | bytes 5242880 | tf_op jit(solution)/shard_map/pallas_call | solution.py:72
  73.2 1.9 %collective-permute-done.8.refs_1_.refs_3_ = bf16[4,128,640]{2,1,0:T(8,128)(2,1)} collective-permute-done((bf16[4,128,640]{2,1,0:T(8,128)(2,1)}, bf16[4,128,640]{2,1,0:T(8,128)(2,1)}, u32[]{:S(2)}, u32[]{:S(2)}) %collective-permute-start.8) | collective-permute-done | bytes 655392 | tf_op jit(solution)/shard_map/ppermute | solution.py:281
  78.9 7.2 %shard_map.120.refs_5_ = f32[768,640]{1,0:T(8,128)} custom-call(bf16[768,2048]{1,0:T(8,128)(2,1)} %shard_map.119.refs_0_.refs_11_, bf16[4,128,640]{2,1,0:T(8,128)(2,1)} %bitcast.27, bf16[4,128,640]{2,1,0:T(8,128)(2,1)} %collective-permute-done.5.refs_2_.refs_5_, bf16[4,128,640]{2,1,0:T(8,128)(2,1)} %collective-permute-done.6.refs_3_.refs_6_, ...), custom_call_target="tpu_custom_call" | custom-call | flops 3019898880 | bytes 4194304 | tf_op jit(solution)/shard_map/pallas_call | solution.py:159
  86.1 6.4 %collective-permute-done.11.refs_1_.refs_5_ = bf16[4,128,640]{2,1,0:T(8,128)(2,1)} collective-permute-done((bf16[4,128,640]{2,1,0:T(8,128)(2,1)}, bf16[4,128,640]{2,1,0:T(8,128)(2,1)}, u32[]{:S(2)}, u32[]{:S(2)}) %collective-permute-start.11) | collective-permute-done | bytes 655392 | tf_op jit(solution)/shard_map/ppermute | solution.py:281
  100.2 7.8 %shard_map.122.refs_10_ = f32[768,384]{1,0:T(8,128)} custom-call(bf16[768,2048]{1,0:T(8,128)(2,1)} %shard_map.119.refs_0_.refs_11_, bf16[32,128,384]{2,1,0:T(8,128)(2,1)} %bitcast.21, bf16[32,128,384]{2,1,0:T(8,128)(2,1)} %bitcast.22), custom_call_target="tpu_custom_call" | custom-call | flops 4831838208 | bytes 4194304 | tf_op jit(solution)/shard_map/pallas_call | solution.py:159
  108.1 7.3 %shard_map.121.refs_9_ = f32[768,640]{1,0:T(8,128)} custom-call(bf16[768,2048]{1,0:T(8,128)(2,1)} %shard_map.119.refs_0_.refs_11_, bf16[4,128,640]{2,1,0:T(8,128)(2,1)} %collective-permute-done.8.refs_1_.refs_3_, bf16[4,128,640]{2,1,0:T(8,128)(2,1)} %collective-permute-done.9.refs_2_.refs_4_, bf16[4,128,640]{2,1,0:T(8,128)(2,1)} %collective-permute-done.8.refs_1_.refs_3_, ...), custom_call_target="tpu_custom_call" | custom-call | flops 2013265920 | bytes 4194304 | tf_op jit(solution)/shard_map/pallas_call | solution.py:159
  115.4 11.2 %shard_map.123 = (bf16[768,1024]{1,0:T(8,128)(2,1)}, f32[32,1,768]{2,1,0:T(1,128)}) custom-call(bf16[768,2048]{1,0:T(8,128)(2,1)} %shard_map.119.refs_0_.refs_11_, bf16[4,128,640]{2,1,0:T(8,128)(2,1)} %collective-permute-done.11.refs_1_.refs_5_, bf16[4,128,640]{2,1,0:T(8,128)(2,1)} %collective-permute-done.12.refs_2_.refs_6_, ...), custom_call_target="tpu_custom_call" | custom-call | flops 4294967296 | bytes 12582912 | tf_op jit(solution)/shard_map/pallas_call | solution.py:204
  126.6 7.9 %all-to-all-start.2 = ((f32[32,1,768]{2,1,0:T(1,128)}), f32[32,1,768]{2,1,0:T(1,128)S(1)}, u32[]{:S(2)}, u32[]{:S(2)}) async-start(f32[32,1,768]{2,1,0:T(1,128)} %get-tuple-element.53), calls=%async_computation.2 | async-start | bytes 196608 | tf_op jit(solution)/shard_map/all_to_all | solution.py:335
  135.5 5.6 %shard_map.124 = bf16[768,1024]{1,0:T(8,128)(2,1)} custom-call(bf16[768,1024]{1,0:T(8,128)(2,1)} %get-tuple-element.52.gated_ref, bf16[1024,1024]{1,0:T(8,128)(2,1)} %w_ref.3, bf16[768,1024]{1,0:T(8,128)(2,1)} %bitcast.20), custom_call_target="tpu_custom_call" | custom-call | flops 1610612736 | bytes 7340032 | tf_op jit(solution)/shard_map/pallas_call | solution.py:237
  141.0 3.7 %all-to-all-done.2 = f32[32,1,768]{2,1,0:T(1,128)S(1)} async-done(((f32[32,1,768]{2,1,0:T(1,128)}), f32[32,1,768]{2,1,0:T(1,128)S(1)}, u32[]{:S(2)}, u32[]{:S(2)}) %all-to-all-start.2) | async-done | bytes 98336 | tf_op jit(solution)/shard_map/all_to_all | solution.py:335
  145.4 2.3 %shard_map.125 = f32[1,768]{1,0:T(1,128)} custom-call(s32[768,1]{1,0:T(8,128)} %copy.13.index_ref, f32[192,128]{1,0:T(8,128)} %bitcast.29), custom_call_target="tpu_custom_call" | custom-call | tf_op jit(solution)/shard_map/pallas_call | solution.py:269
  (66 shorter events, 31.5 us)
Async XLA Ops:
  0.6 15.7 %copy-start.11 = (bf16[1,64,1024]{2,1,0:T(8,128)(2,1)S(1)}, bf16[1,64,1024]{2,1,0:T(8,128)(2,1)}, u32[]{:S(2)}) copy-start(bf16[1,64,1024]{2,1,0:T(8,128)(2,1)} %param.12) | copy-start | bytes 393220
  0.6 13.5 %copy-start.3 = (bf16[1024,256]{1,0:T(8,128)(2,1)S(1)}, bf16[1024,256]{1,0:T(8,128)(2,1)}, u32[]{:S(2)}) copy-start(bf16[1024,256]{1,0:T(8,128)(2,1)} %refs_0_) | copy-start | bytes 1572868
  5.7 37.0 %all-to-all-start = ((bf16[8,128,384]{2,1,0:T(8,128)(2,1)}), bf16[8,128,384]{2,1,0:T(8,128)(2,1)S(1)}, u32[]{:S(2)}, u32[]{:S(2)}) async-start(bf16[8,128,384]{2,1,0:T(8,128)(2,1)} %bitcast.23), calls=%async_computation | async-start | bytes 1572864 | tf_op jit(solution)/shard_map/all_to_all | solution.py:304
  14.2 13.5 %collective-permute-start.3 = (bf16[1024,256]{1,0:T(8,128)(2,1)S(1)}, bf16[1024,256]{1,0:T(8,128)(2,1)S(1)}, u32[]{:S(2)}, u32[]{:S(2)}) collective-permute-start(bf16[1024,256]{1,0:T(8,128)(2,1)S(1)} %copy-done.3), channel_id=1, source_target_pairs={{0,64},{64,128},{128,192},{192,0},{1,65},{65,129},{129,193},{193,1... | collective-permute-start | bytes 1572872 | tf_op jit(solution)/shard_map/ppermute | solution.py:281
  15.8 13.1 %collective-permute-start.4 = (bf16[1024,256]{1,0:T(8,128)(2,1)S(1)}, bf16[1024,256]{1,0:T(8,128)(2,1)S(1)}, u32[]{:S(2)}, u32[]{:S(2)}) collective-permute-start(bf16[1024,256]{1,0:T(8,128)(2,1)S(1)} %copy-done.3), channel_id=1, source_target_pairs={{0,192},{64,0},{128,64},{192,128},{1,193},{65,1},{129,65},{193,129... | collective-permute-start | bytes 1572872 | tf_op jit(solution)/shard_map/ppermute | solution.py:281
  16.4 12.6 %copy-start.2 = (bf16[128,640]{1,0:T(8,128)(2,1)}, bf16[128,640]{1,0:T(8,128)(2,1)S(1)}, u32[]{:S(2)}) copy-start(bf16[128,640]{1,0:T(8,128)(2,1)S(1)} %pad_maximum_fusion.refs_0_) | copy-start | bytes 491524
  16.4 7.4 %collective-permute-start = (bf16[128,640]{1,0:T(8,128)(2,1)S(1)}, bf16[128,640]{1,0:T(8,128)(2,1)S(1)}, u32[]{:S(2)}, u32[]{:S(2)}) collective-permute-start(bf16[128,640]{1,0:T(8,128)(2,1)S(1)} %pad_maximum_fusion.refs_0_), channel_id=1, source_target_pairs={{0,1},{1,2},{2,3},{3,0},{4,5},{5,6},{6,7},{7,4},{8,9},{9,10},{10,1... | collective-permute-start | bytes 491528 | tf_op jit(solution)/shard_map/ppermute | solution.py:281
  17.9 6.7 %collective-permute-start.1 = (bf16[128,640]{1,0:T(8,128)(2,1)S(1)}, bf16[128,640]{1,0:T(8,128)(2,1)S(1)}, u32[]{:S(2)}, u32[]{:S(2)}) collective-permute-start(bf16[128,640]{1,0:T(8,128)(2,1)S(1)} %pad_maximum_fusion.refs_0_), channel_id=1, source_target_pairs={{0,3},{1,0},{2,1},{3,2},{4,7},{5,4},{6,5},{7,6},{8,11},{9,8},{10,9... | collective-permute-start | bytes 491528 | tf_op jit(solution)/shard_map/ppermute | solution.py:281
  19.7 7.8 %collective-permute-start.2 = (bf16[128,640]{1,0:T(8,128)(2,1)S(1)}, bf16[128,640]{1,0:T(8,128)(2,1)S(1)}, u32[]{:S(2)}, u32[]{:S(2)}) collective-permute-start(bf16[128,640]{1,0:T(8,128)(2,1)S(1)} %pad_maximum_fusion.refs_0_), channel_id=1, source_target_pairs={{0,2},{1,3},{2,0},{3,1},{4,6},{5,7},{6,4},{7,5},{8,10},{9,11},{10,... | collective-permute-start | bytes 491528 | tf_op jit(solution)/shard_map/ppermute | solution.py:281
  27.7 15.1 %copy-start.4 = (bf16[1024,256]{1,0:T(8,128)(2,1)}, bf16[1024,256]{1,0:T(8,128)(2,1)S(1)}, u32[]{:S(2)}) copy-start(bf16[1024,256]{1,0:T(8,128)(2,1)S(1)} %collective-permute-done.3.refs_1_) | copy-start | bytes 1572868
  29.0 13.7 %copy-start.5 = (bf16[1024,256]{1,0:T(8,128)(2,1)}, bf16[1024,256]{1,0:T(8,128)(2,1)S(1)}, u32[]{:S(2)}) copy-start(bf16[1024,256]{1,0:T(8,128)(2,1)S(1)} %collective-permute-done.4.refs_2_) | copy-start | bytes 1572868
  31.1 18.6 %collective-permute-start.5 = (bf16[4,128,640]{2,1,0:T(8,128)(2,1)}, bf16[4,128,640]{2,1,0:T(8,128)(2,1)}, u32[]{:S(2)}, u32[]{:S(2)}) collective-permute-start(bf16[4,128,640]{2,1,0:T(8,128)(2,1)} %bitcast.25), channel_id=1, source_target_pairs={{0,4},{4,8},{8,12},{12,16},{16,20},{20,24},{24,28},{28,0},{1,5},{5... | collective-permute-start | bytes 1966088 | tf_op jit(solution)/shard_map/ppermute | solution.py:281
  32.8 16.9 %collective-permute-start.6 = (bf16[4,128,640]{2,1,0:T(8,128)(2,1)}, bf16[4,128,640]{2,1,0:T(8,128)(2,1)}, u32[]{:S(2)}, u32[]{:S(2)}) collective-permute-start(bf16[4,128,640]{2,1,0:T(8,128)(2,1)} %bitcast.26), channel_id=1, source_target_pairs={{0,28},{4,0},{8,4},{12,8},{16,12},{20,16},{24,20},{28,24},{1,29},{... | collective-permute-start | bytes 1966088 | tf_op jit(solution)/shard_map/ppermute | solution.py:281
  34.4 13.1 %collective-permute-start.7 = (bf16[1024,256]{1,0:T(8,128)(2,1)S(1)}, bf16[1024,256]{1,0:T(8,128)(2,1)S(1)}, u32[]{:S(2)}, u32[]{:S(2)}) collective-permute-start(bf16[1024,256]{1,0:T(8,128)(2,1)S(1)} %copy-done.3), channel_id=1, source_target_pairs={{0,128},{64,192},{128,0},{192,64},{1,129},{65,193},{129,1},{193,65... | collective-permute-start | bytes 1572872 | tf_op jit(solution)/shard_map/ppermute | solution.py:281
  52.2 14.8 %collective-permute-start.10 = (bf16[4,1024,256]{2,1,0:T(8,128)(2,1)}, bf16[4,1024,256]{2,1,0:T(8,128)(2,1)}, u32[]{:S(2)}, u32[]{:S(2)}) collective-permute-start(bf16[4,1024,256]{2,1,0:T(8,128)(2,1)} %bitcast.16), channel_id=1, source_target_pairs={{0,32},{32,0},{1,33},{33,1},{2,34},{34,2},{3,35},{35,3},{4,36},{36... | collective-permute-start | bytes 6291464 | tf_op jit(solution)/shard_map/ppermute | solution.py:318
  52.3 46.3 %all-to-all-start.1 = ((bf16[4,8,128,384]{3,2,1,0:T(8,128)(2,1)}), bf16[4,8,128,384]{3,2,1,0:T(8,128)(2,1)S(1)}, u32[]{:S(2)}, u32[]{:S(2)}) async-start(bf16[4,8,128,384]{3,2,1,0:T(8,128)(2,1)} %bitcast.7), calls=%async_computation.1 | async-start | bytes 6291456 | tf_op jit(solution)/shard_map/all_to_all | solution.py:314
  56.6 18.4 %collective-permute-start.8 = (bf16[4,128,640]{2,1,0:T(8,128)(2,1)}, bf16[4,128,640]{2,1,0:T(8,128)(2,1)}, u32[]{:S(2)}, u32[]{:S(2)}) collective-permute-start(bf16[4,128,640]{2,1,0:T(8,128)(2,1)} %collective-permute-done.5.refs_2_.refs_5_), channel_id=1, source_target_pairs={{0,4},{4,8},{8,12},{12,16},{16,20},{20,24},{24,28},{28,0},{1,5},{5... | collective-permute-start | bytes 1966088 | tf_op jit(solution)/shard_map/ppermute | solution.py:281
  57.1 17.9 %collective-permute-start.9 = (bf16[4,128,640]{2,1,0:T(8,128)(2,1)}, bf16[4,128,640]{2,1,0:T(8,128)(2,1)}, u32[]{:S(2)}, u32[]{:S(2)}) collective-permute-start(bf16[4,128,640]{2,1,0:T(8,128)(2,1)} %collective-permute-done.6.refs_3_.refs_6_), channel_id=1, source_target_pairs={{0,28},{4,0},{8,4},{12,8},{16,12},{20,16},{24,20},{28,24},{1,29},{... | collective-permute-start | bytes 1966088 | tf_op jit(solution)/shard_map/ppermute | solution.py:281
  75.0 17.5 %collective-permute-start.11 = (bf16[4,128,640]{2,1,0:T(8,128)(2,1)}, bf16[4,128,640]{2,1,0:T(8,128)(2,1)}, u32[]{:S(2)}, u32[]{:S(2)}) collective-permute-start(bf16[4,128,640]{2,1,0:T(8,128)(2,1)} %collective-permute-done.8.refs_1_.refs_3_), channel_id=1, source_target_pairs={{0,4},{4,8},{8,12},{12,16},{16,20},{20,24},{24,28},{28,0},{1,5},{5... | collective-permute-start | bytes 1966088 | tf_op jit(solution)/shard_map/ppermute | solution.py:281
  76.4 16.1 %collective-permute-start.12 = (bf16[4,128,640]{2,1,0:T(8,128)(2,1)}, bf16[4,128,640]{2,1,0:T(8,128)(2,1)}, u32[]{:S(2)}, u32[]{:S(2)}) collective-permute-start(bf16[4,128,640]{2,1,0:T(8,128)(2,1)} %collective-permute-done.9.refs_2_.refs_4_), channel_id=1, source_target_pairs={{0,28},{4,0},{8,4},{12,8},{16,12},{20,16},{24,20},{28,24},{1,29},{... | collective-permute-start | bytes 1966088 | tf_op jit(solution)/shard_map/ppermute | solution.py:281
  93.6 21.8 %collective-permute-start.13 = (bf16[2,128,640]{2,1,0:T(8,128)(2,1)S(1)}, bf16[2,128,640]{2,1,0:T(8,128)(2,1)}, u32[]{:S(2)}, u32[]{:S(2)}) collective-permute-start(bf16[2,128,640]{2,1,0:T(8,128)(2,1)S(1)} %slice.22), channel_id=1, source_target_pairs={{0,4},{4,8},{8,12},{12,16},{16,20},{20,24},{24,28},{28,0},{1,5},{5... | collective-permute-start | bytes 983048 | tf_op jit(solution)/shard_map/ppermute | solution.py:281
  97.1 18.3 %collective-permute-start.14 = (bf16[2,128,640]{2,1,0:T(8,128)(2,1)}, bf16[2,128,640]{2,1,0:T(8,128)(2,1)}, u32[]{:S(2)}, u32[]{:S(2)}) collective-permute-start(bf16[2,128,640]{2,1,0:T(8,128)(2,1)} %slice.23), channel_id=1, source_target_pairs={{0,28},{4,0},{8,4},{12,8},{16,12},{20,16},{24,20},{28,24},{1,29},{... | collective-permute-start | bytes 983048 | tf_op jit(solution)/shard_map/ppermute | solution.py:281
  115.4 19.1 %copy-start.12 = (s32[1,768]{1,0:T(1,128)S(1)}, s32[1,768]{1,0:T(1,128)}, u32[]{:S(2)}) copy-start(s32[1,768]{1,0:T(1,128)} %param.15) | copy-start | bytes 9220
  126.6 18.1 %all-to-all-start.2 = ((f32[32,1,768]{2,1,0:T(1,128)}), f32[32,1,768]{2,1,0:T(1,128)S(1)}, u32[]{:S(2)}, u32[]{:S(2)}) async-start(f32[32,1,768]{2,1,0:T(1,128)} %get-tuple-element.53), calls=%async_computation.2 | async-start | bytes 196608 | tf_op jit(solution)/shard_map/all_to_all | solution.py:335
  (8 other events, 24.1 us)

commit v3 on v2

--- a/solution.py
+++ b/solution.py
@@ -10,7 +10,7 @@
 
 HEADS = 8
 eps = 1e-05
-VMEM_LIMIT = 58 * 2**20
+VMEM_LIMIT = 24 * 2**20
 
 
 def params():
@@ -60,34 +60,37 @@
     )(tokens, w_out, score_w)
 
 
-def project_kernel(place_ref, normed_ref, w_ref, *rest):
-    x = 0.5 * jnp.dot(normed_ref[...], w_ref[0], preferred_element_type=jnp.float32)
+def project_kernel(place_ref, normed_ref, first_ref, second_ref, *rest, count):
+    w = jnp.where(pl.program_id(0) < count, first_ref[0], second_ref[0])
+    x = 0.5 * jnp.dot(normed_ref[...], w, preferred_element_type=jnp.float32)
     rest[-1][...] = (x + x * jnp.tanh(x)).astype(jnp.bfloat16)
 
 
-def project(normed, blocks, place, total, into=None):
+def project(normed, first, second, place, total, into=None):
     rows, width = normed.shape
-    many, _, columns = blocks.shape
+    count, _, columns = first.shape
+    many = count + second.shape[0]
     more = into is not None
     return pl.pallas_call(
-        project_kernel,
+        functools.partial(project_kernel, count=count),
         grid_spec=pltpu.PrefetchScalarGridSpec(
             num_scalar_prefetch=1,
             grid=(many,),
             in_specs=[
                 pl.BlockSpec((rows, width), lambda j, o: (0, 0)),
-                pl.BlockSpec((1, width, columns), lambda j, o: (j, 0, 0)),
+                pl.BlockSpec((1, width, columns), lambda j, o: (jnp.minimum(j, count - 1), 0, 0)),
+                pl.BlockSpec((1, width, columns), lambda j, o: (jnp.maximum(j - count, 0), 0, 0)),
             ]
             + [pl.BlockSpec(memory_space=pl.ANY)] * more,
             out_specs=pl.BlockSpec((rows, columns), lambda j, o: (0, o[j])),
         ),
         out_shape=jax.ShapeDtypeStruct((rows, total), jnp.bfloat16),
-        input_output_aliases={3: 0} if more else {},
+        input_output_aliases={4: 0} if more else {},
         compiler_params=params(),
         cost_estimate=pl.CostEstimate(
             flops=2 * rows * width * many * columns, bytes_accessed=5 * 2**20, transcendentals=rows * many * columns
         ),
-    )(place, normed, blocks, *([into] if more else []))
+    )(place, normed, first, second, *([into] if more else []))
 
 
 def copies_kernel(*refs):
@@ -304,29 +307,31 @@
     zs = lax.all_to_all(copies(many_z, mine_b)[:, 0], "z", split_axis=0, concat_axis=0, tiled=True)
     w_near = [w_proj, shift(w_proj, "y", 1), shift(w_proj, "y", -1)]
     w_far, xs, w_near = tie((w_proj, xs, w_near))
-    w_parts = w_near + [shift(w_far, "y", 2)]
+    w_far = shift(w_far, "y", 2)
+    swap = [(0, 1), (1, 0)]
+    w_near = copies(1, *w_near)[0]
+    w_other = lax.ppermute(w_near, "core", swap)
     normed, ws = prepare(tokens, w_out, score_w[None, :])
 
     p = q = start = copies(1, *xs)[0]
     zs = copies(many_x, zs)[:, 0]
-    p, q, w_parts, normed, zs = tie((shift(p, "z", 1), shift(q, "z", -1), w_parts, normed, zs))
-    w_mine = copies(1, *w_parts)[0]
+    p, q, w_far, normed, w_other, _ = tie((shift(p, "z", 1), shift(q, "z", -1), w_far, normed, w_other, zs))
     b = lax.all_to_all(zs, "x", split_axis=0, concat_axis=0, tiled=True)
     b = b.reshape(-1, *mine_b.shape)
-    block = (lax.axis_index("y") - jnp.array([0, 1, -1, 2])) % many_y * many_core
-    proj = project(normed, w_mine, (block + core).astype(jnp.int32), 2 * width)
-    w_other = lax.ppermute(w_mine, "core", [(0, 1), (1, 0)])
+    w_far_other = lax.ppermute(w_far, "core", swap)
     near = [start, p, q]
     p, q = shift(p, "z", 1), shift(q, "z", -1)
-    proj = project(normed, w_other, (block + 1 - core).astype(jnp.int32), 2 * width, proj)
+    block = (lax.axis_index("y") - jnp.array([0, 1, -1, 2])) % many_y * many_core
+    mine, other = (block + core).astype(jnp.int32), (block + 1 - core).astype(jnp.int32)
+    proj = project(normed, w_near, w_other, jnp.concatenate([mine[:3], other[:3]]), 2 * width)
+    proj = project(normed, w_far[None], w_far_other[None], jnp.concatenate([mine[3:], other[3:]]), 2 * width, proj)
     p, q, proj = tie((p, q, proj))
-    middle = [p, q]
+    near += [p, q]
     p, q = shift(p, "z", 1), shift(q, "z", -1)
     sums = attend_part(proj, 0, near)
     p, q, sums = tie((p, q, sums))
-    half = many_x // 2
-    far = [p, q, shift(p[:half], "z", 1), shift(q[half:], "z", -1)]
-    sums = attend_part(proj, 0, middle, sums)
+    ring = [(c * many_z + i, c * many_z + (i + (1, -1)[c]) % many_z) for c in range(2) for i in range(many_z)]
+    far = [p, q, lax.ppermute(jnp.where(core == 0, p, q), ("core", "z"), ring)]
     done = attend_part(proj, HEADS_A, [b])
 
     scale = 0.5 * float(head) ** -0.5 / hist_len.astype(jnp.float32)

time: 149 us -> 132 us (0.89)
  Pallas kernels: 68.9 us -> 47.2 us
  local copies, waits for them, and re-layouts: 7.69 us -> 14.4 us
  starting transfers between devices: 43.4 us -> 41.5 us
    unnamed x28 -> x32, local copies, waits for them, and re-layouts: 3.19 us -> 12.1 us
    pallas_call x3 -> x2, Pallas kernels: 22.3 us -> 15.1 us  [attend_part(): pl.pallas_call(functools.partial(partial_kernel, count=len(arrays), facto...]
    ppermute x14 -> x12, waiting for transfers between devices: 19 us -> 14.7 us  [shift(): return lax.ppermute(block, axis, shifted(lax.axis_size(axis), step))]
    ppermute x14 -> x12, starting transfers between devices: 22.6 us -> 18.4 us  [shift(): return lax.ppermute(block, axis, shifted(lax.axis_size(axis), step))]
    pallas_call x2, Pallas kernels: 12.2 us -> 8.31 us  [project(): pl.pallas_call(functools.partial(project_kernel, count=count), grid_spec=...]
    pallas_call x1, Pallas kernels: 11.2 us -> 8.56 us  [finish(): pl.pallas_call(functools.partial(finish_kernel, count=len(arrays), factor...]
    pallas_call x1, Pallas kernels: 5.55 us -> 3.01 us  [project_out(): pl.pallas_call(out_kernel, grid=(rows // tile,), in_specs=[pl.BlockSpec((...]
    pallas_call x4, Pallas kernels: 9.24 us -> 6.89 us  [copies(): pl.pallas_call(copies_kernel, in_specs=[pl.BlockSpec(memory_space=pl.ANY)...]
  transfers between devices with their start and end apart: 18 -> 18, of which waited for: 10 -> 10; matrix products, arithmetic and copies ran while one was open for 3% -> 4% of each run, Pallas kernels for 35% -> 29%
where the time goes in v3:
time: 132 us; the launch traced here: 130 us
  Pallas kernels  47.2 us (36%)
  starting transfers between devices  41.5 us (31%)
  waiting for transfers between devices  21.4 us (16%)
  local copies, waits for them, and re-layouts  14.4 us (11%)
  other arithmetic  3.43 us (3%)
  between operations  2.28 us (2%)
    ppermute x12, starting transfers between devices, shift(): return lax.ppermute(block, axis, shifted(lax.axis_size(axis), step))  18.4 us
    pallas_call x2, Pallas kernels, attend_part(): pl.pallas_call(functools.partial(partial_kernel, count=len(arrays), facto...  15.1 us
    ppermute x12, waiting for transfers between devices, shift(): return lax.ppermute(block, axis, shifted(lax.axis_size(axis), step))  14.7 us
    unnamed x32, local copies, waits for them, and re-layouts  12.1 us
    pallas_call x1, Pallas kernels, finish(): pl.pallas_call(functools.partial(finish_kernel, count=len(arrays), factor...  8.56 us
    all_to_all x1, starting transfers between devices, on_device(): lax.all_to_all(sent, ('z', 'x'), split_axis=0, concat_axis=0, tiled=True)  8.43 us
    pallas_call x2, Pallas kernels, project(): pl.pallas_call(functools.partial(project_kernel, count=count), grid_spec=...  8.31 us
    all_to_all x1, starting transfers between devices, on_device(): lax.all_to_all(copies(many_z, mine_b)[:, 0], 'z', split_axis=0, concat_ax...  8.23 us
  transfers between devices with their start and end apart: 18, of which 10 were waited for; matrix products, arithmetic and copies ran while one was open for 4% of the time, Pallas kernels for 29%

profile of v3, /device:TPU:8, one launch (start us, length us, event | category | flops | bytes accessed | tf_op | source)
XLA Modules:
  0.0 130.2 jit_solution(9482590407622973430)
XLA Ops:
  6.6 8.2 %all-to-all-start = ((bf16[8,128,384]{2,1,0:T(8,128)(2,1)}), bf16[8,128,384]{2,1,0:T(8,128)(2,1)S(1)}, u32[]{:S(2)}, u32[]{:S(2)}) async-start(bf16[8,128,384]{2,1,0:T(8,128)(2,1)} %bitcast.7), calls=%async_computation | async-start | bytes 1572864 | tf_op jit(solution)/shard_map/all_to_all | solution.py:307
  18.2 1.8 %collective-permute-start.2 = (bf16[128,640]{1,0:T(8,128)(2,1)S(1)}, bf16[128,640]{1,0:T(8,128)(2,1)S(1)}, u32[]{:S(2)}, u32[]{:S(2)}) collective-permute-start(bf16[128,640]{1,0:T(8,128)(2,1)S(1)} %pad_maximum_fusion.refs_0_), channel_id=1, source_target_pairs={{0,2},{1,3},{2,0},{3,1},{4,6},{5,7},{6,4},{7,5},{8,10},{9,11},{10,... | collective-permute-start | bytes 491528 | tf_op jit(solution)/shard_map/ppermute | solution.py:284
  20.1 2.2 %collective-permute-done.refs_1_ = bf16[128,640]{1,0:T(8,128)(2,1)S(1)} collective-permute-done((bf16[128,640]{1,0:T(8,128)(2,1)S(1)}, bf16[128,640]{1,0:T(8,128)(2,1)S(1)}, u32[]{:S(2)}, u32[]{:S(2)}) %collective-permute-start) | collective-permute-done | bytes 163872 | tf_op jit(solution)/shard_map/ppermute | solution.py:284
  23.2 2.9 %collective-permute-done.2.refs_3_ = bf16[128,640]{1,0:T(8,128)(2,1)S(1)} collective-permute-done((bf16[128,640]{1,0:T(8,128)(2,1)S(1)}, bf16[128,640]{1,0:T(8,128)(2,1)S(1)}, u32[]{:S(2)}, u32[]{:S(2)}) %collective-permute-start.2) | collective-permute-done | bytes 163872 | tf_op jit(solution)/shard_map/ppermute | solution.py:284
  26.0 2.2 %shard_map.115 = bf16[1,3,1024,256]{3,2,1,0:T(8,128)(2,1)} custom-call(bf16[1024,256]{1,0:T(8,128)(2,1)} %refs_0_, bf16[1024,256]{1,0:T(8,128)(2,1)S(1)} %collective-permute-done.3.refs_1_, bf16[1024,256]{1,0:T(8,128)(2,1)S(1)} %collective-permute-done.4.refs_2_), custom_call_target="tpu_custom_call" | custom-call | bytes 4194304 | tf_op jit(solution)/shard_map/pallas_call | solution.py:114
  30.2 1.8 %collective-permute-start.5 = (bf16[4,128,640]{2,1,0:T(8,128)(2,1)S(1)}, bf16[4,128,640]{2,1,0:T(8,128)(2,1)}, u32[]{:S(2)}, u32[]{:S(2)}) collective-permute-start(bf16[4,128,640]{2,1,0:T(8,128)(2,1)S(1)} %bitcast.23), channel_id=1, source_target_pairs={{0,4},{4,8},{8,12},{12,16},{16,20},{20,24},{24,28},{28,0},{1,5},{5... | collective-permute-start | bytes 1966088 | tf_op jit(solution)/shard_map/ppermute | solution.py:284
  33.5 2.3 %collective-permute-start.7 = (bf16[1024,256]{1,0:T(8,128)(2,1)}, bf16[1024,256]{1,0:T(8,128)(2,1)S(1)}, u32[]{:S(2)}, u32[]{:S(2)}) collective-permute-start(bf16[1024,256]{1,0:T(8,128)(2,1)} %refs_0_), channel_id=1, source_target_pairs={{0,128},{64,192},{128,0},{192,64},{1,129},{65,193},{129,1},{193,65... | collective-permute-start | bytes 1572872 | tf_op jit(solution)/shard_map/ppermute | solution.py:284
  35.8 1.8 %all-to-all-done.refs_0_ = bf16[8,128,384]{2,1,0:T(8,128)(2,1)S(1)} async-done(((bf16[8,128,384]{2,1,0:T(8,128)(2,1)}), bf16[8,128,384]{2,1,0:T(8,128)(2,1)S(1)}, u32[]{:S(2)}, u32[]{:S(2)}) %all-to-all-start) | async-done | bytes 786464 | tf_op jit(solution)/shard_map/all_to_all | solution.py:307
  39.4 4.8 %all-to-all-start.1 = ((bf16[4,8,128,384]{3,2,1,0:T(8,128)(2,1)}), bf16[4,8,128,384]{3,2,1,0:T(8,128)(2,1)}, u32[]{:S(2)}, u32[]{:S(2)}) async-start(bf16[4,8,128,384]{3,2,1,0:T(8,128)(2,1)} %bitcast.8), calls=%async_computation.1 | async-start | bytes 6291456 | tf_op jit(solution)/shard_map/all_to_all | solution.py:319
  45.7 4.0 %shard_map.114 = (bf16[768,1024]{1,0:T(8,128)(2,1)S(1)}, f32[1,1024]{1,0:T(1,128)S(1)}) custom-call(bf16[768,1024]{1,0:T(8,128)(2,1)S(1)} %bitcast.20, bf16[1024,1024]{1,0:T(8,128)(2,1)S(1)} %copy-done, f32[1,1024]{1,0:T(1,128)S(1)} %bitcast.30), custom_call_target="tpu_custom_call" | custom-call | flops 134217728 | bytes 6291456 | tf_op jit(solution)/shard_map/pallas_call | solution.py:45
  54.9 6.5 %shard_map.118.rest_0_ = bf16[768,2048]{1,0:T(8,128)(2,1)S(1)} custom-call(s32[6]{0:T(128)S(1)} %pad_add_fusion.1.place_ref, bf16[768,1024]{1,0:T(8,128)(2,1)S(1)} %get-tuple-element.36.normed_ref, bf16[3,1024,256]{2,1,0:T(8,128)(2,1)} %bitcast.6.first_ref, bf16[3,1024,256]{2,1,0:T(8,128)(2,1)} %collective-permute-done.8.second_ref), custom_call_target="tpu_custom_call" | custom-call | flops 2415919104 | bytes 5242880 | tf_op jit(solution)/shard_map/pallas_call | solution.py:74
  61.3 1.8 %shard_map.119.refs_0_.refs_9_ = bf16[768,2048]{1,0:T(8,128)(2,1)S(1)} custom-call(s32[2]{0:T(128)S(1)} %pad_add_fusion.place_ref, bf16[768,1024]{1,0:T(8,128)(2,1)S(1)} %get-tuple-element.36.normed_ref, bf16[1,1024,256]{2,1,0:T(8,128)(2,1)S(1)} %bitcast.27, bf16[1,1024,256]{2,1,0:T(8,128)(2,1)S(1)} %bitcast.28, ...), custom_call_target="tpu_custom_call", output_to_operand_aliasing={{}: (4, {})} | custom-call | flops 805306368 | bytes 5242880 | tf_op jit(solution)/shard_map/pallas_call | solution.py:74
  64.9 2.6 %collective-permute-done.10.refs_5_.refs_10_ = bf16[4,128,640]{2,1,0:T(8,128)(2,1)} collective-permute-done((bf16[4,128,640]{2,1,0:T(8,128)(2,1)}, bf16[4,128,640]{2,1,0:T(8,128)(2,1)}, u32[]{:S(2)}, u32[]{:S(2)}) %collective-permute-start.10) | collective-permute-done | bytes 655392 | tf_op jit(solution)/shard_map/ppermute | solution.py:284
  67.5 2.6 %collective-permute-done.9.refs_4_.refs_9_ = bf16[4,128,640]{2,1,0:T(8,128)(2,1)} collective-permute-done((bf16[4,128,640]{2,1,0:T(8,128)(2,1)}, bf16[4,128,640]{2,1,0:T(8,128)(2,1)}, u32[]{:S(2)}, u32[]{:S(2)}) %collective-permute-start.9) | collective-permute-done | bytes 655392 | tf_op jit(solution)/shard_map/ppermute | solution.py:284
  70.1 3.2 %collective-permute-start.13 = (bf16[4,128,640]{2,1,0:T(8,128)(2,1)}, bf16[4,128,640]{2,1,0:T(8,128)(2,1)}, u32[]{:S(2)}, u32[]{:S(2)}) collective-permute-start(bf16[4,128,640]{2,1,0:T(8,128)(2,1)} %collective-permute-done.10.refs_5_.refs_10_), channel_id=1, source_target_pairs={{0,28},{4,0},{8,4},{12,8},{16,12},{20,16},{24,20},{28,24},{1,29},{... | collective-permute-start | bytes 1966088 | tf_op jit(solution)/shard_map/ppermute | solution.py:284
  73.3 1.9 %copy-done.5 = bf16[768,2048]{1,0:T(8,128)(2,1)S(1)} copy-done((bf16[768,2048]{1,0:T(8,128)(2,1)S(1)}, bf16[768,2048]{1,0:T(8,128)(2,1)}, u32[]{:S(2)}) %copy-start.5) | copy-done | bytes 3145752
  75.2 7.9 %shard_map.120.refs_7_ = f32[768,640]{1,0:T(8,128)S(1)} custom-call(bf16[768,2048]{1,0:T(8,128)(2,1)S(1)} %copy-done.5, bf16[4,128,640]{2,1,0:T(8,128)(2,1)S(1)} %bitcast.25, bf16[4,128,640]{2,1,0:T(8,128)(2,1)} %collective-permute-done.5.refs_2_.refs_7_, bf16[4,128,640]{2,1,0:T(8,128)(2,1)} %collective-permute-done.6.refs_3_.refs_8_, ...), custom_call_target="tpu_custom_call" | custom-call | flops 5033164800 | bytes 4194304 | tf_op jit(solution)/shard_map/pallas_call | solution.py:162
  84.4 3.2 %collective-permute-done.12.refs_1_.refs_4_ = bf16[4,128,640]{2,1,0:T(8,128)(2,1)S(1)} collective-permute-done((bf16[4,128,640]{2,1,0:T(8,128)(2,1)}, bf16[4,128,640]{2,1,0:T(8,128)(2,1)S(1)}, u32[]{:S(2)}, u32[]{:S(2)}) %collective-permute-start.12) | collective-permute-done | bytes 655392 | tf_op jit(solution)/shard_map/ppermute | solution.py:284
  90.7 1.9 %copy-done.6 = bf16[768,2048]{1,0:T(8,128)(2,1)S(1)} copy-done((bf16[768,2048]{1,0:T(8,128)(2,1)S(1)}, bf16[768,2048]{1,0:T(8,128)(2,1)}, u32[]{:S(2)}) %copy-start.6) | copy-done | bytes 3145752
  92.6 7.3 %shard_map.121.refs_8_ = f32[768,384]{1,0:T(8,128)S(1)} custom-call(bf16[768,2048]{1,0:T(8,128)(2,1)S(1)} %copy-done.6, bf16[32,128,384]{2,1,0:T(8,128)(2,1)} %bitcast.11.refs_1_.refs_2_, bf16[32,128,384]{2,1,0:T(8,128)(2,1)} %bitcast.11.refs_1_.refs_2_), custom_call_target="tpu_custom_call" | custom-call | flops 4831838208 | bytes 4194304 | tf_op jit(solution)/shard_map/pallas_call | solution.py:162
  100.5 8.6 %shard_map.122 = (bf16[768,1024]{1,0:T(8,128)(2,1)S(1)}, f32[32,1,768]{2,1,0:T(1,128)}) custom-call(bf16[768,2048]{1,0:T(8,128)(2,1)S(1)} %copy-done.7, bf16[4,128,640]{2,1,0:T(8,128)(2,1)S(1)} %collective-permute-done.12.refs_1_.refs_4_, bf16[4,128,640]{2,1,0:T(8,128)(2,1)} %collective-permute-done.13.refs_2_.refs_5_, ...), custom_call_target="tpu_custom_call" | custom-call | flops 4294967296 | bytes 12582912 | tf_op jit(solution)/shard_map/pallas_call | solution.py:207
  110.2 8.4 %all-to-all-start.2 = ((f32[32,1,768]{2,1,0:T(1,128)}), f32[32,1,768]{2,1,0:T(1,128)S(1)}, u32[]{:S(2)}, u32[]{:S(2)}) async-start(f32[32,1,768]{2,1,0:T(1,128)} %get-tuple-element.47), calls=%async_computation.2 | async-start | bytes 196608 | tf_op jit(solution)/shard_map/all_to_all | solution.py:340
  121.7 3.0 %shard_map.123 = bf16[768,1024]{1,0:T(8,128)(2,1)} custom-call(bf16[768,1024]{1,0:T(8,128)(2,1)S(1)} %copy-done.9, bf16[1024,1024]{1,0:T(8,128)(2,1)S(1)} %copy-done, bf16[768,1024]{1,0:T(8,128)(2,1)S(1)} %bitcast.22), custom_call_target="tpu_custom_call" | custom-call | flops 1610612736 | bytes 7340032 | tf_op jit(solution)/shard_map/pallas_call | solution.py:240
  124.7 4.2 %all-to-all-done.2 = f32[32,1,768]{2,1,0:T(1,128)S(1)} async-done(((f32[32,1,768]{2,1,0:T(1,128)}), f32[32,1,768]{2,1,0:T(1,128)S(1)}, u32[]{:S(2)}, u32[]{:S(2)}) %all-to-all-start.2) | async-done | bytes 98336 | tf_op jit(solution)/shard_map/all_to_all | solution.py:340
  (72 shorter events, 32.8 us)
Async XLA Ops:
  0.6 25.4 %collective-permute-start.3 = (bf16[1024,256]{1,0:T(8,128)(2,1)}, bf16[1024,256]{1,0:T(8,128)(2,1)S(1)}, u32[]{:S(2)}, u32[]{:S(2)}) collective-permute-start(bf16[1024,256]{1,0:T(8,128)(2,1)} %refs_0_), channel_id=1, source_target_pairs={{0,64},{64,128},{128,192},{192,0},{1,65},{65,129},{129,193},{193,1... | collective-permute-start | bytes 1572872 | tf_op jit(solution)/shard_map/ppermute | solution.py:284
  2.3 23.8 %collective-permute-start.4 = (bf16[1024,256]{1,0:T(8,128)(2,1)}, bf16[1024,256]{1,0:T(8,128)(2,1)S(1)}, u32[]{:S(2)}, u32[]{:S(2)}) collective-permute-start(bf16[1024,256]{1,0:T(8,128)(2,1)} %refs_0_), channel_id=1, source_target_pairs={{0,192},{64,0},{128,64},{192,128},{1,193},{65,1},{129,65},{193,129... | collective-permute-start | bytes 1572872 | tf_op jit(solution)/shard_map/ppermute | solution.py:284
  4.6 10.2 %copy-start.13 = (bf16[1,64,1024]{2,1,0:T(8,128)(2,1)S(1)}, bf16[1,64,1024]{2,1,0:T(8,128)(2,1)}, u32[]{:S(2)}) copy-start(bf16[1,64,1024]{2,1,0:T(8,128)(2,1)} %param.12) | copy-start | bytes 393220
  6.6 31.0 %all-to-all-start = ((bf16[8,128,384]{2,1,0:T(8,128)(2,1)}), bf16[8,128,384]{2,1,0:T(8,128)(2,1)S(1)}, u32[]{:S(2)}, u32[]{:S(2)}) async-start(bf16[8,128,384]{2,1,0:T(8,128)(2,1)} %bitcast.7), calls=%async_computation | async-start | bytes 1572864 | tf_op jit(solution)/shard_map/all_to_all | solution.py:307
  14.9 7.4 %collective-permute-start = (bf16[128,640]{1,0:T(8,128)(2,1)S(1)}, bf16[128,640]{1,0:T(8,128)(2,1)S(1)}, u32[]{:S(2)}, u32[]{:S(2)}) collective-permute-start(bf16[128,640]{1,0:T(8,128)(2,1)S(1)} %pad_maximum_fusion.refs_0_), channel_id=1, source_target_pairs={{0,1},{1,2},{2,3},{3,0},{4,5},{5,6},{6,7},{7,4},{8,9},{9,10},{10,1... | collective-permute-start | bytes 491528 | tf_op jit(solution)/shard_map/ppermute | solution.py:284
  16.5 6.7 %collective-permute-start.1 = (bf16[128,640]{1,0:T(8,128)(2,1)S(1)}, bf16[128,640]{1,0:T(8,128)(2,1)S(1)}, u32[]{:S(2)}, u32[]{:S(2)}) collective-permute-start(bf16[128,640]{1,0:T(8,128)(2,1)S(1)} %pad_maximum_fusion.refs_0_), channel_id=1, source_target_pairs={{0,3},{1,0},{2,1},{3,2},{4,7},{5,4},{6,5},{7,6},{8,11},{9,8},{10,9... | collective-permute-start | bytes 491528 | tf_op jit(solution)/shard_map/ppermute | solution.py:284
  18.2 7.8 %collective-permute-start.2 = (bf16[128,640]{1,0:T(8,128)(2,1)S(1)}, bf16[128,640]{1,0:T(8,128)(2,1)S(1)}, u32[]{:S(2)}, u32[]{:S(2)}) collective-permute-start(bf16[128,640]{1,0:T(8,128)(2,1)S(1)} %pad_maximum_fusion.refs_0_), channel_id=1, source_target_pairs={{0,2},{1,3},{2,0},{3,1},{4,6},{5,7},{6,4},{7,5},{8,10},{9,11},{10,... | collective-permute-start | bytes 491528 | tf_op jit(solution)/shard_map/ppermute | solution.py:284
  28.3 21.7 %collective-permute-start.8 = (bf16[3,1024,256]{2,1,0:T(8,128)(2,1)}, bf16[3,1024,256]{2,1,0:T(8,128)(2,1)}, u32[]{:S(2)}, u32[]{:S(2)}) collective-permute-start(bf16[3,1024,256]{2,1,0:T(8,128)(2,1)} %bitcast.6.first_ref), channel_id=1, source_target_pairs={{0,32},{32,0},{1,33},{33,1},{2,34},{34,2},{3,35},{35,3},{4,36},{36... | collective-permute-start | bytes 4718600 | tf_op jit(solution)/shard_map/ppermute | solution.py:313
  30.2 19.9 %collective-permute-start.5 = (bf16[4,128,640]{2,1,0:T(8,128)(2,1)S(1)}, bf16[4,128,640]{2,1,0:T(8,128)(2,1)}, u32[]{:S(2)}, u32[]{:S(2)}) collective-permute-start(bf16[4,128,640]{2,1,0:T(8,128)(2,1)S(1)} %bitcast.23), channel_id=1, source_target_pairs={{0,4},{4,8},{8,12},{12,16},{16,20},{20,24},{24,28},{28,0},{1,5},{5... | collective-permute-start | bytes 1966088 | tf_op jit(solution)/shard_map/ppermute | solution.py:284
  32.0 18.0 %collective-permute-start.6 = (bf16[4,128,640]{2,1,0:T(8,128)(2,1)S(1)}, bf16[4,128,640]{2,1,0:T(8,128)(2,1)}, u32[]{:S(2)}, u32[]{:S(2)}) collective-permute-start(bf16[4,128,640]{2,1,0:T(8,128)(2,1)S(1)} %bitcast.24), channel_id=1, source_target_pairs={{0,28},{4,0},{8,4},{12,8},{16,12},{20,16},{24,20},{28,24},{1,29},{... | collective-permute-start | bytes 1966088 | tf_op jit(solution)/shard_map/ppermute | solution.py:284
  33.5 16.2 %collective-permute-start.7 = (bf16[1024,256]{1,0:T(8,128)(2,1)}, bf16[1024,256]{1,0:T(8,128)(2,1)S(1)}, u32[]{:S(2)}, u32[]{:S(2)}) collective-permute-start(bf16[1024,256]{1,0:T(8,128)(2,1)} %refs_0_), channel_id=1, source_target_pairs={{0,128},{64,192},{128,0},{192,64},{1,129},{65,193},{129,1},{193,65... | collective-permute-start | bytes 1572872 | tf_op jit(solution)/shard_map/ppermute | solution.py:284
  39.4 4.8 %copy-start = (bf16[1024,1024]{1,0:T(8,128)(2,1)S(1)}, bf16[1024,1024]{1,0:T(8,128)(2,1)}, u32[]{:S(2)}) copy-start(bf16[1024,1024]{1,0:T(8,128)(2,1)} %w_ref.3) | copy-start | bytes 6291460
  39.4 51.2 %all-to-all-start.1 = ((bf16[4,8,128,384]{3,2,1,0:T(8,128)(2,1)}), bf16[4,8,128,384]{3,2,1,0:T(8,128)(2,1)}, u32[]{:S(2)}, u32[]{:S(2)}) async-start(bf16[4,8,128,384]{3,2,1,0:T(8,128)(2,1)} %bitcast.8), calls=%async_computation.1 | async-start | bytes 6291456 | tf_op jit(solution)/shard_map/all_to_all | solution.py:319
  50.0 11.3 %collective-permute-start.11 = (bf16[1024,256]{1,0:T(8,128)(2,1)S(1)}, bf16[1024,256]{1,0:T(8,128)(2,1)S(1)}, u32[]{:S(2)}, u32[]{:S(2)}) collective-permute-start(bf16[1024,256]{1,0:T(8,128)(2,1)S(1)} %collective-permute-done.7), channel_id=1, source_target_pairs={{0,32},{32,0},{1,33},{33,1},{2,34},{34,2},{3,35},{35,3},{4,36},{36... | collective-permute-start | bytes 1572872 | tf_op jit(solution)/shard_map/ppermute | solution.py:321
  50.1 17.4 %collective-permute-start.10 = (bf16[4,128,640]{2,1,0:T(8,128)(2,1)}, bf16[4,128,640]{2,1,0:T(8,128)(2,1)}, u32[]{:S(2)}, u32[]{:S(2)}) collective-permute-start(bf16[4,128,640]{2,1,0:T(8,128)(2,1)} %collective-permute-done.6.refs_3_.refs_8_), channel_id=1, source_target_pairs={{0,28},{4,0},{8,4},{12,8},{16,12},{20,16},{24,20},{28,24},{1,29},{... | collective-permute-start | bytes 1966088 | tf_op jit(solution)/shard_map/ppermute | solution.py:284
  51.7 18.4 %collective-permute-start.9 = (bf16[4,128,640]{2,1,0:T(8,128)(2,1)}, bf16[4,128,640]{2,1,0:T(8,128)(2,1)}, u32[]{:S(2)}, u32[]{:S(2)}) collective-permute-start(bf16[4,128,640]{2,1,0:T(8,128)(2,1)} %collective-permute-done.5.refs_2_.refs_7_), channel_id=1, source_target_pairs={{0,4},{4,8},{8,12},{12,16},{16,20},{20,24},{24,28},{28,0},{1,5},{5... | collective-permute-start | bytes 1966088 | tf_op jit(solution)/shard_map/ppermute | solution.py:284
  70.1 17.5 %collective-permute-start.12 = (bf16[4,128,640]{2,1,0:T(8,128)(2,1)}, bf16[4,128,640]{2,1,0:T(8,128)(2,1)S(1)}, u32[]{:S(2)}, u32[]{:S(2)}) collective-permute-start(bf16[4,128,640]{2,1,0:T(8,128)(2,1)} %collective-permute-done.9.refs_4_.refs_9_), channel_id=1, source_target_pairs={{0,4},{4,8},{8,12},{12,16},{16,20},{20,24},{24,28},{28,0},{1,5},{5... | collective-permute-start | bytes 1966088 | tf_op jit(solution)/shard_map/ppermute | solution.py:284
  70.1 17.5 %collective-permute-start.13 = (bf16[4,128,640]{2,1,0:T(8,128)(2,1)}, bf16[4,128,640]{2,1,0:T(8,128)(2,1)}, u32[]{:S(2)}, u32[]{:S(2)}) collective-permute-start(bf16[4,128,640]{2,1,0:T(8,128)(2,1)} %collective-permute-done.10.refs_5_.refs_10_), channel_id=1, source_target_pairs={{0,28},{4,0},{8,4},{12,8},{16,12},{20,16},{24,20},{28,24},{1,29},{... | collective-permute-start | bytes 1966088 | tf_op jit(solution)/shard_map/ppermute | solution.py:284
  88.5 12.0 %collective-permute-start.14 = (bf16[4,128,640]{2,1,0:T(8,128)(2,1)}, bf16[4,128,640]{2,1,0:T(8,128)(2,1)S(1)}, u32[]{:S(2)}, u32[]{:S(2)}) collective-permute-start(bf16[4,128,640]{2,1,0:T(8,128)(2,1)} %broadcast_select_fusion), channel_id=1, source_target_pairs={{0,4},{4,8},{8,12},{12,16},{16,20},{20,24},{24,28},{28,0},{32,60},... | collective-permute-start | bytes 1966088 | tf_op jit(solution)/shard_map/ppermute | solution.py:334
  92.6 7.9 %copy-start.2 = (bf16[1,768,1024]{2,1,0:T(8,128)(2,1)S(1)}, bf16[1,768,1024]{2,1,0:T(8,128)(2,1)}, u32[]{:S(2)}) copy-start(bf16[1,768,1024]{2,1,0:T(8,128)(2,1)} %param.10) | copy-start | bytes 4718596
  92.6 7.9 %copy-start.7 = (bf16[768,2048]{1,0:T(8,128)(2,1)S(1)}, bf16[768,2048]{1,0:T(8,128)(2,1)}, u32[]{:S(2)}) copy-start(bf16[768,2048]{1,0:T(8,128)(2,1)} %copy-done.4) | copy-start | bytes 9437188
  92.6 7.9 %copy-start.12 = (f32[768,640]{1,0:T(8,128)S(1)}, f32[768,640]{1,0:T(8,128)}, u32[]{:S(2)}) copy-start(f32[768,640]{1,0:T(8,128)} %copy-done.11) | copy-start | bytes 5898244
  100.5 18.1 %copy-start.14 = (s32[1,768]{1,0:T(1,128)S(1)}, s32[1,768]{1,0:T(1,128)}, u32[]{:S(2)}) copy-start(s32[1,768]{1,0:T(1,128)} %param.15) | copy-start | bytes 9220
  110.2 18.7 %all-to-all-start.2 = ((f32[32,1,768]{2,1,0:T(1,128)}), f32[32,1,768]{2,1,0:T(1,128)S(1)}, u32[]{:S(2)}, u32[]{:S(2)}) async-start(f32[32,1,768]{2,1,0:T(1,128)} %get-tuple-element.47), calls=%async_computation.2 | async-start | bytes 196608 | tf_op jit(solution)/shard_map/all_to_all | solution.py:340
  (10 other events, 20.9 us)

commit v4 on v3

--- a/solution.py
+++ b/solution.py
@@ -11,10 +11,11 @@
 HEADS = 8
 eps = 1e-05
 VMEM_LIMIT = 24 * 2**20
-
-
-def params():
-    return pltpu.CompilerParams(vmem_limit_bytes=VMEM_LIMIT)
+VMEM_MOST = 58 * 2**20
+
+
+def params(limit=VMEM_LIMIT):
+    return pltpu.CompilerParams(vmem_limit_bytes=limit)
 
 
 def layer_norm(values):
@@ -28,32 +29,42 @@
     return [(i, (i + step) % size) for i in range(size)]
 
 
-def prepare_kernel(tokens_ref, w_ref, sw_ref, normed_ref, ws_ref):
-    normed_ref[...] = layer_norm(tokens_ref[...].astype(jnp.float32)).astype(jnp.bfloat16)
-    ws_ref[...] = lax.dot_general(
-        sw_ref[...],
-        w_ref[...].astype(jnp.float32),
-        (((1,), (1,)), ((), ())),
-        precision=lax.Precision.HIGHEST,
-        preferred_element_type=jnp.float32,
-    )
-
-
-def prepare(tokens, w_out, score_w, steps=4):
+def prepare_kernel(tokens_ref, w_ref, sw_ref, normed_ref, ws_ref, base_ref):
+    tokens = tokens_ref[...].astype(jnp.float32)
+    normed_ref[...] = layer_norm(tokens).astype(jnp.bfloat16)
+    base_ref[...] = jnp.sum(tokens * sw_ref[...], axis=-1).reshape(1, 1, -1)
+
+    @pl.when(pl.program_id(0) == 0)
+    def _():
+        ws_ref[...] = lax.dot_general(
+            sw_ref[...],
+            w_ref[...].astype(jnp.float32),
+            (((1,), (1,)), ((), ())),
+            precision=lax.Precision.HIGHEST,
+            preferred_element_type=jnp.float32,
+        )
+
+
+def prepare(tokens, w_out, score_w, steps=3):
     rows, width = tokens.shape
-    tile, part = rows // steps, width // steps
+    tile, part = rows // steps, width
     return pl.pallas_call(
         prepare_kernel,
         grid=(steps,),
         in_specs=[
             pl.BlockSpec((tile, width), lambda i: (i, 0)),
-            pl.BlockSpec((part, width), lambda i: (i, 0)),
+            pl.BlockSpec((part, width), lambda i: (0, 0)),
             pl.BlockSpec((1, width), lambda i: (0, 0)),
         ],
-        out_specs=[pl.BlockSpec((tile, width), lambda i: (i, 0)), pl.BlockSpec((1, part), lambda i: (0, i))],
+        out_specs=[
+            pl.BlockSpec((tile, width), lambda i: (i, 0)),
+            pl.BlockSpec((1, part), lambda i: (0, 0)),
+            pl.BlockSpec((1, 1, tile), lambda i: (i, 0, 0)),
+        ],
         out_shape=[
             jax.ShapeDtypeStruct((rows, width), jnp.bfloat16),
             jax.ShapeDtypeStruct((1, width), jnp.float32),
+            jax.ShapeDtypeStruct((steps, 1, tile), jnp.float32),
         ],
         compiler_params=params(),
         cost_estimate=pl.CostEstimate(flops=2**27, bytes_accessed=6 * 2**20, transcendentals=rows),
@@ -126,6 +137,33 @@
     )(*blocks)
 
 
+def stage_kernel(live_ref, keys_ref, values_ref, a_ref, b_ref, *, cut):
+    own = keys_ref.shape[0]
+    valid = lax.broadcasted_iota(jnp.int32, keys_ref.shape, 0) < live_ref[0]
+    keys = jnp.where(valid, keys_ref[...], jnp.zeros((), keys_ref.dtype))
+    values = values_ref[...]
+    a_ref[:own], a_ref[own:] = keys[:, :cut], values[:, :cut]
+    for i in range(b_ref.shape[0]):
+        b_ref[i, :own], b_ref[i, own:] = keys[:, cut:], values[:, cut:]
+
+
+def stage(live, keys, values, cut, times):
+    own, width = keys.shape
+    return pl.pallas_call(
+        functools.partial(stage_kernel, cut=cut),
+        in_specs=[
+            pl.BlockSpec(memory_space=pltpu.SMEM),
+            pl.BlockSpec(memory_space=pltpu.VMEM),
+            pl.BlockSpec(memory_space=pltpu.VMEM),
+        ],
+        out_shape=[
+            jax.ShapeDtypeStruct((2 * own, cut), keys.dtype),
+            jax.ShapeDtypeStruct((times, 2 * own, width - cut), keys.dtype),
+        ],
+        compiler_params=params(VMEM_MOST),
+    )(live, keys, values)
+
+
 def side_by_side(refs):
     blocks = [ref[...].reshape(-1, ref.shape[-1]) for ref in refs]
     return jnp.concatenate(blocks, axis=0) if len(blocks) > 1 else blocks[0]
@@ -176,58 +214,81 @@
 
 def finish_kernel(*refs, count, factor, tile):
     q_ref, ks, vs = refs[0], refs[1 : 1 + count], refs[1 + count : 1 + 2 * count]
-    sums_ref, done_ref, gate_ref, tokens_ref, ws_ref, sw_ref, scale_ref, live_ref, gated_ref, score_ref, attn = refs[1 + 2 * count :]
+    sums_ref, done_ref, proj_ref, base_ref, ws_ref, scale_ref, live_ref = refs[1 + 2 * count : 8 + 2 * count]
+    gated_ref, score_ref, attn, done, gate, gated, into, back = refs[8 + 2 * count :]
     h = pl.program_id(0)
-    rows = q_ref.shape[0]
+    rows, width = gated.shape
+    reads = [
+        pltpu.make_async_copy(done_ref, done, into.at[0]),
+        pltpu.make_async_copy(proj_ref.at[:, pl.ds(0, width)], gate, into.at[1]),
+    ]
+
+    @pl.when(h == 0)
+    def _():
+        for read in reads:
+            read.start()
+
     k, v = side_by_side(ks), side_by_side(vs)
     for r in range(0, rows, tile):
         attn[h, r : r + tile, :] = weigh(q_ref[r : r + tile, :], k, v, factor) + sums_ref[r : r + tile, :]
 
     @pl.when(h == pl.num_programs(0) - 1)
     def _():
-        for r in range(0, rows, tile):
-            heads = [attn[i, r : r + tile, :] for i in range(attn.shape[0])] + [done_ref[r : r + tile, :]]
+        for read in reads:
+            read.wait()
+        writes = []
+        for i, r in enumerate(range(0, rows, tile)):
+            heads = [attn[j, r : r + tile, :] for j in range(attn.shape[0])] + [done[r : r + tile, :]]
             whole = jnp.concatenate(heads, axis=1) * scale_ref[0]
-            gated = (layer_norm(whole) * gate_ref[r : r + tile, :].astype(jnp.float32)).astype(jnp.bfloat16)
-            gated_ref[r : r + tile, :] = gated
-            total = gated.astype(jnp.float32) * ws_ref[...]
-            total += tokens_ref[r : r + tile, :].astype(jnp.float32) * sw_ref[...]
+            part = (layer_norm(whole) * gate[r : r + tile, :].astype(jnp.float32)).astype(jnp.bfloat16)
+            gated[r : r + tile, :] = part
+            write = pltpu.make_async_copy(gated.at[pl.ds(r, tile)], gated_ref.at[pl.ds(r, tile)], back.at[i])
+            write.start()
+            writes.append(write)
+            score = jnp.sum(part.astype(jnp.float32) * ws_ref[...], axis=-1).reshape(1, -1) + base_ref[i]
             slots = r + lax.broadcasted_iota(jnp.int32, (1, tile), 1)
-            score = jnp.sum(total, axis=-1).reshape(1, -1)
             score = jnp.where(slots < live_ref[0], score, 0.0)
             score_ref[:, :, r : r + tile] = jnp.broadcast_to(score[None], (score_ref.shape[0], 1, tile))
-
-
-def finish(proj, arrays, sums, done, tokens, ws, score_w, scale, live, parts):
-    rows, width = tokens.shape
+        for write in writes:
+            write.wait()
+
+
+def finish(proj, arrays, sums, done, base, ws, scale, live, parts):
+    rows, width = proj.shape[0], proj.shape[1] // 2
     head = width // HEADS
     left = arrays[0].shape[2] // head
-    whole = pl.BlockSpec((rows, width), lambda h: (0, 0))
-    line = pl.BlockSpec((1, width), lambda h: (0, 0))
-    return pl.pallas_call(
-        functools.partial(finish_kernel, count=len(arrays), factor=float(head) ** -0.5, tile=256),
+    tile = base.shape[2]
+    smem = pl.BlockSpec(memory_space=pltpu.SMEM)
+    return pl.pallas_call(
+        functools.partial(finish_kernel, count=len(arrays), factor=float(head) ** -0.5, tile=tile),
         grid=(left,),
         in_specs=[pl.BlockSpec((rows, head), lambda h: (0, HEADS + h))]
         + key_specs(arrays, head, lambda h: h)
         + [
             pl.BlockSpec((rows, head), lambda h: (0, h)),
-            pl.BlockSpec(done.shape, lambda h: (0, 0)),
-            whole,
-            whole,
-            line,
-            line,
-            pl.BlockSpec(memory_space=pltpu.SMEM),
-            pl.BlockSpec(memory_space=pltpu.SMEM),
-        ],
-        out_specs=[whole, pl.BlockSpec((parts, 1, rows), lambda h: (0, 0, 0))],
+            pl.BlockSpec(memory_space=pl.ANY),
+            pl.BlockSpec(memory_space=pl.ANY),
+            pl.BlockSpec(base.shape, lambda h: (0, 0, 0)),
+            pl.BlockSpec((1, width), lambda h: (0, 0)),
+            smem,
+            smem,
+        ],
+        out_specs=[pl.BlockSpec(memory_space=pltpu.HBM), pl.BlockSpec((parts, 1, rows), lambda h: (0, 0, 0))],
         out_shape=[
             jax.ShapeDtypeStruct((rows, width), jnp.bfloat16),
             jax.ShapeDtypeStruct((parts, 1, rows), jnp.float32),
         ],
-        scratch_shapes=[pltpu.VMEM((left, rows, head), jnp.float32)],
-        compiler_params=params(),
+        scratch_shapes=[
+            pltpu.VMEM((left, rows, head), jnp.float32),
+            pltpu.VMEM(done.shape, jnp.float32),
+            pltpu.VMEM((rows, width), jnp.bfloat16),
+            pltpu.VMEM((rows, width), jnp.bfloat16),
+            pltpu.SemaphoreType.DMA((2,)),
+            pltpu.SemaphoreType.DMA((rows // tile,)),
+        ],
+        compiler_params=params(VMEM_MOST),
         cost_estimate=pl.CostEstimate(flops=2**32, bytes_accessed=12 * 2**20, transcendentals=2**22),
-    )(proj, *arrays, *arrays, sums, done, proj, tokens, ws, score_w, scale, live)
+    )(proj, *arrays, *arrays, sums, done, proj, base, ws, scale, live)
 
 
 def out_kernel(gated_ref, w_ref, tokens_ref, out_ref):
@@ -247,7 +308,7 @@
         ],
         out_specs=pl.BlockSpec((tile, width), lambda i: (i, 0)),
         out_shape=jax.ShapeDtypeStruct((rows, width), jnp.bfloat16),
-        compiler_params=params(),
+        compiler_params=params(VMEM_MOST),
         cost_estimate=pl.CostEstimate(flops=2 * rows * width * width, bytes_accessed=7 * 2**20, transcendentals=0),
     )(gated, w_out, tokens)
 
@@ -296,28 +357,23 @@
     many_y, many_core = lax.axis_size("y"), lax.axis_size("core")
     parts, many_z, many_x = lax.axis_size(("z", "x")), lax.axis_size("z"), lax.axis_size("x")
 
-    position = cand * own + jnp.arange(own, dtype=jnp.int32)
-    keys = jnp.where((position < hist_len[0])[:, None], hist_keys[0], jnp.zeros((), jnp.bfloat16))
-    values = hist_values[0]
-    cut = HEADS_A * head
-    mine_a = jnp.concatenate([keys[:, :cut], values[:, :cut]], axis=0)
-    mine_b = jnp.concatenate([keys[:, cut:], values[:, cut:]], axis=0)
+    mine_a, mine_b = stage(hist_len - cand * own, hist_keys[0], hist_values[0], HEADS_A * head, many_z)
 
     xs = [mine_a, shift(mine_a, "x", 1), shift(mine_a, "x", -1), shift(mine_a, "x", 2)]
-    zs = lax.all_to_all(copies(many_z, mine_b)[:, 0], "z", split_axis=0, concat_axis=0, tiled=True)
+    zs = lax.all_to_all(mine_b, "z", split_axis=0, concat_axis=0, tiled=True)
     w_near = [w_proj, shift(w_proj, "y", 1), shift(w_proj, "y", -1)]
     w_far, xs, w_near = tie((w_proj, xs, w_near))
     w_far = shift(w_far, "y", 2)
     swap = [(0, 1), (1, 0)]
     w_near = copies(1, *w_near)[0]
     w_other = lax.ppermute(w_near, "core", swap)
-    normed, ws = prepare(tokens, w_out, score_w[None, :])
+    normed, ws, base = prepare(tokens, w_out, score_w[None, :])
 
     p = q = start = copies(1, *xs)[0]
     zs = copies(many_x, zs)[:, 0]
     p, q, w_far, normed, w_other, _ = tie((shift(p, "z", 1), shift(q, "z", -1), w_far, normed, w_other, zs))
     b = lax.all_to_all(zs, "x", split_axis=0, concat_axis=0, tiled=True)
-    b = b.reshape(-1, *mine_b.shape)
+    b = b.reshape(-1, *mine_b.shape[1:])
     w_far_other = lax.ppermute(w_far, "core", swap)
     near = [start, p, q]
     p, q = shift(p, "z", 1), shift(q, "z", -1)
@@ -336,7 +392,7 @@
 
     scale = 0.5 * float(head) ** -0.5 / hist_len.astype(jnp.float32)
     live = cand_count - cand * rows
-    gated, sent = finish(proj, far, sums, done, tokens, ws, score_w[None, :], scale, live, parts)
+    gated, sent = finish(proj, far, sums, done, base, ws, scale, live, parts)
     every = lax.all_to_all(sent, ("z", "x"), split_axis=0, concat_axis=0, tiled=True)
     layer_out = project_out(gated, w_out, tokens)
     ranked = pick(impressions[0], every)

time: 132 us -> 131 us (level)
  local copies, waits for them, and re-layouts: 14.4 us -> 6.25 us
  Pallas kernels: 47.2 us -> 52.7 us
  waiting for transfers between devices: 21.4 us -> 24.2 us
    unnamed x32 -> x28, local copies, waits for them, and re-layouts: 12.1 us -> 4.81 us
    pallas_call x1, Pallas kernels: 3.01 us -> 5.57 us  [project_out(): pl.pallas_call(out_kernel, grid=(rows // tile,), in_specs=[pl.BlockSpec((...]
    pallas_call x4 -> x3, Pallas kernels: 6.89 us -> 4.85 us  [copies(): pl.pallas_call(copies_kernel, in_specs=[pl.BlockSpec(memory_space=pl.ANY)...]
    pallas_call x0 -> x1, Pallas kernels: none -> 2.01 us  [stage(): pl.pallas_call(functools.partial(stage_kernel, cut=cut), in_specs=[pl.Blo...]
    pallas_call x1, Pallas kernels: 8.56 us -> 10.2 us  [finish(): pl.pallas_call(functools.partial(finish_kernel, count=len(arrays), factor...]
    ppermute x1, waiting for transfers between devices: 0.63 us -> 2.04 us  [on_device(): far = [p, q, lax.ppermute(jnp.where(core == 0, p, q), ('core', 'z'), ring)]]
  transfers between devices with their start and end apart: 18 -> 18, of which waited for: 10 -> 9; matrix products, arithmetic and copies ran while one was open for 4% -> 4% of each run, Pallas kernels for 29% -> 32%
where the time goes in v4:
time: 131 us; the launch traced here: 130 us
  Pallas kernels  52.7 us (40%)
  starting transfers between devices  41.4 us (32%)
  waiting for transfers between devices  24.2 us (18%)
  local copies, waits for them, and re-layouts  6.25 us (5%)
  other arithmetic  3.4 us (3%)
  between operations  2.32 us (2%)
    ppermute x12, starting transfers between devices, shift(): return lax.ppermute(block, axis, shifted(lax.axis_size(axis), step))  18.4 us
    pallas_call x2, Pallas kernels, attend_part(): pl.pallas_call(functools.partial(partial_kernel, count=len(arrays), facto...  15 us
    ppermute x12, waiting for transfers between devices, shift(): return lax.ppermute(block, axis, shifted(lax.axis_size(axis), step))  14.9 us
    pallas_call x1, Pallas kernels, finish(): pl.pallas_call(functools.partial(finish_kernel, count=len(arrays), factor...  10.2 us
    pallas_call x2, Pallas kernels, project(): pl.pallas_call(functools.partial(project_kernel, count=count), grid_spec=...  9.33 us
    all_to_all x1, starting transfers between devices, on_device(): lax.all_to_all(sent, ('z', 'x'), split_axis=0, concat_axis=0, tiled=True)  8.43 us
    all_to_all x1, starting transfers between devices, on_device(): zs = lax.all_to_all(mine_b, 'z', split_axis=0, concat_axis=0, tiled=True)  8.35 us
    pallas_call x1, Pallas kernels, project_out(): pl.pallas_call(out_kernel, grid=(rows // tile,), in_specs=[pl.BlockSpec((...  5.57 us
  transfers between devices with their start and end apart: 18, of which 9 were waited for; matrix products, arithmetic and copies ran while one was open for 4% of the time, Pallas kernels for 32%

profile of v4, /device:TPU:8, one launch (start us, length us, event | category | flops | bytes accessed | tf_op | source)
XLA Modules:
  0.0 130.3 jit_solution(17705768913160025905)
XLA Ops:
  3.7 2.0 %shard_map.113 = (bf16[128,640]{1,0:T(8,128)(2,1)}, bf16[8,128,384]{2,1,0:T(8,128)(2,1)}) custom-call(s32[1]{0:T(128)S(6)} %sub.23.live_ref, bf16[64,1024]{1,0:T(8,128)(2,1)} %bitcast.27, bf16[64,1024]{1,0:T(8,128)(2,1)} %bitcast.28), custom_call_target="tpu_custom_call" | custom-call | tf_op jit(solution)/shard_map/pallas_call | solution.py:152
  5.7 8.3 %all-to-all-start = ((bf16[8,128,384]{2,1,0:T(8,128)(2,1)}), bf16[8,128,384]{2,1,0:T(8,128)(2,1)S(1)}, u32[]{:S(2)}, u32[]{:S(2)}) async-start(bf16[8,128,384]{2,1,0:T(8,128)(2,1)} %get-tuple-element.38), calls=%async_computation | async-start | bytes 1572864 | tf_op jit(solution)/shard_map/all_to_all | solution.py:363
  17.3 1.8 %collective-permute-start.2 = (bf16[128,640]{1,0:T(8,128)(2,1)S(1)}, bf16[128,640]{1,0:T(8,128)(2,1)S(1)}, u32[]{:S(2)}, u32[]{:S(2)}) collective-permute-start(bf16[128,640]{1,0:T(8,128)(2,1)S(1)} %copy-done.6), channel_id=1, source_target_pairs={{0,2},{1,3},{2,0},{3,1},{4,6},{5,7},{6,4},{7,5},{8,10},{9,11},{10,... | collective-permute-start | bytes 491528 | tf_op jit(solution)/shard_map/ppermute | solution.py:345
  19.1 2.2 %collective-permute-done.refs_1_ = bf16[128,640]{1,0:T(8,128)(2,1)S(1)} collective-permute-done((bf16[128,640]{1,0:T(8,128)(2,1)S(1)}, bf16[128,640]{1,0:T(8,128)(2,1)S(1)}, u32[]{:S(2)}, u32[]{:S(2)}) %collective-permute-start) | collective-permute-done | bytes 163872 | tf_op jit(solution)/shard_map/ppermute | solution.py:345
  22.2 2.9 %collective-permute-done.2.refs_3_ = bf16[128,640]{1,0:T(8,128)(2,1)S(1)} collective-permute-done((bf16[128,640]{1,0:T(8,128)(2,1)S(1)}, bf16[128,640]{1,0:T(8,128)(2,1)S(1)}, u32[]{:S(2)}, u32[]{:S(2)}) %collective-permute-start.2) | collective-permute-done | bytes 163872 | tf_op jit(solution)/shard_map/ppermute | solution.py:345
  26.5 1.8 %shard_map.114 = bf16[1,4,128,640]{3,2,1,0:T(8,128)(2,1)S(1)} custom-call(bf16[128,640]{1,0:T(8,128)(2,1)S(1)} %copy-done.6, bf16[128,640]{1,0:T(8,128)(2,1)S(1)} %collective-permute-done.refs_1_, bf16[128,640]{1,0:T(8,128)(2,1)S(1)} %collective-permute-done.1.refs_2_, bf16[128,640]{1,0:T(8,128)(2,1)S(1)} %collective-permute-done.2.refs_3_), custom_call_target="tpu_custom_call" | custom-call | bytes 4194304 | tf_op jit(solution)/shard_map/pallas_call | solution.py:125
  31.6 2.3 %collective-permute-start.7 = (bf16[1024,256]{1,0:T(8,128)(2,1)S(1)}, bf16[1024,256]{1,0:T(8,128)(2,1)}, u32[]{:S(2)}, u32[]{:S(2)}) collective-permute-start(bf16[1024,256]{1,0:T(8,128)(2,1)S(1)} %copy-done.5), channel_id=1, source_target_pairs={{0,128},{64,192},{128,0},{192,64},{1,129},{65,193},{129,1},{193,65... | collective-permute-start | bytes 1572872 | tf_op jit(solution)/shard_map/ppermute | solution.py:345
  33.9 2.8 %all-to-all-done.refs_0_ = bf16[8,128,384]{2,1,0:T(8,128)(2,1)S(1)} async-done(((bf16[8,128,384]{2,1,0:T(8,128)(2,1)}), bf16[8,128,384]{2,1,0:T(8,128)(2,1)S(1)}, u32[]{:S(2)}, u32[]{:S(2)}) %all-to-all-start) | async-done | bytes 786464 | tf_op jit(solution)/shard_map/all_to_all | solution.py:363
  36.8 1.8 %shard_map.117 = bf16[4,1,8,128,384]{4,3,2,1,0:T(8,128)(2,1)} custom-call(bf16[8,128,384]{2,1,0:T(8,128)(2,1)S(1)} %all-to-all-done.refs_0_), custom_call_target="tpu_custom_call" | custom-call | bytes 4194304 | tf_op jit(solution)/shard_map/pallas_call | solution.py:125
  38.6 4.8 %all-to-all-start.1 = ((bf16[4,8,128,384]{3,2,1,0:T(8,128)(2,1)}), bf16[4,8,128,384]{3,2,1,0:T(8,128)(2,1)}, u32[]{:S(2)}, u32[]{:S(2)}) async-start(bf16[4,8,128,384]{3,2,1,0:T(8,128)(2,1)} %bitcast.7), calls=%async_computation.1 | async-start | bytes 6291456 | tf_op jit(solution)/shard_map/all_to_all | solution.py:375
  44.9 4.4 %shard_map.115 = (bf16[768,1024]{1,0:T(8,128)(2,1)S(1)}, f32[1,1024]{1,0:T(1,128)S(1)}, f32[3,1,256]{2,1,0:T(1,128)S(1)}) custom-call(bf16[768,1024]{1,0:T(8,128)(2,1)S(1)} %bitcast.18, bf16[1024,1024]{1,0:T(8,128)(2,1)S(1)} %copy-done, f32[1,1024]{1,0:T(1,128)S(1)} %bitcast.25), custom_call_target="tpu_custom_call" | custom-call | flops 134217728 | bytes 6291456 | tf_op jit(solution)/shard_map/pallas_call | solution.py:51
  54.2 6.4 %shard_map.118.rest_0_ = bf16[768,2048]{1,0:T(8,128)(2,1)S(1)} custom-call(s32[6]{0:T(128)S(1)} %pad_add_fusion.1.place_ref, bf16[768,1024]{1,0:T(8,128)(2,1)S(1)} %get-tuple-element.41.normed_ref, bf16[3,1024,256]{2,1,0:T(8,128)(2,1)} %bitcast.6.first_ref, bf16[3,1024,256]{2,1,0:T(8,128)(2,1)} %collective-permute-done.8.second_ref), custom_call_target="tpu_custom_call" | custom-call | flops 2415919104 | bytes 5242880 | tf_op jit(solution)/shard_map/pallas_call | solution.py:85
  60.7 2.9 %shard_map.119.refs_0_.refs_9_ = bf16[768,2048]{1,0:T(8,128)(2,1)S(1)} custom-call(s32[2]{0:T(128)S(1)} %pad_add_fusion.place_ref, bf16[768,1024]{1,0:T(8,128)(2,1)S(1)} %get-tuple-element.41.normed_ref, bf16[1,1024,256]{2,1,0:T(8,128)(2,1)} %bitcast.8.first_ref, bf16[1,1024,256]{2,1,0:T(8,128)(2,1)S(1)} %bitcast.23, ...), custom_call_target="tpu_custom_call", output_to_operand_aliasing={{}: (4, {})} | custom-call | flops 805306368 | bytes 5242880 | tf_op jit(solution)/shard_map/pallas_call | solution.py:85
  63.6 3.3 %collective-permute-done.10.refs_5_.refs_10_ = bf16[4,128,640]{2,1,0:T(8,128)(2,1)} collective-permute-done((bf16[4,128,640]{2,1,0:T(8,128)(2,1)}, bf16[4,128,640]{2,1,0:T(8,128)(2,1)}, u32[]{:S(2)}, u32[]{:S(2)}) %collective-permute-start.10) | collective-permute-done | bytes 655392 | tf_op jit(solution)/shard_map/ppermute | solution.py:345
  68.7 2.9 %collective-permute-start.13 = (bf16[4,128,640]{2,1,0:T(8,128)(2,1)}, bf16[4,128,640]{2,1,0:T(8,128)(2,1)}, u32[]{:S(2)}, u32[]{:S(2)}) collective-permute-start(bf16[4,128,640]{2,1,0:T(8,128)(2,1)} %collective-permute-done.10.refs_5_.refs_10_), channel_id=1, source_target_pairs={{0,28},{4,0},{8,4},{12,8},{16,12},{20,16},{24,20},{28,24},{1,29},{... | collective-permute-start | bytes 1966088 | tf_op jit(solution)/shard_map/ppermute | solution.py:345
  72.7 7.9 %shard_map.120.refs_7_ = f32[768,640]{1,0:T(8,128)S(1)} custom-call(bf16[768,2048]{1,0:T(8,128)(2,1)S(1)} %shard_map.119.refs_0_.refs_9_, bf16[4,128,640]{2,1,0:T(8,128)(2,1)S(1)} %bitcast.21, bf16[4,128,640]{2,1,0:T(8,128)(2,1)} %collective-permute-done.5.refs_2_.refs_7_, bf16[4,128,640]{2,1,0:T(8,128)(2,1)} %collective-permute-done.6.refs_3_.refs_8_, ...), custom_call_target="tpu_custom_call" | custom-call | flops 5033164800 | bytes 4194304 | tf_op jit(solution)/shard_map/pallas_call | solution.py:200
  81.8 4.1 %collective-permute-done.12.refs_1_.refs_4_ = bf16[4,128,640]{2,1,0:T(8,128)(2,1)} collective-permute-done((bf16[4,128,640]{2,1,0:T(8,128)(2,1)}, bf16[4,128,640]{2,1,0:T(8,128)(2,1)}, u32[]{:S(2)}, u32[]{:S(2)}) %collective-permute-start.12) | collective-permute-done | bytes 655392 | tf_op jit(solution)/shard_map/ppermute | solution.py:345
  86.0 2.0 %broadcast_select_fusion = bf16[4,128,640]{2,1,0:T(8,128)(2,1)} fusion(bf16[4,128,640]{2,1,0:T(8,128)(2,1)} %collective-permute-done.12.refs_1_.refs_4_, bf16[4,128,640]{2,1,0:T(8,128)(2,1)} %collective-permute-done.13.refs_2_.refs_5_, pred[]{:T(512)S(6)} %eq.5), kind=kLoop, calls=%fused_computation | loop fusion | flops 327680 | bytes 1966081 | tf_op jit(solution)/shard_map/jit(_where)/select_n | solution.py:390
  89.9 7.1 %shard_map.121.refs_8_ = f32[768,384]{1,0:T(8,128)S(1)} custom-call(bf16[768,2048]{1,0:T(8,128)(2,1)S(1)} %shard_map.119.refs_0_.refs_9_, bf16[32,128,384]{2,1,0:T(8,128)(2,1)} %bitcast.10.refs_1_.refs_2_, bf16[32,128,384]{2,1,0:T(8,128)(2,1)} %bitcast.10.refs_1_.refs_2_), custom_call_target="tpu_custom_call" | custom-call | flops 4831838208 | bytes 4194304 | tf_op jit(solution)/shard_map/pallas_call | solution.py:200
  98.0 2.0 %collective-permute-done.14.refs_3_.refs_6_ = bf16[4,128,640]{2,1,0:T(8,128)(2,1)} collective-permute-done((bf16[4,128,640]{2,1,0:T(8,128)(2,1)}, bf16[4,128,640]{2,1,0:T(8,128)(2,1)}, u32[]{:S(2)}, u32[]{:S(2)}) %collective-permute-start.14) | collective-permute-done | bytes 655392 | tf_op jit(solution)/shard_map/ppermute | solution.py:390
  100.1 10.2 %shard_map.122 = (bf16[768,1024]{1,0:T(8,128)(2,1)}, f32[32,1,768]{2,1,0:T(1,128)}) custom-call(bf16[768,2048]{1,0:T(8,128)(2,1)} %copy-done.2, bf16[4,128,640]{2,1,0:T(8,128)(2,1)} %collective-permute-done.12.refs_1_.refs_4_, bf16[4,128,640]{2,1,0:T(8,128)(2,1)} %collective-permute-done.13.refs_2_.refs_5_, ...), custom_call_target="tpu_custom_call" | custom-call | flops 4294967296 | bytes 12582912 | tf_op jit(solution)/shard_map/pallas_call | solution.py:262
  110.2 8.4 %all-to-all-start.2 = ((f32[32,1,768]{2,1,0:T(1,128)}), f32[32,1,768]{2,1,0:T(1,128)S(1)}, u32[]{:S(2)}, u32[]{:S(2)}) async-start(f32[32,1,768]{2,1,0:T(1,128)} %get-tuple-element.53), calls=%async_computation.2 | async-start | bytes 196608 | tf_op jit(solution)/shard_map/all_to_all | solution.py:396
  118.9 5.6 %shard_map.123 = bf16[768,1024]{1,0:T(8,128)(2,1)} custom-call(bf16[768,1024]{1,0:T(8,128)(2,1)} %get-tuple-element.52.gated_ref, bf16[1024,1024]{1,0:T(8,128)(2,1)} %w_ref.3, bf16[768,1024]{1,0:T(8,128)(2,1)} %bitcast.17), custom_call_target="tpu_custom_call" | custom-call | flops 1610612736 | bytes 7340032 | tf_op jit(solution)/shard_map/pallas_call | solution.py:301
  124.5 4.5 %all-to-all-done.2 = f32[32,1,768]{2,1,0:T(1,128)S(1)} async-done(((f32[32,1,768]{2,1,0:T(1,128)}), f32[32,1,768]{2,1,0:T(1,128)S(1)}, u32[]{:S(2)}, u32[]{:S(2)}) %all-to-all-start.2) | async-done | bytes 98336 | tf_op jit(solution)/shard_map/all_to_all | solution.py:396
  (60 shorter events, 25.4 us)
Async XLA Ops:
  0.6 24.5 %copy-start.5 = (bf16[1024,256]{1,0:T(8,128)(2,1)S(1)}, bf16[1024,256]{1,0:T(8,128)(2,1)}, u32[]{:S(2)}) copy-start(bf16[1024,256]{1,0:T(8,128)(2,1)} %refs_0_) | copy-start | bytes 1572868
  0.6 24.5 %collective-permute-start.3 = (bf16[1024,256]{1,0:T(8,128)(2,1)}, bf16[1024,256]{1,0:T(8,128)(2,1)S(1)}, u32[]{:S(2)}, u32[]{:S(2)}) collective-permute-start(bf16[1024,256]{1,0:T(8,128)(2,1)} %refs_0_), channel_id=1, source_target_pairs={{0,64},{64,128},{128,192},{192,0},{1,65},{65,129},{129,193},{193,1... | collective-permute-start | bytes 1572872 | tf_op jit(solution)/shard_map/ppermute | solution.py:345
  2.3 22.8 %collective-permute-start.4 = (bf16[1024,256]{1,0:T(8,128)(2,1)}, bf16[1024,256]{1,0:T(8,128)(2,1)S(1)}, u32[]{:S(2)}, u32[]{:S(2)}) collective-permute-start(bf16[1024,256]{1,0:T(8,128)(2,1)} %refs_0_), channel_id=1, source_target_pairs={{0,192},{64,0},{128,64},{192,128},{1,193},{65,1},{129,65},{193,129... | collective-permute-start | bytes 1572872 | tf_op jit(solution)/shard_map/ppermute | solution.py:345
  5.7 31.1 %all-to-all-start = ((bf16[8,128,384]{2,1,0:T(8,128)(2,1)}), bf16[8,128,384]{2,1,0:T(8,128)(2,1)S(1)}, u32[]{:S(2)}, u32[]{:S(2)}) async-start(bf16[8,128,384]{2,1,0:T(8,128)(2,1)} %get-tuple-element.38), calls=%async_computation | async-start | bytes 1572864 | tf_op jit(solution)/shard_map/all_to_all | solution.py:363
  14.0 7.4 %collective-permute-start = (bf16[128,640]{1,0:T(8,128)(2,1)S(1)}, bf16[128,640]{1,0:T(8,128)(2,1)S(1)}, u32[]{:S(2)}, u32[]{:S(2)}) collective-permute-start(bf16[128,640]{1,0:T(8,128)(2,1)S(1)} %copy-done.6), channel_id=1, source_target_pairs={{0,1},{1,2},{2,3},{3,0},{4,5},{5,6},{6,7},{7,4},{8,9},{9,10},{10,1... | collective-permute-start | bytes 491528 | tf_op jit(solution)/shard_map/ppermute | solution.py:345
  15.6 6.7 %collective-permute-start.1 = (bf16[128,640]{1,0:T(8,128)(2,1)S(1)}, bf16[128,640]{1,0:T(8,128)(2,1)S(1)}, u32[]{:S(2)}, u32[]{:S(2)}) collective-permute-start(bf16[128,640]{1,0:T(8,128)(2,1)S(1)} %copy-done.6), channel_id=1, source_target_pairs={{0,3},{1,0},{2,1},{3,2},{4,7},{5,4},{6,5},{7,6},{8,11},{9,8},{10,9... | collective-permute-start | bytes 491528 | tf_op jit(solution)/shard_map/ppermute | solution.py:345
  17.3 7.8 %collective-permute-start.2 = (bf16[128,640]{1,0:T(8,128)(2,1)S(1)}, bf16[128,640]{1,0:T(8,128)(2,1)S(1)}, u32[]{:S(2)}, u32[]{:S(2)}) collective-permute-start(bf16[128,640]{1,0:T(8,128)(2,1)S(1)} %copy-done.6), channel_id=1, source_target_pairs={{0,2},{1,3},{2,0},{3,1},{4,6},{5,7},{6,4},{7,5},{8,10},{9,11},{10,... | collective-permute-start | bytes 491528 | tf_op jit(solution)/shard_map/ppermute | solution.py:345
  26.4 22.9 %collective-permute-start.8 = (bf16[3,1024,256]{2,1,0:T(8,128)(2,1)}, bf16[3,1024,256]{2,1,0:T(8,128)(2,1)}, u32[]{:S(2)}, u32[]{:S(2)}) collective-permute-start(bf16[3,1024,256]{2,1,0:T(8,128)(2,1)} %bitcast.6.first_ref), channel_id=1, source_target_pairs={{0,32},{32,0},{1,33},{33,1},{2,34},{34,2},{3,35},{35,3},{4,36},{36... | collective-permute-start | bytes 4718600 | tf_op jit(solution)/shard_map/ppermute | solution.py:369
  28.3 10.3 %copy-start.3 = (bf16[1,4,128,640]{3,2,1,0:T(8,128)(2,1)}, bf16[1,4,128,640]{3,2,1,0:T(8,128)(2,1)S(1)}, u32[]{:S(2)}) copy-start(bf16[1,4,128,640]{3,2,1,0:T(8,128)(2,1)S(1)} %shard_map.114) | copy-start | bytes 1966084
  28.3 21.0 %collective-permute-start.5 = (bf16[4,128,640]{2,1,0:T(8,128)(2,1)S(1)}, bf16[4,128,640]{2,1,0:T(8,128)(2,1)}, u32[]{:S(2)}, u32[]{:S(2)}) collective-permute-start(bf16[4,128,640]{2,1,0:T(8,128)(2,1)S(1)} %bitcast.19), channel_id=1, source_target_pairs={{0,4},{4,8},{8,12},{12,16},{16,20},{20,24},{24,28},{28,0},{1,5},{5... | collective-permute-start | bytes 1966088 | tf_op jit(solution)/shard_map/ppermute | solution.py:345
  30.1 19.3 %collective-permute-start.6 = (bf16[4,128,640]{2,1,0:T(8,128)(2,1)S(1)}, bf16[4,128,640]{2,1,0:T(8,128)(2,1)}, u32[]{:S(2)}, u32[]{:S(2)}) collective-permute-start(bf16[4,128,640]{2,1,0:T(8,128)(2,1)S(1)} %bitcast.20), channel_id=1, source_target_pairs={{0,28},{4,0},{8,4},{12,8},{16,12},{20,16},{24,20},{28,24},{1,29},{... | collective-permute-start | bytes 1966088 | tf_op jit(solution)/shard_map/ppermute | solution.py:345
  31.6 17.7 %collective-permute-start.7 = (bf16[1024,256]{1,0:T(8,128)(2,1)S(1)}, bf16[1024,256]{1,0:T(8,128)(2,1)}, u32[]{:S(2)}, u32[]{:S(2)}) collective-permute-start(bf16[1024,256]{1,0:T(8,128)(2,1)S(1)} %copy-done.5), channel_id=1, source_target_pairs={{0,128},{64,192},{128,0},{192,64},{1,129},{65,193},{129,1},{193,65... | collective-permute-start | bytes 1572872 | tf_op jit(solution)/shard_map/ppermute | solution.py:345
  38.6 51.2 %all-to-all-start.1 = ((bf16[4,8,128,384]{3,2,1,0:T(8,128)(2,1)}), bf16[4,8,128,384]{3,2,1,0:T(8,128)(2,1)}, u32[]{:S(2)}, u32[]{:S(2)}) async-start(bf16[4,8,128,384]{3,2,1,0:T(8,128)(2,1)} %bitcast.7), calls=%async_computation.1 | async-start | bytes 6291456 | tf_op jit(solution)/shard_map/all_to_all | solution.py:375
  49.3 11.4 %copy-start.8 = (f32[1,1024]{1,0:T(1,128)}, f32[1,1024]{1,0:T(1,128)S(1)}, u32[]{:S(2)}) copy-start(f32[1,1024]{1,0:T(1,128)S(1)} %get-tuple-element.51.refs_11_) | copy-start | bytes 12292
  49.3 11.4 %copy-start.9 = (f32[3,1,256]{2,1,0:T(1,128)}, f32[3,1,256]{2,1,0:T(1,128)S(1)}, u32[]{:S(2)}) copy-start(f32[3,1,256]{2,1,0:T(1,128)S(1)} %get-tuple-element.50.refs_10_) | copy-start | bytes 9220
  49.4 11.3 %collective-permute-start.11 = (bf16[1024,256]{1,0:T(8,128)(2,1)}, bf16[1024,256]{1,0:T(8,128)(2,1)S(1)}, u32[]{:S(2)}, u32[]{:S(2)}) collective-permute-start(bf16[1024,256]{1,0:T(8,128)(2,1)} %collective-permute-done.7), channel_id=1, source_target_pairs={{0,32},{32,0},{1,33},{33,1},{2,34},{34,2},{3,35},{35,3},{4,36},{36... | collective-permute-start | bytes 1572872 | tf_op jit(solution)/shard_map/ppermute | solution.py:377
  49.5 17.5 %collective-permute-start.10 = (bf16[4,128,640]{2,1,0:T(8,128)(2,1)}, bf16[4,128,640]{2,1,0:T(8,128)(2,1)}, u32[]{:S(2)}, u32[]{:S(2)}) collective-permute-start(bf16[4,128,640]{2,1,0:T(8,128)(2,1)} %collective-permute-done.6.refs_3_.refs_8_), channel_id=1, source_target_pairs={{0,28},{4,0},{8,4},{12,8},{16,12},{20,16},{24,20},{28,24},{1,29},{... | collective-permute-start | bytes 1966088 | tf_op jit(solution)/shard_map/ppermute | solution.py:345
  50.0 18.4 %collective-permute-start.9 = (bf16[4,128,640]{2,1,0:T(8,128)(2,1)}, bf16[4,128,640]{2,1,0:T(8,128)(2,1)}, u32[]{:S(2)}, u32[]{:S(2)}) collective-permute-start(bf16[4,128,640]{2,1,0:T(8,128)(2,1)} %collective-permute-done.5.refs_2_.refs_7_), channel_id=1, source_target_pairs={{0,4},{4,8},{8,12},{12,16},{16,20},{20,24},{24,28},{28,0},{1,5},{5... | collective-permute-start | bytes 1966088 | tf_op jit(solution)/shard_map/ppermute | solution.py:345
  63.6 26.3 %copy-start.2 = (bf16[768,2048]{1,0:T(8,128)(2,1)}, bf16[768,2048]{1,0:T(8,128)(2,1)S(1)}, u32[]{:S(2)}) copy-start(bf16[768,2048]{1,0:T(8,128)(2,1)S(1)} %shard_map.119.refs_0_.refs_9_) | copy-start | bytes 9437188
  68.4 17.6 %collective-permute-start.12 = (bf16[4,128,640]{2,1,0:T(8,128)(2,1)}, bf16[4,128,640]{2,1,0:T(8,128)(2,1)}, u32[]{:S(2)}, u32[]{:S(2)}) collective-permute-start(bf16[4,128,640]{2,1,0:T(8,128)(2,1)} %collective-permute-done.9.refs_4_.refs_9_), channel_id=1, source_target_pairs={{0,4},{4,8},{8,12},{12,16},{16,20},{20,24},{24,28},{28,0},{1,5},{5... | collective-permute-start | bytes 1966088 | tf_op jit(solution)/shard_map/ppermute | solution.py:345
  68.7 17.3 %collective-permute-start.13 = (bf16[4,128,640]{2,1,0:T(8,128)(2,1)}, bf16[4,128,640]{2,1,0:T(8,128)(2,1)}, u32[]{:S(2)}, u32[]{:S(2)}) collective-permute-start(bf16[4,128,640]{2,1,0:T(8,128)(2,1)} %collective-permute-done.10.refs_5_.refs_10_), channel_id=1, source_target_pairs={{0,28},{4,0},{8,4},{12,8},{16,12},{20,16},{24,20},{28,24},{1,29},{... | collective-permute-start | bytes 1966088 | tf_op jit(solution)/shard_map/ppermute | solution.py:345
  88.0 12.1 %collective-permute-start.14 = (bf16[4,128,640]{2,1,0:T(8,128)(2,1)}, bf16[4,128,640]{2,1,0:T(8,128)(2,1)}, u32[]{:S(2)}, u32[]{:S(2)}) collective-permute-start(bf16[4,128,640]{2,1,0:T(8,128)(2,1)} %broadcast_select_fusion), channel_id=1, source_target_pairs={{0,4},{4,8},{8,12},{12,16},{16,20},{20,24},{24,28},{28,0},{32,60},... | collective-permute-start | bytes 1966088 | tf_op jit(solution)/shard_map/ppermute | solution.py:390
  100.1 18.6 %copy-start.12 = (s32[1,768]{1,0:T(1,128)S(1)}, s32[1,768]{1,0:T(1,128)}, u32[]{:S(2)}) copy-start(s32[1,768]{1,0:T(1,128)} %param.15) | copy-start | bytes 9220
  110.2 18.7 %all-to-all-start.2 = ((f32[32,1,768]{2,1,0:T(1,128)}), f32[32,1,768]{2,1,0:T(1,128)S(1)}, u32[]{:S(2)}, u32[]{:S(2)}) async-start(f32[32,1,768]{2,1,0:T(1,128)} %get-tuple-element.53), calls=%async_computation.2 | async-start | bytes 196608 | tf_op jit(solution)/shard_map/all_to_all | solution.py:396
  (8 other events, 27.2 us)

commit v5 on v4

--- a/solution.py
+++ b/solution.py
@@ -198,7 +198,7 @@
     sums = pl.BlockSpec((rows, head), lambda h: (0, h))
     more = before is not None
     return pl.pallas_call(
-        functools.partial(partial_kernel, count=len(arrays), factor=float(head) ** -0.5, tile=256, more=more),
+        functools.partial(partial_kernel, count=len(arrays), factor=float(head) ** -0.5, tile=rows, more=more),
         grid=(heads,),
         in_specs=[pl.BlockSpec((rows, head), lambda h: (0, HEADS + first + h))]
         + key_specs(arrays, head, lambda h: h)
@@ -229,8 +229,7 @@
             read.start()
 
     k, v = side_by_side(ks), side_by_side(vs)
-    for r in range(0, rows, tile):
-        attn[h, r : r + tile, :] = weigh(q_ref[r : r + tile, :], k, v, factor) + sums_ref[r : r + tile, :]
+    attn[h] = weigh(q_ref[...], k, v, factor) + sums_ref[...]
 
     @pl.when(h == pl.num_programs(0) - 1)
     def _():

time: 131 us -> 131 us (level)
  no operation moved by 1% of the time
where the time goes in v5:
time: 131 us; the launch traced here: 130 us
  Pallas kernels  53.2 us (41%)
  starting transfers between devices  41.4 us (32%)
  waiting for transfers between devices  23.6 us (18%)
  local copies, waits for them, and re-layouts  6.25 us (5%)
  other arithmetic  3.4 us (3%)
  between operations  2.32 us (2%)
    ppermute x12, starting transfers between devices, shift(): return lax.ppermute(block, axis, shifted(lax.axis_size(axis), step))  18.4 us
    pallas_call x2, Pallas kernels, attend_part(): pl.pallas_call(functools.partial(partial_kernel, count=len(arrays), facto...  15.5 us
    ppermute x12, waiting for transfers between devices, shift(): return lax.ppermute(block, axis, shifted(lax.axis_size(axis), step))  14.4 us
    pallas_call x1, Pallas kernels, finish(): pl.pallas_call(functools.partial(finish_kernel, count=len(arrays), factor...  10.2 us
    pallas_call x2, Pallas kernels, project(): pl.pallas_call(functools.partial(project_kernel, count=count), grid_spec=...  9.33 us
    all_to_all x1, starting transfers between devices, on_device(): lax.all_to_all(sent, ('z', 'x'), split_axis=0, concat_axis=0, tiled=True)  8.43 us
    all_to_all x1, starting transfers between devices, on_device(): zs = lax.all_to_all(mine_b, 'z', split_axis=0, concat_axis=0, tiled=True)  8.35 us
    pallas_call x1, Pallas kernels, project_out(): pl.pallas_call(out_kernel, grid=(rows // tile,), in_specs=[pl.BlockSpec((...  5.57 us
  transfers between devices with their start and end apart: 18, of which 9 were waited for; matrix products, arithmetic and copies ran while one was open for 4% of the time, Pallas kernels for 32%

profile of v5, /device:TPU:8, one launch (start us, length us, event | category | flops | bytes accessed | tf_op | source)
XLA Modules:
  0.0 130.2 jit_solution(9701092729611342759)
XLA Ops:
  3.7 2.0 %shard_map.113 = (bf16[128,640]{1,0:T(8,128)(2,1)}, bf16[8,128,384]{2,1,0:T(8,128)(2,1)}) custom-call(s32[1]{0:T(128)S(6)} %sub.23.live_ref, bf16[64,1024]{1,0:T(8,128)(2,1)} %bitcast.27, bf16[64,1024]{1,0:T(8,128)(2,1)} %bitcast.28), custom_call_target="tpu_custom_call" | custom-call | tf_op jit(solution)/shard_map/pallas_call | solution.py:152
  5.7 8.3 %all-to-all-start = ((bf16[8,128,384]{2,1,0:T(8,128)(2,1)}), bf16[8,128,384]{2,1,0:T(8,128)(2,1)S(1)}, u32[]{:S(2)}, u32[]{:S(2)}) async-start(bf16[8,128,384]{2,1,0:T(8,128)(2,1)} %get-tuple-element.38), calls=%async_computation | async-start | bytes 1572864 | tf_op jit(solution)/shard_map/all_to_all | solution.py:362
  17.3 1.8 %collective-permute-start.2 = (bf16[128,640]{1,0:T(8,128)(2,1)S(1)}, bf16[128,640]{1,0:T(8,128)(2,1)S(1)}, u32[]{:S(2)}, u32[]{:S(2)}) collective-permute-start(bf16[128,640]{1,0:T(8,128)(2,1)S(1)} %copy-done.6), channel_id=1, source_target_pairs={{0,2},{1,3},{2,0},{3,1},{4,6},{5,7},{6,4},{7,5},{8,10},{9,11},{10,... | collective-permute-start | bytes 491528 | tf_op jit(solution)/shard_map/ppermute | solution.py:344
  19.1 2.2 %collective-permute-done.refs_1_ = bf16[128,640]{1,0:T(8,128)(2,1)S(1)} collective-permute-done((bf16[128,640]{1,0:T(8,128)(2,1)S(1)}, bf16[128,640]{1,0:T(8,128)(2,1)S(1)}, u32[]{:S(2)}, u32[]{:S(2)}) %collective-permute-start) | collective-permute-done | bytes 163872 | tf_op jit(solution)/shard_map/ppermute | solution.py:344
  22.2 2.9 %collective-permute-done.2.refs_3_ = bf16[128,640]{1,0:T(8,128)(2,1)S(1)} collective-permute-done((bf16[128,640]{1,0:T(8,128)(2,1)S(1)}, bf16[128,640]{1,0:T(8,128)(2,1)S(1)}, u32[]{:S(2)}, u32[]{:S(2)}) %collective-permute-start.2) | collective-permute-done | bytes 163872 | tf_op jit(solution)/shard_map/ppermute | solution.py:344
  26.5 1.8 %shard_map.114 = bf16[1,4,128,640]{3,2,1,0:T(8,128)(2,1)S(1)} custom-call(bf16[128,640]{1,0:T(8,128)(2,1)S(1)} %copy-done.6, bf16[128,640]{1,0:T(8,128)(2,1)S(1)} %collective-permute-done.refs_1_, bf16[128,640]{1,0:T(8,128)(2,1)S(1)} %collective-permute-done.1.refs_2_, bf16[128,640]{1,0:T(8,128)(2,1)S(1)} %collective-permute-done.2.refs_3_), custom_call_target="tpu_custom_call" | custom-call | bytes 4194304 | tf_op jit(solution)/shard_map/pallas_call | solution.py:125
  31.6 2.3 %collective-permute-start.7 = (bf16[1024,256]{1,0:T(8,128)(2,1)S(1)}, bf16[1024,256]{1,0:T(8,128)(2,1)}, u32[]{:S(2)}, u32[]{:S(2)}) collective-permute-start(bf16[1024,256]{1,0:T(8,128)(2,1)S(1)} %copy-done.5), channel_id=1, source_target_pairs={{0,128},{64,192},{128,0},{192,64},{1,129},{65,193},{129,1},{193,65... | collective-permute-start | bytes 1572872 | tf_op jit(solution)/shard_map/ppermute | solution.py:344
  33.9 2.8 %all-to-all-done.refs_0_ = bf16[8,128,384]{2,1,0:T(8,128)(2,1)S(1)} async-done(((bf16[8,128,384]{2,1,0:T(8,128)(2,1)}), bf16[8,128,384]{2,1,0:T(8,128)(2,1)S(1)}, u32[]{:S(2)}, u32[]{:S(2)}) %all-to-all-start) | async-done | bytes 786464 | tf_op jit(solution)/shard_map/all_to_all | solution.py:362
  36.8 1.8 %shard_map.117 = bf16[4,1,8,128,384]{4,3,2,1,0:T(8,128)(2,1)} custom-call(bf16[8,128,384]{2,1,0:T(8,128)(2,1)S(1)} %all-to-all-done.refs_0_), custom_call_target="tpu_custom_call" | custom-call | bytes 4194304 | tf_op jit(solution)/shard_map/pallas_call | solution.py:125
  38.6 4.8 %all-to-all-start.1 = ((bf16[4,8,128,384]{3,2,1,0:T(8,128)(2,1)}), bf16[4,8,128,384]{3,2,1,0:T(8,128)(2,1)}, u32[]{:S(2)}, u32[]{:S(2)}) async-start(bf16[4,8,128,384]{3,2,1,0:T(8,128)(2,1)} %bitcast.7), calls=%async_computation.1 | async-start | bytes 6291456 | tf_op jit(solution)/shard_map/all_to_all | solution.py:374
  44.9 4.4 %shard_map.115 = (bf16[768,1024]{1,0:T(8,128)(2,1)S(1)}, f32[1,1024]{1,0:T(1,128)S(1)}, f32[3,1,256]{2,1,0:T(1,128)S(1)}) custom-call(bf16[768,1024]{1,0:T(8,128)(2,1)S(1)} %bitcast.18, bf16[1024,1024]{1,0:T(8,128)(2,1)S(1)} %copy-done, f32[1,1024]{1,0:T(1,128)S(1)} %bitcast.25), custom_call_target="tpu_custom_call" | custom-call | flops 134217728 | bytes 6291456 | tf_op jit(solution)/shard_map/pallas_call | solution.py:51
  54.2 6.4 %shard_map.118.rest_0_ = bf16[768,2048]{1,0:T(8,128)(2,1)S(1)} custom-call(s32[6]{0:T(128)S(1)} %pad_add_fusion.1.place_ref, bf16[768,1024]{1,0:T(8,128)(2,1)S(1)} %get-tuple-element.41.normed_ref, bf16[3,1024,256]{2,1,0:T(8,128)(2,1)} %bitcast.6.first_ref, bf16[3,1024,256]{2,1,0:T(8,128)(2,1)} %collective-permute-done.8.second_ref), custom_call_target="tpu_custom_call" | custom-call | flops 2415919104 | bytes 5242880 | tf_op jit(solution)/shard_map/pallas_call | solution.py:85
  60.7 2.9 %shard_map.119.refs_0_.refs_9_ = bf16[768,2048]{1,0:T(8,128)(2,1)S(1)} custom-call(s32[2]{0:T(128)S(1)} %pad_add_fusion.place_ref, bf16[768,1024]{1,0:T(8,128)(2,1)S(1)} %get-tuple-element.41.normed_ref, bf16[1,1024,256]{2,1,0:T(8,128)(2,1)} %bitcast.8.first_ref, bf16[1,1024,256]{2,1,0:T(8,128)(2,1)S(1)} %bitcast.23, ...), custom_call_target="tpu_custom_call", output_to_operand_aliasing={{}: (4, {})} | custom-call | flops 805306368 | bytes 5242880 | tf_op jit(solution)/shard_map/pallas_call | solution.py:85
  63.6 3.3 %collective-permute-done.10.refs_5_.refs_10_ = bf16[4,128,640]{2,1,0:T(8,128)(2,1)} collective-permute-done((bf16[4,128,640]{2,1,0:T(8,128)(2,1)}, bf16[4,128,640]{2,1,0:T(8,128)(2,1)}, u32[]{:S(2)}, u32[]{:S(2)}) %collective-permute-start.10) | collective-permute-done | bytes 655392 | tf_op jit(solution)/shard_map/ppermute | solution.py:344
  68.7 2.9 %collective-permute-start.13 = (bf16[4,128,640]{2,1,0:T(8,128)(2,1)}, bf16[4,128,640]{2,1,0:T(8,128)(2,1)}, u32[]{:S(2)}, u32[]{:S(2)}) collective-permute-start(bf16[4,128,640]{2,1,0:T(8,128)(2,1)} %collective-permute-done.10.refs_5_.refs_10_), channel_id=1, source_target_pairs={{0,28},{4,0},{8,4},{12,8},{16,12},{20,16},{24,20},{28,24},{1,29},{... | collective-permute-start | bytes 1966088 | tf_op jit(solution)/shard_map/ppermute | solution.py:344
  72.7 8.3 %shard_map.120.refs_7_ = f32[768,640]{1,0:T(8,128)S(1)} custom-call(bf16[768,2048]{1,0:T(8,128)(2,1)S(1)} %shard_map.119.refs_0_.refs_9_, bf16[4,128,640]{2,1,0:T(8,128)(2,1)S(1)} %bitcast.21, bf16[4,128,640]{2,1,0:T(8,128)(2,1)} %collective-permute-done.5.refs_2_.refs_7_, bf16[4,128,640]{2,1,0:T(8,128)(2,1)} %collective-permute-done.6.refs_3_.refs_8_, ...), custom_call_target="tpu_custom_call" | custom-call | flops 5033164800 | bytes 4194304 | tf_op jit(solution)/shard_map/pallas_call | solution.py:200
  82.3 3.7 %collective-permute-done.12.refs_1_.refs_4_ = bf16[4,128,640]{2,1,0:T(8,128)(2,1)} collective-permute-done((bf16[4,128,640]{2,1,0:T(8,128)(2,1)}, bf16[4,128,640]{2,1,0:T(8,128)(2,1)}, u32[]{:S(2)}, u32[]{:S(2)}) %collective-permute-start.12) | collective-permute-done | bytes 655392 | tf_op jit(solution)/shard_map/ppermute | solution.py:344
  86.0 2.0 %broadcast_select_fusion = bf16[4,128,640]{2,1,0:T(8,128)(2,1)} fusion(bf16[4,128,640]{2,1,0:T(8,128)(2,1)} %collective-permute-done.12.refs_1_.refs_4_, bf16[4,128,640]{2,1,0:T(8,128)(2,1)} %collective-permute-done.13.refs_2_.refs_5_, pred[]{:T(512)S(6)} %eq.5), kind=kLoop, calls=%fused_computation | loop fusion | flops 327680 | bytes 1966081 | tf_op jit(solution)/shard_map/jit(_where)/select_n | solution.py:389
  89.9 7.2 %shard_map.121.refs_8_ = f32[768,384]{1,0:T(8,128)S(1)} custom-call(bf16[768,2048]{1,0:T(8,128)(2,1)S(1)} %shard_map.119.refs_0_.refs_9_, bf16[32,128,384]{2,1,0:T(8,128)(2,1)} %bitcast.10.refs_1_.refs_2_, bf16[32,128,384]{2,1,0:T(8,128)(2,1)} %bitcast.10.refs_1_.refs_2_), custom_call_target="tpu_custom_call" | custom-call | flops 4831838208 | bytes 4194304 | tf_op jit(solution)/shard_map/pallas_call | solution.py:200
  98.1 2.0 %collective-permute-done.14.refs_3_.refs_6_ = bf16[4,128,640]{2,1,0:T(8,128)(2,1)} collective-permute-done((bf16[4,128,640]{2,1,0:T(8,128)(2,1)}, bf16[4,128,640]{2,1,0:T(8,128)(2,1)}, u32[]{:S(2)}, u32[]{:S(2)}) %collective-permute-start.14) | collective-permute-done | bytes 655392 | tf_op jit(solution)/shard_map/ppermute | solution.py:389
  100.1 10.2 %shard_map.122 = (bf16[768,1024]{1,0:T(8,128)(2,1)}, f32[32,1,768]{2,1,0:T(1,128)}) custom-call(bf16[768,2048]{1,0:T(8,128)(2,1)} %copy-done.2, bf16[4,128,640]{2,1,0:T(8,128)(2,1)} %collective-permute-done.12.refs_1_.refs_4_, bf16[4,128,640]{2,1,0:T(8,128)(2,1)} %collective-permute-done.13.refs_2_.refs_5_, ...), custom_call_target="tpu_custom_call" | custom-call | flops 4294967296 | bytes 12582912 | tf_op jit(solution)/shard_map/pallas_call | solution.py:261
  110.2 8.4 %all-to-all-start.2 = ((f32[32,1,768]{2,1,0:T(1,128)}), f32[32,1,768]{2,1,0:T(1,128)S(1)}, u32[]{:S(2)}, u32[]{:S(2)}) async-start(f32[32,1,768]{2,1,0:T(1,128)} %get-tuple-element.53), calls=%async_computation.2 | async-start | bytes 196608 | tf_op jit(solution)/shard_map/all_to_all | solution.py:395
  118.9 5.6 %shard_map.123 = bf16[768,1024]{1,0:T(8,128)(2,1)} custom-call(bf16[768,1024]{1,0:T(8,128)(2,1)} %get-tuple-element.52.gated_ref, bf16[1024,1024]{1,0:T(8,128)(2,1)} %w_ref.3, bf16[768,1024]{1,0:T(8,128)(2,1)} %bitcast.17), custom_call_target="tpu_custom_call" | custom-call | flops 1610612736 | bytes 7340032 | tf_op jit(solution)/shard_map/pallas_call | solution.py:300
  124.4 4.4 %all-to-all-done.2 = f32[32,1,768]{2,1,0:T(1,128)S(1)} async-done(((f32[32,1,768]{2,1,0:T(1,128)}), f32[32,1,768]{2,1,0:T(1,128)S(1)}, u32[]{:S(2)}, u32[]{:S(2)}) %all-to-all-start.2) | async-done | bytes 98336 | tf_op jit(solution)/shard_map/all_to_all | solution.py:395
  (60 shorter events, 25.4 us)
Async XLA Ops:
  0.6 24.5 %copy-start.5 = (bf16[1024,256]{1,0:T(8,128)(2,1)S(1)}, bf16[1024,256]{1,0:T(8,128)(2,1)}, u32[]{:S(2)}) copy-start(bf16[1024,256]{1,0:T(8,128)(2,1)} %refs_0_) | copy-start | bytes 1572868
  0.6 24.5 %collective-permute-start.3 = (bf16[1024,256]{1,0:T(8,128)(2,1)}, bf16[1024,256]{1,0:T(8,128)(2,1)S(1)}, u32[]{:S(2)}, u32[]{:S(2)}) collective-permute-start(bf16[1024,256]{1,0:T(8,128)(2,1)} %refs_0_), channel_id=1, source_target_pairs={{0,64},{64,128},{128,192},{192,0},{1,65},{65,129},{129,193},{193,1... | collective-permute-start | bytes 1572872 | tf_op jit(solution)/shard_map/ppermute | solution.py:344
  2.3 22.8 %collective-permute-start.4 = (bf16[1024,256]{1,0:T(8,128)(2,1)}, bf16[1024,256]{1,0:T(8,128)(2,1)S(1)}, u32[]{:S(2)}, u32[]{:S(2)}) collective-permute-start(bf16[1024,256]{1,0:T(8,128)(2,1)} %refs_0_), channel_id=1, source_target_pairs={{0,192},{64,0},{128,64},{192,128},{1,193},{65,1},{129,65},{193,129... | collective-permute-start | bytes 1572872 | tf_op jit(solution)/shard_map/ppermute | solution.py:344
  5.7 31.1 %all-to-all-start = ((bf16[8,128,384]{2,1,0:T(8,128)(2,1)}), bf16[8,128,384]{2,1,0:T(8,128)(2,1)S(1)}, u32[]{:S(2)}, u32[]{:S(2)}) async-start(bf16[8,128,384]{2,1,0:T(8,128)(2,1)} %get-tuple-element.38), calls=%async_computation | async-start | bytes 1572864 | tf_op jit(solution)/shard_map/all_to_all | solution.py:362
  14.0 7.4 %collective-permute-start = (bf16[128,640]{1,0:T(8,128)(2,1)S(1)}, bf16[128,640]{1,0:T(8,128)(2,1)S(1)}, u32[]{:S(2)}, u32[]{:S(2)}) collective-permute-start(bf16[128,640]{1,0:T(8,128)(2,1)S(1)} %copy-done.6), channel_id=1, source_target_pairs={{0,1},{1,2},{2,3},{3,0},{4,5},{5,6},{6,7},{7,4},{8,9},{9,10},{10,1... | collective-permute-start | bytes 491528 | tf_op jit(solution)/shard_map/ppermute | solution.py:344
  15.6 6.7 %collective-permute-start.1 = (bf16[128,640]{1,0:T(8,128)(2,1)S(1)}, bf16[128,640]{1,0:T(8,128)(2,1)S(1)}, u32[]{:S(2)}, u32[]{:S(2)}) collective-permute-start(bf16[128,640]{1,0:T(8,128)(2,1)S(1)} %copy-done.6), channel_id=1, source_target_pairs={{0,3},{1,0},{2,1},{3,2},{4,7},{5,4},{6,5},{7,6},{8,11},{9,8},{10,9... | collective-permute-start | bytes 491528 | tf_op jit(solution)/shard_map/ppermute | solution.py:344
  17.3 7.8 %collective-permute-start.2 = (bf16[128,640]{1,0:T(8,128)(2,1)S(1)}, bf16[128,640]{1,0:T(8,128)(2,1)S(1)}, u32[]{:S(2)}, u32[]{:S(2)}) collective-permute-start(bf16[128,640]{1,0:T(8,128)(2,1)S(1)} %copy-done.6), channel_id=1, source_target_pairs={{0,2},{1,3},{2,0},{3,1},{4,6},{5,7},{6,4},{7,5},{8,10},{9,11},{10,... | collective-permute-start | bytes 491528 | tf_op jit(solution)/shard_map/ppermute | solution.py:344
  26.4 22.9 %collective-permute-start.8 = (bf16[3,1024,256]{2,1,0:T(8,128)(2,1)}, bf16[3,1024,256]{2,1,0:T(8,128)(2,1)}, u32[]{:S(2)}, u32[]{:S(2)}) collective-permute-start(bf16[3,1024,256]{2,1,0:T(8,128)(2,1)} %bitcast.6.first_ref), channel_id=1, source_target_pairs={{0,32},{32,0},{1,33},{33,1},{2,34},{34,2},{3,35},{35,3},{4,36},{36... | collective-permute-start | bytes 4718600 | tf_op jit(solution)/shard_map/ppermute | solution.py:368
  28.3 10.3 %copy-start.3 = (bf16[1,4,128,640]{3,2,1,0:T(8,128)(2,1)}, bf16[1,4,128,640]{3,2,1,0:T(8,128)(2,1)S(1)}, u32[]{:S(2)}) copy-start(bf16[1,4,128,640]{3,2,1,0:T(8,128)(2,1)S(1)} %shard_map.114) | copy-start | bytes 1966084
  28.3 21.0 %collective-permute-start.5 = (bf16[4,128,640]{2,1,0:T(8,128)(2,1)S(1)}, bf16[4,128,640]{2,1,0:T(8,128)(2,1)}, u32[]{:S(2)}, u32[]{:S(2)}) collective-permute-start(bf16[4,128,640]{2,1,0:T(8,128)(2,1)S(1)} %bitcast.19), channel_id=1, source_target_pairs={{0,4},{4,8},{8,12},{12,16},{16,20},{20,24},{24,28},{28,0},{1,5},{5... | collective-permute-start | bytes 1966088 | tf_op jit(solution)/shard_map/ppermute | solution.py:344
  30.1 19.3 %collective-permute-start.6 = (bf16[4,128,640]{2,1,0:T(8,128)(2,1)S(1)}, bf16[4,128,640]{2,1,0:T(8,128)(2,1)}, u32[]{:S(2)}, u32[]{:S(2)}) collective-permute-start(bf16[4,128,640]{2,1,0:T(8,128)(2,1)S(1)} %bitcast.20), channel_id=1, source_target_pairs={{0,28},{4,0},{8,4},{12,8},{16,12},{20,16},{24,20},{28,24},{1,29},{... | collective-permute-start | bytes 1966088 | tf_op jit(solution)/shard_map/ppermute | solution.py:344
  31.6 17.7 %collective-permute-start.7 = (bf16[1024,256]{1,0:T(8,128)(2,1)S(1)}, bf16[1024,256]{1,0:T(8,128)(2,1)}, u32[]{:S(2)}, u32[]{:S(2)}) collective-permute-start(bf16[1024,256]{1,0:T(8,128)(2,1)S(1)} %copy-done.5), channel_id=1, source_target_pairs={{0,128},{64,192},{128,0},{192,64},{1,129},{65,193},{129,1},{193,65... | collective-permute-start | bytes 1572872 | tf_op jit(solution)/shard_map/ppermute | solution.py:344
  38.6 51.2 %all-to-all-start.1 = ((bf16[4,8,128,384]{3,2,1,0:T(8,128)(2,1)}), bf16[4,8,128,384]{3,2,1,0:T(8,128)(2,1)}, u32[]{:S(2)}, u32[]{:S(2)}) async-start(bf16[4,8,128,384]{3,2,1,0:T(8,128)(2,1)} %bitcast.7), calls=%async_computation.1 | async-start | bytes 6291456 | tf_op jit(solution)/shard_map/all_to_all | solution.py:374
  49.3 11.4 %copy-start.8 = (f32[1,1024]{1,0:T(1,128)}, f32[1,1024]{1,0:T(1,128)S(1)}, u32[]{:S(2)}) copy-start(f32[1,1024]{1,0:T(1,128)S(1)} %get-tuple-element.51.refs_11_) | copy-start | bytes 12292
  49.3 11.4 %copy-start.9 = (f32[3,1,256]{2,1,0:T(1,128)}, f32[3,1,256]{2,1,0:T(1,128)S(1)}, u32[]{:S(2)}) copy-start(f32[3,1,256]{2,1,0:T(1,128)S(1)} %get-tuple-element.50.refs_10_) | copy-start | bytes 9220
  49.4 11.3 %collective-permute-start.11 = (bf16[1024,256]{1,0:T(8,128)(2,1)}, bf16[1024,256]{1,0:T(8,128)(2,1)S(1)}, u32[]{:S(2)}, u32[]{:S(2)}) collective-permute-start(bf16[1024,256]{1,0:T(8,128)(2,1)} %collective-permute-done.7), channel_id=1, source_target_pairs={{0,32},{32,0},{1,33},{33,1},{2,34},{34,2},{3,35},{35,3},{4,36},{36... | collective-permute-start | bytes 1572872 | tf_op jit(solution)/shard_map/ppermute | solution.py:376
  49.5 17.5 %collective-permute-start.10 = (bf16[4,128,640]{2,1,0:T(8,128)(2,1)}, bf16[4,128,640]{2,1,0:T(8,128)(2,1)}, u32[]{:S(2)}, u32[]{:S(2)}) collective-permute-start(bf16[4,128,640]{2,1,0:T(8,128)(2,1)} %collective-permute-done.6.refs_3_.refs_8_), channel_id=1, source_target_pairs={{0,28},{4,0},{8,4},{12,8},{16,12},{20,16},{24,20},{28,24},{1,29},{... | collective-permute-start | bytes 1966088 | tf_op jit(solution)/shard_map/ppermute | solution.py:344
  50.0 18.4 %collective-permute-start.9 = (bf16[4,128,640]{2,1,0:T(8,128)(2,1)}, bf16[4,128,640]{2,1,0:T(8,128)(2,1)}, u32[]{:S(2)}, u32[]{:S(2)}) collective-permute-start(bf16[4,128,640]{2,1,0:T(8,128)(2,1)} %collective-permute-done.5.refs_2_.refs_7_), channel_id=1, source_target_pairs={{0,4},{4,8},{8,12},{12,16},{16,20},{20,24},{24,28},{28,0},{1,5},{5... | collective-permute-start | bytes 1966088 | tf_op jit(solution)/shard_map/ppermute | solution.py:344
  63.6 26.3 %copy-start.2 = (bf16[768,2048]{1,0:T(8,128)(2,1)}, bf16[768,2048]{1,0:T(8,128)(2,1)S(1)}, u32[]{:S(2)}) copy-start(bf16[768,2048]{1,0:T(8,128)(2,1)S(1)} %shard_map.119.refs_0_.refs_9_) | copy-start | bytes 9437188
  68.4 17.6 %collective-permute-start.12 = (bf16[4,128,640]{2,1,0:T(8,128)(2,1)}, bf16[4,128,640]{2,1,0:T(8,128)(2,1)}, u32[]{:S(2)}, u32[]{:S(2)}) collective-permute-start(bf16[4,128,640]{2,1,0:T(8,128)(2,1)} %collective-permute-done.9.refs_4_.refs_9_), channel_id=1, source_target_pairs={{0,4},{4,8},{8,12},{12,16},{16,20},{20,24},{24,28},{28,0},{1,5},{5... | collective-permute-start | bytes 1966088 | tf_op jit(solution)/shard_map/ppermute | solution.py:344
  68.7 17.3 %collective-permute-start.13 = (bf16[4,128,640]{2,1,0:T(8,128)(2,1)}, bf16[4,128,640]{2,1,0:T(8,128)(2,1)}, u32[]{:S(2)}, u32[]{:S(2)}) collective-permute-start(bf16[4,128,640]{2,1,0:T(8,128)(2,1)} %collective-permute-done.10.refs_5_.refs_10_), channel_id=1, source_target_pairs={{0,28},{4,0},{8,4},{12,8},{16,12},{20,16},{24,20},{28,24},{1,29},{... | collective-permute-start | bytes 1966088 | tf_op jit(solution)/shard_map/ppermute | solution.py:344
  88.0 12.1 %collective-permute-start.14 = (bf16[4,128,640]{2,1,0:T(8,128)(2,1)}, bf16[4,128,640]{2,1,0:T(8,128)(2,1)}, u32[]{:S(2)}, u32[]{:S(2)}) collective-permute-start(bf16[4,128,640]{2,1,0:T(8,128)(2,1)} %broadcast_select_fusion), channel_id=1, source_target_pairs={{0,4},{4,8},{8,12},{12,16},{16,20},{20,24},{24,28},{28,0},{32,60},... | collective-permute-start | bytes 1966088 | tf_op jit(solution)/shard_map/ppermute | solution.py:389
  100.1 18.6 %copy-start.12 = (s32[1,768]{1,0:T(1,128)S(1)}, s32[1,768]{1,0:T(1,128)}, u32[]{:S(2)}) copy-start(s32[1,768]{1,0:T(1,128)} %param.15) | copy-start | bytes 9220
  110.2 18.6 %all-to-all-start.2 = ((f32[32,1,768]{2,1,0:T(1,128)}), f32[32,1,768]{2,1,0:T(1,128)S(1)}, u32[]{:S(2)}, u32[]{:S(2)}) async-start(f32[32,1,768]{2,1,0:T(1,128)} %get-tuple-element.53), calls=%async_computation.2 | async-start | bytes 196608 | tf_op jit(solution)/shard_map/all_to_all | solution.py:395
  (8 other events, 27.2 us)
